TPU v7x, 256 devices: a whole 4x4x8 slice. The times are simulated.
256 devices in a mesh: grp: 2 (over x_lo), tx: 8 (over z), ty: 16 (over x_hi, y, core).
Axes of the slice: x: 4 (x_hi: 2, x_lo: 2; x = x_hi * 2 + x_lo), y: 4, z: 8, core: 2. Of those that a mesh axis runs over, the one named last changes fastest.
Arguments:
- features: bfloat16 [2, 128, 512, 8, 96], P('grp', 'tx', 'ty'), may hold values from -6 to 6
- voxel_mask: int32 [2, 128, 512, 8], P('grp', 'tx', 'ty'), may hold values 0 or 1
- brick_order: int32 [256, 8], P(('grp', 'tx', 'ty')), may hold values from 0 to 7, each once within a row
- brick_count: int32 [256], P(('grp', 'tx', 'ty')), may hold values from 1 to 2, 320 in all
- w_conv1: bfloat16 [27, 9216], P(None, ('tx', 'ty')), may hold values from -0.125 to 0.125
- w_down: bfloat16 [8, 18432], P(None, ('tx', 'ty')), may hold values from -0.21875 to 0.21875
- w_conv2: bfloat16 [27, 36864], P(None, ('tx', 'ty')), may hold values from -0.078125 to 0.078125
- cotangent: bfloat16 [2, 64, 256, 4, 192], P('grp', 'tx', 'ty'), may hold values from -0.019897461 to 0.019897461
Outputs:
- output: bfloat16 [2, 64, 256, 4, 192], P('grp', 'tx', 'ty')
- grad_conv1: float32 [27, 9216], P(None, ('tx', 'ty'))
- grad_down: float32 [8, 18432], P(None, ('tx', 'ty'))
- grad_conv2: float32 [27, 36864], P(None, ('tx', 'ty'))
Inputs may be any that keep to these rules, and one draw needn't show every extreme that they name: `brick_order`: each row lists every brick position of its tile once. `brick_count`: some tile has exactly 2 active bricks.
All inputs are finite; a program needn't handle non-finite values. No bound on the sum of `voxel_mask` or of `brick_count` on one device may be relied on, other than what follows from the above.
Results may differ from a plain program's by a relative error of at most 0.01.
Values may be sent and summed in bfloat16 or wider, within the bound.
A program may use at most 128 MiB of HBM per device.

v0:
```python
import jax
import jax.numpy as jnp
from jax import lax
from jax.sharding import PartitionSpec as P

C1 = 96
C2 = 192
GX = 2
GY = 4
CAP = 2


tap_offsets = [(ox, oy, oz) for ox in range(3) for oy in range(3) for oz in range(3)]


def extended(block, sides, width):
    for axis, dim in sides:
        count = lax.axis_size(axis)
        forward = [(i, i + 1) for i in range(count - 1)]
        backward = [(target, source) for source, target in forward]
        low = lax.ppermute(
            lax.slice_in_dim(block, block.shape[dim] - width, None, axis=dim), axis, forward
        )
        high = lax.ppermute(lax.slice_in_dim(block, 0, width, axis=dim), axis, backward)
        block = jnp.concatenate([low, block, high], axis=dim)
    return block


def live_flags(order, count, bricks):
    places = jnp.arange(bricks, dtype=jnp.int32)
    ranks = jnp.arange(order.shape[0], dtype=jnp.int32)
    match = (order[:, None] == places[None, :]) & (ranks[:, None] < count)
    return jnp.any(match, axis=0).astype(jnp.float32)


def to_blocks(tile, cols_x, cols_y, edge):
    return (
        tile.reshape(cols_x, edge, cols_y, edge, tile.shape[2], tile.shape[3])
        .transpose(0, 2, 1, 3, 4, 5)
        .reshape(cols_x * cols_y, edge, edge, tile.shape[2], tile.shape[3])
    )


def from_blocks(blocks, cols_x, cols_y):
    edge = blocks.shape[1]
    return (
        blocks.reshape(cols_x, cols_y, edge, edge, blocks.shape[3], blocks.shape[4])
        .transpose(0, 2, 1, 3, 4, 5)
        .reshape(cols_x * edge, cols_y * edge, blocks.shape[3], blocks.shape[4])
    )


def windows(padded, slots, cols_y, edge):
    span = edge + 2

    def single(place):
        start_x = place // cols_y * edge
        start_y = place % cols_y * edge
        nought = jnp.zeros((), jnp.int32)
        return lax.dynamic_slice(
            padded,
            (start_x, start_y, nought, nought),
            (span, span, padded.shape[2], padded.shape[3]),
        )

    return jax.vmap(single)(slots)


def conv_taps(wins, weight, edge):
    total = None
    for index, (ox, oy, oz) in enumerate(tap_offsets):
        piece = wins[:, ox : ox + edge, oy : oy + edge, oz : oz + edge, :].reshape(
            -1, wins.shape[-1]
        )
        term = jnp.dot(piece, weight[index], preferred_element_type=jnp.float32)
        total = term if total is None else total + term
    return total.reshape(wins.shape[0], edge, edge, edge, weight.shape[2])


def conv_back(wins, weight, edge):
    total = None
    for index, (ox, oy, oz) in enumerate(tap_offsets):
        piece = wins[
            :, 2 - ox : 2 - ox + edge, 2 - oy : 2 - oy + edge, 2 - oz : 2 - oz + edge, :
        ].reshape(-1, wins.shape[-1])
        term = lax.dot_general(
            piece, weight[index], (((1,), (1,)), ((), ())), preferred_element_type=jnp.float32
        )
        total = term if total is None else total + term
    return total.reshape(wins.shape[0], edge, edge, edge, weight.shape[1])


def tap_grads(wins, grads, edge):
    flat_grads = grads.reshape(-1, grads.shape[-1])
    terms = []
    for ox, oy, oz in tap_offsets:
        piece = wins[:, ox : ox + edge, oy : oy + edge, oz : oz + edge, :].reshape(
            -1, wins.shape[-1]
        )
        terms.append(
            lax.dot_general(
                piece, flat_grads, (((0,), (0,)), ((), ())), preferred_element_type=jnp.float32
            )
        )
    return jnp.stack(terms)


def down_patches(tile):
    size_x, size_y, depth, chans = tile.shape
    return (
        tile.reshape(size_x // 2, 2, size_y // 2, 2, depth // 2, 2, chans)
        .transpose(0, 2, 4, 1, 3, 5, 6)
        .reshape(-1, 8 * chans)
    )


def undo_patches(flat, size_x, size_y, depth, chans):
    return (
        flat.reshape(size_x // 2, size_y // 2, depth // 2, 2, 2, 2, chans)
        .transpose(0, 3, 1, 4, 2, 5, 6)
        .reshape(size_x, size_y, depth, chans)
    )


def silu_slope(value):
    sig = jax.nn.sigmoid(value)
    return sig * (1.0 + value * (1.0 - sig))


def pad_depth(tile):
    return jnp.pad(tile, ((0, 0), (0, 0), (1, 1), (0, 0)))


def local(features, voxel_mask, brick_order, brick_count, w_conv1, w_down, w_conv2, cotangent):
    feats = features[0]
    occupancy = voxel_mask[0]
    order = brick_order[0]
    count = brick_count[0]
    cot_tile = cotangent[0]
    size_x, size_y = (feats.shape[0], feats.shape[1])
    half_x, half_y = (size_x // 2, size_y // 2)
    bricks = GX * GY
    full_one, full_down, full_two = (
        lax.all_gather(w_conv1, ("tx", "ty"), axis=1, tiled=True),
        lax.all_gather(w_down, ("tx", "ty"), axis=1, tiled=True),
        lax.all_gather(w_conv2, ("tx", "ty"), axis=1, tiled=True),
    )
    kern_one = full_one.reshape(27, C1, C1)
    kern_down = full_down.reshape(8 * C1, C2)
    kern_two = full_two.reshape(27, C2, C2)
    live = live_flags(order, count, bricks).reshape(GX, GY)
    live_map = jnp.repeat(jnp.repeat(live, 8, axis=0), 8, axis=1)
    live_mask = occupancy.astype(jnp.float32) * live_map[..., None]
    masked = feats * live_mask[..., None].astype(jnp.bfloat16)
    slots = order[:CAP]
    padded_one = pad_depth(extended(masked, (("tx", 0), ("ty", 1)), 1))
    wins_one = windows(padded_one, slots, GY, 8)
    act_one = conv_taps(wins_one, kern_one, 8)
    mask_blocks = to_blocks(live_mask[..., None], GX, GY, 8)[slots]
    hidden_blocks = (mask_blocks * jax.nn.silu(act_one)).astype(jnp.bfloat16)
    hidden = from_blocks(
        jnp.zeros((bricks, 8, 8, 8, C1), jnp.bfloat16).at[slots].set(hidden_blocks), GX, GY
    )
    coarse_mask = live_mask.reshape(half_x, 2, half_y, 2, 4, 2).max(axis=(1, 3, 5))
    patches = down_patches(hidden)
    raw = jnp.dot(patches, kern_down, preferred_element_type=jnp.float32).reshape(
        half_x, half_y, 4, C2
    )
    down = (coarse_mask[..., None] * raw).astype(jnp.bfloat16)
    padded_down = pad_depth(extended(down, (("tx", 0), ("ty", 1)), 1))
    wins_two = windows(padded_down, slots, GY, 4)
    act_two = conv_taps(wins_two, kern_two, 4)
    act_tile = from_blocks(
        jnp.zeros((bricks, 4, 4, 4, C2), jnp.float32).at[slots].set(act_two), GX, GY
    )
    output = (coarse_mask[..., None] * (down.astype(jnp.float32) + act_tile)).astype(jnp.bfloat16)
    grad_two = coarse_mask[..., None].astype(jnp.bfloat16) * cot_tile
    padded_grad = pad_depth(extended(grad_two, (("tx", 0), ("ty", 1)), 1))
    grad_blocks = to_blocks(grad_two, GX, GY, 4)[slots]
    grad_conv2 = tap_grads(wins_two, grad_blocks, 4)
    back = conv_back(windows(padded_grad, slots, GY, 4), kern_two, 4)
    back_tile = from_blocks(
        jnp.zeros((bricks, 4, 4, 4, C2), jnp.float32).at[slots].set(back), GX, GY
    )
    grad_down_in = (coarse_mask[..., None] * (cot_tile.astype(jnp.float32) + back_tile)).astype(
        jnp.bfloat16
    )
    flat_in = grad_down_in.reshape(-1, C2)
    grad_down = lax.dot_general(
        patches, flat_in, (((0,), (0,)), ((), ())), preferred_element_type=jnp.float32
    )
    grad_hidden = undo_patches(
        lax.dot_general(
            flat_in, kern_down, (((1,), (1,)), ((), ())), preferred_element_type=jnp.float32
        ),
        size_x,
        size_y,
        8,
        C1,
    )
    hidden_grad_blocks = to_blocks(grad_hidden, GX, GY, 8)[slots]
    grad_one = (mask_blocks * hidden_grad_blocks * silu_slope(act_one)).astype(jnp.bfloat16)
    grad_conv1 = tap_grads(wins_one, grad_one, 8)
    flat_one = grad_conv1.reshape(27, C1 * C1)
    flat_down = grad_down.reshape(8, C1 * C2)
    flat_two = grad_conv2.reshape(27, C2 * C2)
    total_one, total_down, total_two = lax.psum(
        (flat_one, flat_down, flat_two), ("grp", "tx", "ty")
    )
    position = lax.axis_index(("tx", "ty"))
    shards = lax.axis_size(("tx", "ty"))
    width_one = C1 * C1 // shards
    width_down = C1 * C2 // shards
    width_two = C2 * C2 // shards
    share_one = lax.dynamic_slice_in_dim(total_one, position * width_one, width_one, 1)
    share_down = lax.dynamic_slice_in_dim(total_down, position * width_down, width_down, 1)
    share_two = lax.dynamic_slice_in_dim(total_two, position * width_two, width_two, 1)
    return (output[None], share_one, share_down, share_two)


def solution(mesh):
    return jax.shard_map(
        local,
        mesh=mesh,
        in_specs=(
            P("grp", "tx", "ty", None, None),
            P("grp", "tx", "ty", None),
            P(("grp", "tx", "ty"), None),
            P(("grp", "tx", "ty")),
            P(None, ("tx", "ty")),
            P(None, ("tx", "ty")),
            P(None, ("tx", "ty")),
            P("grp", "tx", "ty", None, None),
        ),
        out_specs=(
            P("grp", "tx", "ty", None, None),
            P(None, ("tx", "ty")),
            P(None, ("tx", "ty")),
            P(None, ("tx", "ty")),
        ),
        check_vma=False,
    )
```

profile of v0, /device:TPU:8, one launch (start us, length us, event | category | flops | bytes accessed | tf_op | source)
XLA Modules:
  0.0 957.6 jit_solution(13780769802894573607)
XLA Ops:
  10.0 1.8 bitcast_multiply_fusion
  12.5 1.4 collective-permute-start.1
  13.9 4.5 collective-permute-start
  20.0 1.3 collective-permute-start.9
  21.3 4.5 collective-permute-start.8
  26.5 180.4 %all-gather = bf16[128,72,27]{1,2,0:T(8,128)(2,1)S(1)} all-gather(bf16[1,72,27]{1,2,0:T(8,128)(2,1)S(1)} %bitcast.636), channel_id=1, replica_groups=mesh['grp'=2,'tx'=8,'ty'=16] {'tx','ty'}, dimensions={0}, use_global_device_ids=true | all-gather | bytes 501552 | tf_op jit(solution)/shard_map/all_gather | solution.py:144
  207.3 1.6 reshape.1031
  208.9 1.4 slice_reduce_fusion.46
  210.3 2.7 slice_reduce_fusion.27
  214.1 183.2 %all-gather.1 = bf16[128,144,8]{1,2,0:T(8,128)(2,1)S(1)} all-gather(bf16[1,144,8]{1,2,0:T(8,128)(2,1)S(1)} %bitcast.637), channel_id=1, replica_groups=mesh['grp'=2,'tx'=8,'ty'=16] {'tx','ty'}, dimensions={0}, use_global_device_ids=true | all-gather | bytes 297216 | tf_op jit(solution)/shard_map/all_gather | solution.py:145
  398.0 2.2 collective-permute-start.11
  400.3 2.6 collective-permute-start.10
  404.4 1.2 reshape.895
  424.6 1.2 gather_fusion
  425.8 1.2 gather_fusion.5
  430.2 3.4 collective-permute-start.3
  433.6 2.0 collective-permute-start.2
  436.4 1.5 reshape.926
  437.9 1.5 reshape.927
  440.8 1.5 reshape.930
  470.1 4.4 copy.113
  474.5 5.4 reshape.1035
  480.0 3.9 slice_reduce_fusion.19
  483.8 11.0 %slice_reduce_fusion = (bf16[36864]{0:T(1024)(128)(2,1)}, bf16[36864]{0:T(1024)(128)(2,1)}, bf16[36864]{0:T(1024)(128)(2,1)}, bf16[36864]{0:T(1024)(128)(2,1)}, ...) fusion(bf16[27,36864]{1,0:T(8,128)(2,1)S(1)} %bitcast.588), kind=kLoop, calls=%fused_computation.217 | loop fusion | bytes 2801664 | tf_op jit(solution)/shard_map/slice | solution.py:75
  494.8 1.7 squeeze.231
  506.4 1.2 fusion.31
  518.4 1.6 gather_fusion.4
  520.0 1.3 multiply_convert_fusion
  544.4 1.8 dot_general.445
  546.2 1.6 fusion
  548.4 1.3 collective-permute-start.5
  549.7 4.5 collective-permute-start.4
  556.5 3.0 collective-permute-start.7
  559.7 2.1 collective-permute-start.6
  565.5 1.2 reshape.957
  566.6 4.3 stack.195
  623.4 1.8 stack.213
  625.2 1.8 stack.214
  627.0 1.8 stack.215
  629.6 1.8 stack.217
  632.2 1.8 stack.219
  634.9 1.8 stack.221
  636.7 2.0 stack.222
  646.3 18.2 %stack.223 = f32[27,36864]{1,0:T(8,128)} concatenate(f32[1,36864]{1,0:T(1,128)S(1)} %stack.196, f32[1,36864]{1,0:T(1,128)S(1)} %stack.197, f32[1,36864]{1,0:T(1,128)S(1)} %stack.198, f32[1,36864]{1,0:T(1,128)S(1)} %stack.199, f32[1,36864]{1,0:T(1,128)S(1)} %stack.200, f32[1,36864]{1,0:T(1,128)S(1)} %stack.201, f32[1,36864]{1,0:T(1,128)S(1)} %stack.202, f32[1,36864]{1,0:T(1,128)S(1)} %stack.203, ...), dimensions={0} | concatenate | bytes 7962624 | tf_op jit(solution)/shard_map/stack | solution.py:105
  670.5 275.7 %all-reduce.6.cloned.1.call-done = (f32[27,9216]{1,0:T(8,128)}, f32[8,18432]{1,0:T(8,128)}, f32[27,36864]{1,0:T(8,128)}) async-done(((f32[27,9216]{1,0:T(8,128)}, f32[8,18432]{1,0:T(8,128)}, f32[27,36864]{1,0:T(8,128)}), (f32[27,9216]{1,0:T(8,128)}, f32[8,18432]{1,0:T(8,128)}, f32[27,36864]{1,0:T(8,128)})) %all-reduce.6.cloned.1.call-update) | async-done | bytes 5566480 | tf_op jit(solution)/shard_map/psum | solution.py:207
  946.2 1.4 constant_dynamic-slice_fusion.1
  947.7 1.4 constant_dynamic-slice_fusion
  949.0 1.5 constant_dynamic-slice_fusion.2
  (834 shorter events, 176.1 us)
Async XLA Ops:
  7.2 463.0 %all-gather.5.cloned.1.call-start = ((), (), s32[]{:S(2)}) async-start(), calls=%async_computation | async-start | bytes 3170304 | tf_op jit(solution)/shard_map/all_gather | solution.py:146
  12.5 417.0 %collective-permute-start.1 = (bf16[1,32,8,96]{3,2,1,0:T(8,128)(2,1)}, bf16[1,32,8,96]{3,2,1,0:T(8,128)(2,1)S(1)}, u32[]{:S(2)}, u32[]{:S(2)}) collective-permute-start(bf16[1,32,8,96]{3,2,1,0:T(8,128)(2,1)} %get-tuple-element.87), channel_id=1, source_target_pairs={{16,0},{32,16},{48,32},{64,48},{80,64},{96,80},{112,96},{17,1},{33... | collective-permute-start | bytes 147464 | tf_op jit(solution)/shard_map/ppermute | solution.py:24
  13.9 415.6 %collective-permute-start = (bf16[1,32,8,96]{3,2,1,0:T(8,128)(2,1)}, bf16[1,32,8,96]{3,2,1,0:T(8,128)(2,1)S(1)}, u32[]{:S(2)}, u32[]{:S(2)}) collective-permute-start(bf16[1,32,8,96]{3,2,1,0:T(8,128)(2,1)} %get-tuple-element.86), channel_id=1, source_target_pairs={{0,16},{16,32},{32,48},{48,64},{64,80},{80,96},{96,112},{1,17},{17... | collective-permute-start | bytes 147464 | tf_op jit(solution)/shard_map/ppermute | solution.py:21
  19.6 193.4 %copy-start.79 = (f32[8,16,4]{1,2,0:T(4,128)}, f32[8,16,4]{1,2,0:T(4,128)S(1)}, u32[]{:S(2)}) copy-start(f32[8,16,4]{1,2,0:T(4,128)S(1)} %multiply_reduce_fusion) | copy-start | bytes 6148
  20.0 377.4 %collective-permute-start.9 = (bf16[1,16,4,192]{3,2,1,0:T(4,128)(2,1)S(1)}, bf16[1,16,4,192]{3,2,1,0:T(4,128)(2,1)S(1)}, u32[]{:S(2)}, u32[]{:S(2)}) collective-permute-start(bf16[1,16,4,192]{3,2,1,0:T(4,128)(2,1)S(1)} %get-tuple-element.122), channel_id=1, source_target_pairs={{16,0},{32,16},{48,32},{64,48},{80,64},{96,80},{112,96},{17,1},{33... | collective-permute-start | bytes 73736 | tf_op jit(solution)/shard_map/ppermute | solution.py:24
  21.3 376.1 %collective-permute-start.8 = (bf16[1,16,4,192]{3,2,1,0:T(4,128)(2,1)S(1)}, bf16[1,16,4,192]{3,2,1,0:T(4,128)(2,1)S(1)}, u32[]{:S(2)}, u32[]{:S(2)}) collective-permute-start(bf16[1,16,4,192]{3,2,1,0:T(4,128)(2,1)S(1)} %get-tuple-element.121), channel_id=1, source_target_pairs={{0,16},{16,32},{32,48},{48,64},{64,80},{80,96},{96,112},{1,17},{17... | collective-permute-start | bytes 73736 | tf_op jit(solution)/shard_map/ppermute | solution.py:21
  25.9 920.3 %all-reduce.6.cloned.1.call-start = ((), (), s32[]{:S(2)}) async-start(), calls=%async_computation.1 | async-start | bytes 12976128 | tf_op jit(solution)/shard_map/psum | solution.py:207
  26.5 376.3 %copy-start.218 = (s32[2]{0:T(128)}, s32[2]{0:T(128)S(1)}, u32[]{:S(2)}) copy-start(s32[2]{0:T(128)S(1)} %get-tuple-element.179) | copy-start | bytes 28
  213.1 189.8 %copy-start.54 = (f32[8,16,4]{2,1,0:T(8,128)}, f32[8,16,4]{2,1,0:T(8,128)S(1)}, u32[]{:S(2)}) copy-start(f32[8,16,4]{2,1,0:T(8,128)S(1)} %copy.189) | copy-start | bytes 6148
  398.0 29.0 %collective-permute-start.11 = (bf16[10,1,4,192]{3,2,1,0:T(4,128)(2,1)}, bf16[10,1,4,192]{3,2,1,0:T(4,128)(2,1)}, u32[]{:S(2)}, u32[]{:S(2)}) collective-permute-start(bf16[10,1,4,192]{3,2,1,0:T(4,128)(2,1)} %get-tuple-element.118), channel_id=1, source_target_pairs={{1,0},{2,1},{3,2},{4,3},{5,4},{6,5},{7,6},{8,7},{9,8},{10,9},{11,1... | collective-permute-start | bytes 46088 | tf_op jit(solution)/shard_map/ppermute | solution.py:24
  400.3 26.8 %collective-permute-start.10 = (bf16[10,1,4,192]{3,2,1,0:T(4,128)(2,1)}, bf16[10,1,4,192]{3,2,1,0:T(4,128)(2,1)}, u32[]{:S(2)}, u32[]{:S(2)}) collective-permute-start(bf16[10,1,4,192]{3,2,1,0:T(4,128)(2,1)} %get-tuple-element.117), channel_id=1, source_target_pairs={{0,1},{1,2},{2,3},{3,4},{4,5},{5,6},{6,7},{7,8},{8,9},{9,10},{10,1... | collective-permute-start | bytes 46088 | tf_op jit(solution)/shard_map/ppermute | solution.py:21
  402.9 22.9 %copy-start.223 = (s32[1024]{0:T(1024)}, s32[1024]{0:T(1024)S(1)}, u32[]{:S(2)}) copy-start(s32[1024]{0:T(1024)S(1)} %pad_clamp_fusion) | copy-start | bytes 12292
  403.8 10.2 %copy-start.189 = (bf16[9216]{0:T(1024)(128)(2,1)S(1)}, bf16[9216]{0:T(1024)(128)(2,1)}, u32[]{:S(2)}) copy-start(bf16[9216]{0:T(1024)(128)(2,1)} %get-tuple-element.65) | copy-start | bytes 55300
  403.8 10.9 %copy-start.188 = (bf16[9216]{0:T(1024)(128)(2,1)S(1)}, bf16[9216]{0:T(1024)(128)(2,1)}, u32[]{:S(2)}) copy-start(bf16[9216]{0:T(1024)(128)(2,1)} %get-tuple-element.64) | copy-start | bytes 55300
  403.8 11.6 %copy-start.187 = (bf16[9216]{0:T(1024)(128)(2,1)S(1)}, bf16[9216]{0:T(1024)(128)(2,1)}, u32[]{:S(2)}) copy-start(bf16[9216]{0:T(1024)(128)(2,1)} %get-tuple-element.63) | copy-start | bytes 55300
  403.8 12.3 %copy-start.186 = (bf16[9216]{0:T(1024)(128)(2,1)S(1)}, bf16[9216]{0:T(1024)(128)(2,1)}, u32[]{:S(2)}) copy-start(bf16[9216]{0:T(1024)(128)(2,1)} %get-tuple-element.62) | copy-start | bytes 55300
  403.8 12.9 %copy-start.185 = (bf16[9216]{0:T(1024)(128)(2,1)S(1)}, bf16[9216]{0:T(1024)(128)(2,1)}, u32[]{:S(2)}) copy-start(bf16[9216]{0:T(1024)(128)(2,1)} %get-tuple-element.61) | copy-start | bytes 55300
  403.8 13.6 %copy-start.184 = (bf16[9216]{0:T(1024)(128)(2,1)S(1)}, bf16[9216]{0:T(1024)(128)(2,1)}, u32[]{:S(2)}) copy-start(bf16[9216]{0:T(1024)(128)(2,1)} %get-tuple-element.60) | copy-start | bytes 55300
  403.8 14.3 %copy-start.183 = (bf16[9216]{0:T(1024)(128)(2,1)S(1)}, bf16[9216]{0:T(1024)(128)(2,1)}, u32[]{:S(2)}) copy-start(bf16[9216]{0:T(1024)(128)(2,1)} %get-tuple-element.59) | copy-start | bytes 55300
  403.8 15.0 %copy-start.182 = (bf16[9216]{0:T(1024)(128)(2,1)S(1)}, bf16[9216]{0:T(1024)(128)(2,1)}, u32[]{:S(2)}) copy-start(bf16[9216]{0:T(1024)(128)(2,1)} %get-tuple-element.58) | copy-start | bytes 55300
  403.8 15.7 %copy-start.181 = (bf16[9216]{0:T(1024)(128)(2,1)S(1)}, bf16[9216]{0:T(1024)(128)(2,1)}, u32[]{:S(2)}) copy-start(bf16[9216]{0:T(1024)(128)(2,1)} %get-tuple-element.57) | copy-start | bytes 55300
  403.9 16.4 %copy-start.180 = (bf16[9216]{0:T(1024)(128)(2,1)S(1)}, bf16[9216]{0:T(1024)(128)(2,1)}, u32[]{:S(2)}) copy-start(bf16[9216]{0:T(1024)(128)(2,1)} %get-tuple-element.56) | copy-start | bytes 55300
  403.9 17.1 %copy-start.179 = (bf16[9216]{0:T(1024)(128)(2,1)S(1)}, bf16[9216]{0:T(1024)(128)(2,1)}, u32[]{:S(2)}) copy-start(bf16[9216]{0:T(1024)(128)(2,1)} %get-tuple-element.55) | copy-start | bytes 55300
  403.9 17.7 %copy-start.178 = (bf16[9216]{0:T(1024)(128)(2,1)S(1)}, bf16[9216]{0:T(1024)(128)(2,1)}, u32[]{:S(2)}) copy-start(bf16[9216]{0:T(1024)(128)(2,1)} %get-tuple-element.54) | copy-start | bytes 55300
  403.9 18.4 %copy-start.177 = (bf16[9216]{0:T(1024)(128)(2,1)S(1)}, bf16[9216]{0:T(1024)(128)(2,1)}, u32[]{:S(2)}) copy-start(bf16[9216]{0:T(1024)(128)(2,1)} %get-tuple-element.53) | copy-start | bytes 55300
  403.9 19.1 %copy-start.176 = (bf16[9216]{0:T(1024)(128)(2,1)S(1)}, bf16[9216]{0:T(1024)(128)(2,1)}, u32[]{:S(2)}) copy-start(bf16[9216]{0:T(1024)(128)(2,1)} %get-tuple-element.52) | copy-start | bytes 55300
  403.9 19.8 %copy-start.175 = (bf16[9216]{0:T(1024)(128)(2,1)S(1)}, bf16[9216]{0:T(1024)(128)(2,1)}, u32[]{:S(2)}) copy-start(bf16[9216]{0:T(1024)(128)(2,1)} %get-tuple-element.51) | copy-start | bytes 55300
  406.3 20.7 %copy-start.140 = (bf16[1,16,4,192]{3,2,1,0:T(4,128)(2,1)S(1)}, bf16[1,16,4,192]{3,2,1,0:T(4,128)(2,1)}, u32[]{:S(2)}) copy-start(bf16[1,16,4,192]{3,2,1,0:T(4,128)(2,1)} %copy-done.139) | copy-start | bytes 73732
  406.3 20.7 %copy-start.142 = (bf16[1,16,4,192]{3,2,1,0:T(4,128)(2,1)S(1)}, bf16[1,16,4,192]{3,2,1,0:T(4,128)(2,1)}, u32[]{:S(2)}) copy-start(bf16[1,16,4,192]{3,2,1,0:T(4,128)(2,1)} %copy-done.141) | copy-start | bytes 73732
  418.1 10.0 %copy-start.216 = (s32[2]{0:T(128)S(1)}, s32[2]{0:T(128)}, u32[]{:S(2)}) copy-start(s32[2]{0:T(128)} %get-tuple-element.81) | copy-start | bytes 28
  430.2 26.8 %collective-permute-start.3 = (bf16[18,1,8,96]{3,2,1,0:T(8,128)(2,1)}, bf16[18,1,8,96]{3,2,1,0:T(8,128)(2,1)}, u32[]{:S(2)}, u32[]{:S(2)}) collective-permute-start(bf16[18,1,8,96]{3,2,1,0:T(8,128)(2,1)} %get-tuple-element.85), channel_id=1, source_target_pairs={{1,0},{2,1},{3,2},{4,3},{5,4},{6,5},{7,6},{8,7},{9,8},{10,9},{11,1... | collective-permute-start | bytes 82952 | tf_op jit(solution)/shard_map/ppermute | solution.py:24
  433.6 23.4 %collective-permute-start.2 = (bf16[18,1,8,96]{3,2,1,0:T(8,128)(2,1)}, bf16[18,1,8,96]{3,2,1,0:T(8,128)(2,1)}, u32[]{:S(2)}, u32[]{:S(2)}) collective-permute-start(bf16[18,1,8,96]{3,2,1,0:T(8,128)(2,1)} %get-tuple-element.84), channel_id=1, source_target_pairs={{0,1},{1,2},{2,3},{3,4},{4,5},{5,6},{6,7},{7,8},{8,9},{9,10},{10,1... | collective-permute-start | bytes 82952 | tf_op jit(solution)/shard_map/ppermute | solution.py:21
  498.3 10.4 %copy-start.50 = (bf16[192,192]{1,0:T(8,128)(2,1)}, bf16[192,192]{1,0:T(8,128)(2,1)S(1)}, u32[]{:S(2)}) copy-start(bf16[192,192]{1,0:T(8,128)(2,1)S(1)} %squeeze.233) | copy-start | bytes 221188
  499.4 10.4 %copy-start.48 = (bf16[192,192]{1,0:T(8,128)(2,1)}, bf16[192,192]{1,0:T(8,128)(2,1)S(1)}, u32[]{:S(2)}) copy-start(bf16[192,192]{1,0:T(8,128)(2,1)S(1)} %squeeze.234) | copy-start | bytes 221188
  500.5 10.4 %copy-start.46 = (bf16[192,192]{1,0:T(8,128)(2,1)}, bf16[192,192]{1,0:T(8,128)(2,1)S(1)}, u32[]{:S(2)}) copy-start(bf16[192,192]{1,0:T(8,128)(2,1)S(1)} %squeeze.235) | copy-start | bytes 221188
  505.0 9.7 %copy-start.8 = (bf16[192,192]{1,0:T(8,128)(2,1)}, bf16[192,192]{1,0:T(8,128)(2,1)S(1)}, u32[]{:S(2)}) copy-start(bf16[192,192]{1,0:T(8,128)(2,1)S(1)} %squeeze.254) | copy-start | bytes 221188
  505.2 9.7 %copy-start.6 = (bf16[192,192]{1,0:T(8,128)(2,1)}, bf16[192,192]{1,0:T(8,128)(2,1)S(1)}, u32[]{:S(2)}) copy-start(bf16[192,192]{1,0:T(8,128)(2,1)S(1)} %squeeze.255) | copy-start | bytes 221188
  505.3 9.8 %copy-start.4 = (bf16[192,192]{1,0:T(8,128)(2,1)}, bf16[192,192]{1,0:T(8,128)(2,1)S(1)}, u32[]{:S(2)}) copy-start(bf16[192,192]{1,0:T(8,128)(2,1)S(1)} %squeeze.256) | copy-start | bytes 221188
  521.4 19.2 %copy-start.82 = (bf16[2,8,8,8,96]{4,3,2,1,0:T(8,128)(2,1)}, bf16[2,8,8,8,96]{4,3,2,1,0:T(8,128)(2,1)S(1)}, u32[]{:S(2)}) copy-start(bf16[2,8,8,8,96]{4,3,2,1,0:T(8,128)(2,1)S(1)} %get-tuple-element.88) | copy-start | bytes 589828
  548.4 8.0 collective-permute-start.5
  549.7 6.7 collective-permute-start.4
  556.5 14.5 %collective-permute-start.7 = (bf16[10,1,4,192]{3,1,2,0:T(2,128)(2,1)S(1)}, bf16[10,1,4,192]{3,1,2,0:T(2,128)(2,1)S(1)}, u32[]{:S(2)}, u32[]{:S(2)}) collective-permute-start(bf16[10,1,4,192]{3,1,2,0:T(2,128)(2,1)S(1)} %get-tuple-element.120), channel_id=1, source_target_pairs={{1,0},{2,1},{3,2},{4,3},{5,4},{6,5},{7,6},{8,7},{9,8},{10,9},{11,1... | collective-permute-start | bytes 46088 | tf_op jit(solution)/shard_map/ppermute | solution.py:24
  559.7 11.3 %collective-permute-start.6 = (bf16[10,1,4,192]{3,1,2,0:T(2,128)(2,1)S(1)}, bf16[10,1,4,192]{3,1,2,0:T(2,128)(2,1)S(1)}, u32[]{:S(2)}, u32[]{:S(2)}) collective-permute-start(bf16[10,1,4,192]{3,1,2,0:T(2,128)(2,1)S(1)} %get-tuple-element.119), channel_id=1, source_target_pairs={{0,1},{1,2},{2,3},{3,4},{4,5},{5,6},{6,7},{7,8},{8,9},{9,10},{10,1... | collective-permute-start | bytes 46088 | tf_op jit(solution)/shard_map/ppermute | solution.py:21
  607.5 10.5 %copy-start.138 = (f32[192,192]{1,0:T(8,128)S(1)}, f32[192,192]{1,0:T(8,128)}, u32[]{:S(2)}) copy-start(f32[192,192]{1,0:T(8,128)} %convolution_bitcast_fusion.8) | copy-start | bytes 442372
  623.4 10.7 %copy-start.130 = (f32[192,192]{1,0:T(8,128)S(1)}, f32[192,192]{1,0:T(8,128)}, u32[]{:S(2)}) copy-start(f32[192,192]{1,0:T(8,128)} %convolution_bitcast_fusion.11) | copy-start | bytes 442372
  628.7 10.0 %copy-start.52 = (bf16[192,192]{1,0:T(8,128)(2,1)S(1)}, bf16[192,192]{1,0:T(8,128)(2,1)}, u32[]{:S(2)}) copy-start(bf16[192,192]{1,0:T(8,128)(2,1)} %squeeze.232) | copy-start | bytes 221188
  629.6 10.3 %copy-start.51 = (bf16[192,192]{1,0:T(8,128)(2,1)S(1)}, bf16[192,192]{1,0:T(8,128)(2,1)}, u32[]{:S(2)}) copy-start(bf16[192,192]{1,0:T(8,128)(2,1)} %copy-done.50) | copy-start | bytes 221188
  632.2 9.9 %copy-start.47 = (bf16[192,192]{1,0:T(8,128)(2,1)S(1)}, bf16[192,192]{1,0:T(8,128)(2,1)}, u32[]{:S(2)}) copy-start(bf16[192,192]{1,0:T(8,128)(2,1)} %copy-done.46) | copy-start | bytes 221188
  (193 other events, 711.1 us)
Sparse Core Ops, SparseCore 0:
  26.0 119.7 all-gather.4
  664.7 281.4 all-reduce.5
where the time goes:
time: 968 us; the launch traced here: 958 us
  blocking collectives  364 us (38%)
  waiting for transfers between devices  276 us (29%)
  local copies, waits for them, and re-layouts  185 us (19%)
  matrix products  70.1 us (7%)
  starting transfers between devices  33 us (3%)
  between operations  19.1 us (2%)
  other arithmetic  11 us (1%)
    psum x1, waiting for transfers between devices, local(): lax.psum((flat_one, flat_down, flat_two), ('grp', 'tx', 'ty'))  276 us
    all_gather x1, blocking collectives, local(): lax.all_gather(w_down, ('tx', 'ty'), axis=1, tiled=True)  183 us
    all_gather x1, blocking collectives, local(): lax.all_gather(w_conv1, ('tx', 'ty'), axis=1, tiled=True)  180 us
    another operation x56, local copies, waits for them, and re-layouts, tap_grads(): return jnp.stack(terms)  50.4 us
    dot_general x54, matrix products, tap_grads(): lax.dot_general(piece, flat_grads, (((0,), (0,)), ((), ())), preferred_el...  42.6 us
    squeeze x54, local copies, waits for them, and re-layouts, conv_taps(): term = jnp.dot(piece, weight[index], preferred_element_type=jnp.float32)  29.6 us
    reshape x27, local copies, waits for them, and re-layouts, conv_back(): piece = wins[:, 2 - ox:2 - ox + edge, 2 - oy:2 - oy + edge, 2 - oz:2 - oz...  20.6 us
    ppermute x6, starting transfers between devices, extended(): lax.ppermute(lax.slice_in_dim(block, block.shape[dim] - width, None, axis...  20.3 us
  transfers between devices with their start and end apart: 14, of which 1 were waited for; matrix products, arithmetic and copies ran while one was open for 9% of the time, Pallas kernels for 0%

commit v1 on v0

v1 whole, which is shorter than its diff:
```python
import jax
import jax.numpy as jnp
from jax import lax
from jax.experimental import pallas as pl
from jax.experimental.pallas import tpu as pltpu
from jax.sharding import PartitionSpec as P

C1 = 96
C2 = 192
GX = 2
GY = 4
CAP = 2
GROUPS = 32
N_TX = 8
N_TY = 16
MESH = pl.DeviceIdType.MESH
f32 = jnp.float32
bf16 = jnp.bfloat16
TAPS = [(ox, oy, oz) for ox in range(3) for oy in range(3) for oz in range(3)]
VMEM_LIMIT = 60 * 1024 * 1024


def lane_tiles(rows):
    return [rows[:, i * 128 : (i + 1) * 128] for i in range(rows.shape[1] // 128)]


def relane(count, segments):
    lanes = lax.broadcasted_iota(jnp.int32, segments[0][0][0].shape, 1)
    out = [None] * count
    rolled = {}
    for tiles, src, dst, length in segments:
        while length > 0:
            step = min(length, 128 - src % 128, 128 - dst % 128)
            tile, shift = tiles[src // 128], (dst - src) % 128
            key = (id(tile), shift)
            if key not in rolled:
                rolled[key] = pltpu.roll(tile, shift, 1) if shift else tile
            low, high, target = dst % 128, dst % 128 + step, dst // 128
            base = jnp.zeros_like(tile) if out[target] is None else out[target]
            if step == 128:
                out[target] = rolled[key]
            else:
                inside = lanes < high
                if low:
                    inside = inside & (lanes >= low)
                out[target] = jnp.where(inside, rolled[key], base)
            src, dst, length = src + step, dst + step, length - step
    return [jnp.zeros_like(segments[0][0][0]) if t is None else t for t in out]


PIECES_ONE = [[(0, 0, 0, 72), (1, 0, 72, 24)], [(1, 24, 0, 48), (2, 0, 48, 48)], [(2, 48, 0, 24), (3, 0, 24, 72)]]
PIECES_DOWN = [
    [(0, 0, 0, 144), (1, 0, 144, 48)],
    [(1, 48, 0, 96), (2, 0, 96, 96)],
    [(2, 96, 0, 48), (3, 0, 48, 144)],
]
PIECES_TWO = [
    [(0, 0, 0, 192)],
    [(0, 192, 0, 96), (1, 0, 96, 96)],
    [(1, 96, 0, 192)],
    [(2, 0, 0, 192)],
    [(2, 192, 0, 96), (3, 0, 96, 96)],
    [(3, 96, 0, 192)],
]
BASE_ONE = 288


def to_row(shards, pieces, base, count):
    return relane(count, [(shards[s], base + a, b, n) for s, a, b, n in pieces])


def join(tiles):
    return tiles[0] if len(tiles) == 1 else jnp.concatenate(tiles, axis=1)


def depth_shifts(slab):
    axis = slab.ndim - 2
    depth = lax.broadcasted_iota(jnp.int32, slab.shape, axis)
    below = jnp.where(depth == 0, 0.0, pltpu.roll(slab, 1, axis))
    above = jnp.where(depth == 7, 0.0, pltpu.roll(slab, 7, axis))
    return below, slab, above


def first_level(slots, mp, mask, cm, wg, x1, act, pm, down, wd, w1g, wde, wdo, w1, hs):
    w1g[pl.ds(C1 * 32, 32 * 32), :] = jnp.zeros((32 * 32, 128), f32)
    wde[:, pl.ds(C1 * 8, 32 * 8), :] = jnp.zeros((2, 32 * 8, 128), f32)
    wdo[:, pl.ds(C1 * 8, 32 * 8), :] = jnp.zeros((2, 32 * 8, 128), f32)

    def unpack(a, carry):
        shards = [lane_tiles(wg[a * 4 + b].astype(f32)) for b in range(4)]
        for k in range(3):
            row = a * 3 + k
            w1g[pl.ds(pl.multiple_of(row * 32, 32), 32), :] = join(to_row(shards, PIECES_ONE[k], BASE_ONE, 1))
        last = [[tile[24:32] for tile in tiles] for tiles in shards]
        for k in range(3):
            at = pl.ds(pl.multiple_of((a * 3 + k) * 8, 8), 8)
            for dst, base in ((wde, 0), (wdo, 144)):
                for c, tile in enumerate(to_row(last, PIECES_DOWN[k], base, 2)):
                    dst[c, at, :] = tile
        return carry

    lax.fori_loop(0, GROUPS, unpack, 0)
    for t in range(27):
        w1[t * 128 : (t + 1) * 128, :] = w1g[pl.ds(t, 128, stride=32), :].astype(bf16)
    for t in range(8):
        src = wdo if t % 2 else wde
        for c in range(2):
            wd[t * 128 : (t + 1) * 128, c * 128 : (c + 1) * 128] = src[
                c, pl.ds(3 + t // 2, 128, stride=8), :
            ].astype(bf16)

    down[...] = jnp.zeros_like(down)
    hs[...] = jnp.zeros_like(hs)
    for i in range(CAP):
        place = slots[i]
        px, py = place // GY, place % GY
        window = mp[pl.ds(px * 8, 10), pl.ds(py * 8, 10)]
        shifted = depth_shifts(window)
        for t, (ox, oy, oz) in enumerate(TAPS):
            piece = shifted[oz][ox : ox + 8, oy : oy + 8].reshape(512, 128)
            x1[i * 512 : (i + 1) * 512, t * 128 : (t + 1) * 128] = piece.astype(bf16)
        value = jnp.dot(x1[i * 512 : (i + 1) * 512, :], w1[...], preferred_element_type=f32)
        act[i * 512 : (i + 1) * 512, :] = value
        live = mask[pl.ds(px * 8, 8), pl.ds(py * 8, 8)].reshape(512, 128)
        hidden = (live * jax.nn.silu(value)).astype(bf16).astype(f32).reshape(4, 2, 4, 2, 8, 128)
        for p in range(2):
            for q in range(2):
                for b in range(4):
                    hs[:, p * 2 + q, b * 16 : b * 16 + 8, :] = hidden[:, p, b, q]
        for t in range(8):
            patch = hs[:, t // 2, pl.ds(t % 2, 32, stride=2), :].reshape(128, 128)
            pm[i * 128 : (i + 1) * 128, t * 128 : (t + 1) * 128] = patch.astype(bf16)
        raw = jnp.dot(pm[i * 128 : (i + 1) * 128, :], wd[...], preferred_element_type=f32)
        coarse = cm[pl.ds(px * 4, 4), pl.ds(py * 4, 4)]
        down[pl.ds(px * 4, 4), pl.ds(py * 4, 4)] = (
            (coarse * raw.reshape(4, 4, 8, 256)).astype(bf16).astype(f32)
        )


def level_one(slots, mp, mask, cm, wg):
    return pl.pallas_call(
        first_level,
        grid_spec=pltpu.PrefetchScalarGridSpec(
            num_scalar_prefetch=1,
            grid=(1,),
            in_specs=[pl.BlockSpec(memory_space=pltpu.VMEM)] * 4,
            out_specs=[pl.BlockSpec(memory_space=pltpu.VMEM)] * 5,
            scratch_shapes=[
                pltpu.VMEM((128 * 32, 128), f32),
                pltpu.VMEM((2, 128 * 8, 128), f32),
                pltpu.VMEM((2, 128 * 8, 128), f32),
                pltpu.VMEM((27 * 128, 128), bf16),
                pltpu.VMEM((4, 4, 64, 128), f32),
            ],
        ),
        out_shape=[
            jax.ShapeDtypeStruct((1024, 27 * 128), bf16),
            jax.ShapeDtypeStruct((1024, 128), f32),
            jax.ShapeDtypeStruct((256, 1024), bf16),
            jax.ShapeDtypeStruct((8, 16, 8, 256), f32),
            jax.ShapeDtypeStruct((1024, 256), bf16),
        ],
        compiler_params=pltpu.CompilerParams(vmem_limit_bytes=VMEM_LIMIT),
        name="level_one",
    )(slots, mp, mask, cm, wg)


def second_level(slots, dp, gp, mask, cm, wg, x1, act, pm, wd, out, packed, big, w2, x2, r1, rde, rdo, gs):
    def unpack(a, carry):
        shards = [lane_tiles(wg[a * 4 + b].astype(f32)) for b in range(4)]
        for k in range(6):
            row = a * 6 + k
            for c, tile in enumerate(to_row(shards, PIECES_TWO[k], 0, 2)):
                big[c, pl.ds(pl.multiple_of(row * 32, 32), 32), :] = tile
        return carry

    lax.fori_loop(0, GROUPS, unpack, 0)
    big[:, pl.ds(C2 * 32, 64 * 32), :] = jnp.zeros((2, 64 * 32, 128), f32)

    def order(t, carry):
        for c in range(2):
            w2[pl.ds(pl.multiple_of(t * 256, 256), 256), c * 128 : (c + 1) * 128] = big[
                c, pl.ds(t, 256, stride=32), :
            ].astype(bf16)
        return carry

    lax.fori_loop(0, 27, order, 0)
    out[...] = jnp.zeros_like(out)
    grads, coarses, downs = [], [], []
    for i in range(CAP):
        place = slots[i]
        px, py = place // GY, place % GY
        shifted = depth_shifts(dp[pl.ds(px * 4, 6), pl.ds(py * 4, 6)])
        for t, (ox, oy, oz) in enumerate(TAPS):
            piece = shifted[oz][ox : ox + 4, oy : oy + 4].reshape(128, 256)
            x2[i * 128 : (i + 1) * 128, t * 256 : (t + 1) * 256] = piece.astype(bf16)
        downs.append(shifted[1][1:5, 1:5].reshape(128, 256))
        grads.append(gp[pl.ds(px * 4 + 1, 4), pl.ds(py * 4 + 1, 4)].reshape(128, 256))
        coarses.append(cm[pl.ds(px * 4, 4), pl.ds(py * 4, 4)].reshape(128, 256))
    grad_two = jnp.concatenate(grads, axis=0)
    coarse = jnp.concatenate(coarses, axis=0)
    value = jnp.dot(x2[...], w2[...], preferred_element_type=f32)
    result = coarse * (jnp.concatenate(downs, axis=0) + value)
    for i in range(CAP):
        place = slots[i]
        px, py = place // GY, place % GY
        out[pl.ds(px * 4, 4), pl.ds(py * 4, 4)] = result[i * 128 : (i + 1) * 128].reshape(4, 4, 8, 256)

    turned = grad_two.T.astype(bf16)
    for t in range(27):
        flipped = jnp.dot(turned, x2[:, t * 256 : (t + 1) * 256], preferred_element_type=f32)
        flipped = flipped.T
        for c in range(2):
            big[c, t * 256 : (t + 1) * 256, :] = flipped[:, c * 128 : (c + 1) * 128]

    for i in range(CAP):
        place = slots[i]
        px, py = place // GY, place % GY
        shifted = depth_shifts(gp[pl.ds(px * 4, 6), pl.ds(py * 4, 6)])
        for t, (ox, oy, oz) in enumerate(TAPS):
            piece = shifted[2 - oz][2 - ox : 6 - ox, 2 - oy : 6 - oy].reshape(128, 256)
            x2[i * 128 : (i + 1) * 128, t * 256 : (t + 1) * 256] = piece.astype(bf16)
    back = None
    for t in range(27):
        term = lax.dot_general(
            x2[:, t * 256 : (t + 1) * 256],
            w2[t * 256 : (t + 1) * 256, :],
            (((1,), (1,)), ((), ())),
            preferred_element_type=f32,
        )
        back = term if back is None else back + term
    grad_in = (grad_two + coarse * back).astype(bf16)

    rde[...] = jnp.zeros_like(rde)
    rdo[...] = jnp.zeros_like(rdo)
    turned_in = grad_in.astype(f32).T.astype(bf16)
    for t in range(8):
        flipped = jnp.dot(turned_in, pm[:, t * 128 : (t + 1) * 128], preferred_element_type=f32)
        dst = rdo if t % 2 else rde
        flipped = flipped.T
        for c in range(2):
            dst[c, (3 + t // 2) * 128 : (4 + t // 2) * 128, :] = flipped[:, c * 128 : (c + 1) * 128]

    for i in range(CAP):
        place = slots[i]
        px, py = place // GY, place % GY
        for t in range(8):
            part = lax.dot_general(
                grad_in[i * 128 : (i + 1) * 128],
                wd[t * 128 : (t + 1) * 128, :],
                (((1,), (1,)), ((), ())),
                preferred_element_type=f32,
            )
            gs[:, t // 2, pl.ds(t % 2, 32, stride=2), :] = part.reshape(4, 32, 128)
        rows = []
        for p in range(2):
            for b in range(4):
                for q in range(2):
                    rows.append(gs[:, p * 2 + q, b * 16 : b * 16 + 8, :])
        hidden = jnp.stack(rows, axis=1).reshape(512, 128)
        live = mask[pl.ds(px * 8, 8), pl.ds(py * 8, 8)].reshape(512, 128)
        value = act[i * 512 : (i + 1) * 512, :]
        sig = jax.nn.sigmoid(value)
        grad_one = live * hidden * (sig * (1.0 + value * (1.0 - sig)))
        turned_one = grad_one.astype(bf16).astype(f32).T.astype(bf16)
        for t in range(27):
            flipped = jnp.dot(
                turned_one, x1[i * 512 : (i + 1) * 512, t * 128 : (t + 1) * 128], preferred_element_type=f32
            ).T
            at = pl.ds(t * 128, 128)
            if i:
                r1[at, :] = r1[at, :] + flipped
            else:
                r1[at, :] = flipped

    edge = lax.broadcasted_iota(jnp.int32, (8, 128), 0) < 3

    def pack(a, carry):
        segs = [[] for _ in range(4)]
        lasts = [[] for _ in range(4)]
        for k in range(6):
            ci = a * 6 + k
            tiles = [big[c, pl.ds(ci, 32, stride=256), :] for c in range(2)]
            for s, at, lane, n in PIECES_TWO[k]:
                segs[s].append((tiles, lane, at, n))
        for k in range(3):
            ci = a * 3 + k
            tiles = [r1[pl.ds(ci, 32, stride=128), :]]
            for s, at, lane, n in PIECES_ONE[k]:
                segs[s].append((tiles, lane, BASE_ONE + at, n))
            for src, base in ((rde, 0), (rdo, 144)):
                tiles = [src[c, pl.ds(ci, 8, stride=128), :] for c in range(2)]
                for s, at, lane, n in PIECES_DOWN[k]:
                    lasts[s].append((tiles, lane, base + at, n))
        for s in range(4):
            wide = relane(3, segs[s])
            tail = relane(3, lasts[s])
            done = [
                jnp.concatenate([w[:24], jnp.where(edge, w[24:], l)], axis=0) for w, l in zip(wide, tail)
            ]
            packed[a * 4 + s] = join(done).astype(bf16)
        return carry

    lax.fori_loop(0, GROUPS, pack, 0)


def level_two(slots, dp, gp, mask, cm, wg, x1, act, pm, wd):
    return pl.pallas_call(
        second_level,
        grid_spec=pltpu.PrefetchScalarGridSpec(
            num_scalar_prefetch=1,
            grid=(1,),
            in_specs=[pl.BlockSpec(memory_space=pltpu.VMEM)] * 9,
            out_specs=[pl.BlockSpec(memory_space=pltpu.VMEM)] * 2,
            scratch_shapes=[
                pltpu.VMEM((2, 32 * 256, 128), f32),
                pltpu.VMEM((27 * 256, 256), bf16),
                pltpu.VMEM((256, 27 * 256), bf16),
                pltpu.VMEM((32 * 128, 128), f32),
                pltpu.VMEM((2, 8 * 128, 128), f32),
                pltpu.VMEM((2, 8 * 128, 128), f32),
                pltpu.VMEM((4, 4, 64, 128), f32),
            ],
        ),
        out_shape=[
            jax.ShapeDtypeStruct((8, 16, 8, 256), f32),
            jax.ShapeDtypeStruct((128, 32, 384), bf16),
        ],
        compiler_params=pltpu.CompilerParams(vmem_limit_bytes=VMEM_LIMIT),
        name="level_two",
    )(slots, dp, gp, mask, cm, wg, x1, act, pm, wd)


def pack_shard(w_conv1, w_down, w_conv2):
    top = jnp.concatenate([w_conv2, w_conv1, jnp.zeros((27, 24), w_conv1.dtype)], axis=1)
    low = jnp.pad(w_down.reshape(4, 288), ((0, 1), (0, 96)))
    return jnp.concatenate([top, low], axis=0)


def unpack_shard(total):
    return total[:27, 288:360], total[27:31, :288].reshape(8, 144), total[:27, :288]


def barrier_with(peers):
    barrier = pltpu.get_barrier_semaphore()
    for peer in peers:
        pl.semaphore_signal(barrier, inc=1, device_id=peer, device_id_type=MESH)
    pl.semaphore_wait(barrier, len(peers))


def place():
    grp, tx, ty = lax.axis_index("grp"), lax.axis_index("tx"), lax.axis_index("ty")
    return grp, tx, ty, ty // 8, (ty // 2) % 4, ty % 2


def other(value, bits):
    if bits == 1:
        return value + 1 - 2 * (value % 2)
    if bits == 2:
        return (value + 2) % 4
    return 3 - value


def ring_peers(grp, tx, ty):
    return [(grp, (tx + d) % N_TX, ty) for d in range(1, N_TX)]


def cube_peers(grp, tx, hi, y, core):
    def ty_of(h, v, c):
        return h * 8 + v * 2 + c

    return {
        "core": (grp, tx, ty_of(hi, y, 1 - core)),
        "y1": (grp, tx, ty_of(hi, other(y, 1), core)),
        "y3": (grp, tx, ty_of(hi, other(y, 3), core)),
        "x": (1 - grp, tx, ty_of(1 - hi, y, core)),
        "grp": (1 - grp, tx, ty_of(hi, y, core)),
    }


STEPS = [(dx, dy) for dx in (-1, 0, 1) for dy in (-1, 0, 1) if dx or dy]


def halo_peers(grp, tx, ty):
    return [(grp, (tx + dx + N_TX) % N_TX, (ty + dy + N_TY) % N_TY) for dx, dy in STEPS]


def edge_out(step, size):
    return pl.ds(0, 1) if step < 0 else pl.ds(size - 1, 1) if step > 0 else pl.ds(0, size)


def edge_in(step, size):
    return pl.ds(size + 1, 1) if step < 0 else pl.ds(0, 1) if step > 0 else pl.ds(1, size)


def halo_copies(src, dst, peers, send, recv, base):
    size_x, size_y = src.shape[0], src.shape[1]
    copies = []
    for k, (dx, dy) in enumerate(STEPS):
        copies.append(
            pltpu.make_async_remote_copy(
                src_ref=src.at[edge_out(dx, size_x), edge_out(dy, size_y)],
                dst_ref=dst.at[edge_in(dx, size_x), edge_in(dy, size_y)],
                send_sem=send.at[base + k],
                recv_sem=recv.at[base + k],
                device_id=peers[k],
                device_id_type=MESH,
            )
        )
    return copies


def clear_edges(dst, tx, ty):
    size_x, size_y = dst.shape[0], dst.shape[1]

    @pl.when(tx == 0)
    def _():
        dst[0:1] = jnp.zeros((1,) + dst.shape[1:], dst.dtype)

    @pl.when(tx == N_TX - 1)
    def _():
        dst[size_x - 1 : size_x] = jnp.zeros((1,) + dst.shape[1:], dst.dtype)

    @pl.when(ty == 0)
    def _():
        dst[:, 0:1] = jnp.zeros((size_x, 1) + dst.shape[2:], dst.dtype)

    @pl.when(ty == N_TY - 1)
    def _():
        dst[:, size_y - 1 : size_y] = jnp.zeros((size_x, 1) + dst.shape[2:], dst.dtype)


def gather_kernel(shard, tile, grad, wg, mp, gp, send, recv, own):
    grp, tx, ty, hi, y, core = place()
    cube = cube_peers(grp, tx, hi, y, core)
    line = ring_peers(grp, tx, ty)
    around = halo_peers(grp, tx, ty)
    barrier_with(line + [cube["core"], cube["y1"], cube["y3"], cube["x"]] + around)
    sent = []

    def start(k, src, dst, peer):
        copy = pltpu.make_async_remote_copy(
            src_ref=src, dst_ref=dst, send_sem=send.at[k], recv_sem=recv.at[k], device_id=peer, device_id_type=MESH
        )
        copy.start()
        sent.append(copy)
        return copy

    line_copies = [start(16 + d, shard, wg.at[tx, hi, y, core], line[d]) for d in range(N_TX - 1)]
    mine = pltpu.make_async_copy(shard, wg.at[tx, hi, y, core], own.at[0])
    mine.start()
    halos = halo_copies(tile, mp, around, send, recv, 0) + halo_copies(grad, gp, around, send, recv, 8)
    for copy in halos:
        copy.start()
    inner = [
        pltpu.make_async_copy(tile, mp.at[pl.ds(1, 16), pl.ds(1, 32)], own.at[1]),
        pltpu.make_async_copy(grad, gp.at[pl.ds(1, 8), pl.ds(1, 16)], own.at[2]),
    ]
    for copy in inner:
        copy.start()

    mine.wait()
    for copy in line_copies:
        copy.wait_recv()
    column = wg.at[:, hi, y, core]
    across = start(23, column, column, cube["x"])
    partner = [start(30, column, column, cube["core"])]
    across.wait_recv()
    first, second = pl.ds(0, 16), pl.ds(16, 16)

    def part(v, rows):
        return wg.at[:, :, v, core, rows]

    near = start(24, part(y, first), part(y, first), cube["y1"])
    far = start(25, part(y, second), part(y, second), cube["y3"])
    twin = wg.at[:, 1 - hi, y, core]
    partner.append(start(31, twin, twin, cube["core"]))
    y1, y2, y3 = other(y, 1), other(y, 2), other(y, 3)
    near.wait_recv()
    far.wait_recv()
    last = [
        start(26, part(y, first), part(y, first), cube["y3"]),
        start(27, part(y1, first), part(y1, first), cube["y3"]),
        start(28, part(y, second), part(y, second), cube["y1"]),
        start(29, part(y3, second), part(y3, second), cube["y1"]),
    ]
    partner.append(start(32, part(y1, first), part(y1, first), cube["core"]))
    partner.append(start(33, part(y3, second), part(y3, second), cube["core"]))
    arrived = [part(y3, first), part(y2, first), part(y1, second), part(y2, second)]
    for k, (copy, ref) in enumerate(zip(last, arrived)):
        copy.wait_recv()
        partner.append(start(34 + k, ref, ref, cube["core"]))
    for copy in halos:
        copy.wait()
    for copy in inner:
        copy.wait()
    for copy in partner:
        copy.wait_recv()
    for copy in sent:
        copy.wait_send()
    clear_edges(mp, tx, ty)
    clear_edges(gp, tx, ty)


def gather(shard, tile, grad):
    return pl.pallas_call(
        gather_kernel,
        in_specs=[pl.BlockSpec(memory_space=pltpu.VMEM)] * 3,
        out_specs=[pl.BlockSpec(memory_space=pltpu.VMEM)] * 3,
        out_shape=[
            jax.ShapeDtypeStruct((8, 2, 4, 2, 32, 384), bf16),
            jax.ShapeDtypeStruct((18, 34, 8, 128), f32),
            jax.ShapeDtypeStruct((10, 18, 8, 256), f32),
        ],
        scratch_shapes=[
            pltpu.SemaphoreType.DMA((38,)),
            pltpu.SemaphoreType.DMA((38,)),
            pltpu.SemaphoreType.DMA((3,)),
        ],
        compiler_params=pltpu.CompilerParams(collective_id=0, has_side_effects=True, vmem_limit_bytes=VMEM_LIMIT),
        name="gather",
    )(shard, tile, grad)


def halo_kernel(tile, dst, send, recv, own):
    grp, tx, ty, _, _, _ = place()
    around = halo_peers(grp, tx, ty)
    barrier_with(around)
    halos = halo_copies(tile, dst, around, send, recv, 0)
    for copy in halos:
        copy.start()
    inner = pltpu.make_async_copy(tile, dst.at[pl.ds(1, 8), pl.ds(1, 16)], own.at[0])
    inner.start()
    inner.wait()
    for copy in halos:
        copy.wait()
    clear_edges(dst, tx, ty)


def halo(tile):
    return pl.pallas_call(
        halo_kernel,
        in_specs=[pl.BlockSpec(memory_space=pltpu.VMEM)],
        out_specs=pl.BlockSpec(memory_space=pltpu.VMEM),
        out_shape=jax.ShapeDtypeStruct((10, 18, 8, 256), f32),
        scratch_shapes=[
            pltpu.SemaphoreType.DMA((8,)),
            pltpu.SemaphoreType.DMA((8,)),
            pltpu.SemaphoreType.DMA((1,)),
        ],
        compiler_params=pltpu.CompilerParams(collective_id=1, has_side_effects=True, vmem_limit_bytes=VMEM_LIMIT),
        name="halo",
    )(tile)


def scatter_kernel(packed, total, sums, rd, ry2, ry1, rx, rz, half, rg, send, recv):
    grp, tx, ty, hi, y, core = place()
    cube = cube_peers(grp, tx, hi, y, core)
    line = ring_peers(grp, tx, ty)
    barrier_with(line + [cube[k] for k in ("core", "y1", "y3", "x", "grp")])
    y1, y2, y3 = other(y, 1), other(y, 2), other(y, 3)
    sent = []

    def start(k, src, dst, peer):
        copy = pltpu.make_async_remote_copy(
            src_ref=src, dst_ref=dst, send_sem=send.at[k], recv_sem=recv.at[k], device_id=peer, device_id_type=MESH
        )
        copy.start()
        sent.append(copy)
        return copy

    def add(z, h, v, rows, left, right):
        both = left[...].astype(f32) + right[...].astype(f32)
        sums[z, h, v, rows, :] = both.astype(bf16)

    first, second, whole = pl.ds(0, 16), pl.ds(16, 16), pl.ds(0, 32)

    order = [y2, y3, y1, y]
    pieces = [start(k, packed.at[:, :, v, 1 - core], rd.at[:, :, v], cube["core"]) for k, v in enumerate(order)]
    for k, v in enumerate(order):
        pieces[k].wait_recv()

        def take(z, carry):
            for h in range(2):
                add(z, h, v, whole, packed.at[z, h, v, core], rd.at[z, h, v])
            return carry

        lax.fori_loop(0, 8, take, 0)

    def part(v, rows):
        return sums.at[:, :, v, rows]

    last = [
        start(4, part(y3, first), ry2.at[0, :, :, first], cube["y3"]),
        start(5, part(y2, first), ry2.at[1, :, :, first], cube["y3"]),
        start(6, part(y1, second), ry2.at[0, :, :, second], cube["y1"]),
        start(7, part(y2, second), ry2.at[1, :, :, second], cube["y1"]),
    ]
    for copy in last:
        copy.wait_recv()

    def take_far(z, carry):
        for h in range(2):
            add(z, h, y, whole, sums.at[z, h, y], ry2.at[0, z, h])
            add(z, h, y1, first, sums.at[z, h, y1, first], ry2.at[1, z, h, first])
            add(z, h, y3, second, sums.at[z, h, y3, second], ry2.at[1, z, h, second])
        return carry

    lax.fori_loop(0, 8, take_far, 0)
    near = [
        start(8, part(y1, first), ry1.at[:, :, first], cube["y1"]),
        start(9, part(y3, second), ry1.at[:, :, second], cube["y3"]),
    ]
    for copy in near:
        copy.wait_recv()

    def take_near(z, carry):
        for h in range(2):
            add(z, h, y, whole, sums.at[z, h, y], ry1.at[z, h])
        return carry

    lax.fori_loop(0, 8, take_near, 0)

    across = start(10, sums.at[:, 1 - hi, y], rx, cube["x"])
    across.wait_recv()

    def take_across(z, carry):
        add(z, hi, y, whole, sums.at[z, hi, y], rx.at[z])
        return carry

    lax.fori_loop(0, 8, take_across, 0)
    spread = [
        start(11 + d, sums.at[(tx + d + 1) % N_TX, hi, y], rz.at[d], line[d]) for d in range(N_TX - 1)
    ]
    value = sums[tx, hi, y].astype(f32)
    for d, copy in enumerate(spread):
        copy.wait_recv()
        value = value + rz[d].astype(f32)
    half[...] = value
    swap = start(18, half, rg, cube["grp"])
    swap.wait_recv()
    total[...] = half[...] + rg[...]
    for copy in sent:
        copy.wait_send()


def scatter(packed):
    return pl.pallas_call(
        scatter_kernel,
        in_specs=[pl.BlockSpec(memory_space=pltpu.VMEM)],
        out_specs=pl.BlockSpec(memory_space=pltpu.VMEM),
        out_shape=jax.ShapeDtypeStruct((32, 384), f32),
        scratch_shapes=[
            pltpu.VMEM((8, 2, 4, 32, 384), bf16),
            pltpu.VMEM((8, 2, 4, 32, 384), bf16),
            pltpu.VMEM((2, 8, 2, 32, 384), bf16),
            pltpu.VMEM((8, 2, 32, 384), bf16),
            pltpu.VMEM((8, 32, 384), bf16),
            pltpu.VMEM((7, 32, 384), bf16),
            pltpu.VMEM((32, 384), f32),
            pltpu.VMEM((32, 384), f32),
            pltpu.SemaphoreType.DMA((19,)),
            pltpu.SemaphoreType.DMA((19,)),
        ],
        compiler_params=pltpu.CompilerParams(collective_id=2, has_side_effects=True, vmem_limit_bytes=VMEM_LIMIT),
        name="scatter",
    )(packed)


def live_flags(order, count, bricks):
    places = jnp.arange(bricks, dtype=jnp.int32)
    ranks = jnp.arange(order.shape[0], dtype=jnp.int32)
    match = (order[:, None] == places[None, :]) & (ranks[:, None] < count)
    return jnp.any(match, axis=0).astype(f32)


def local(features, voxel_mask, brick_order, brick_count, w_conv1, w_down, w_conv2, cotangent):
    order = brick_order[0]
    slots = order[:CAP]
    shard = pack_shard(w_conv1, w_down, w_conv2)
    live = live_flags(order, brick_count[0], GX * GY).reshape(GX, GY)
    live_map = jnp.repeat(jnp.repeat(live, 8, axis=0), 8, axis=1)
    live_mask = voxel_mask[0].astype(f32) * live_map[..., None]
    mask = jnp.broadcast_to(live_mask[..., None], (16, 32, 8, 128))
    masked = jnp.pad(features[0].astype(f32), ((0, 0), (0, 0), (0, 0), (0, 32))) * mask
    coarse = live_mask.reshape(8, 2, 16, 2, 4, 2).max(axis=(1, 3, 5))
    coarse = jnp.broadcast_to(jnp.pad(coarse, ((0, 0), (0, 0), (0, 4)))[..., None], (8, 16, 8, 256))
    grad_two = jnp.pad(cotangent[0].astype(f32), ((0, 0), (0, 0), (0, 4), (0, 64))) * coarse
    wg, mp, gp = gather(shard, masked, grad_two)
    wg = wg.reshape(128, 32, 384)
    x1, act, pm, down, wd = level_one(slots, mp, mask, coarse, wg)
    dp = halo(down)
    out, packed = level_two(slots, dp, gp, mask, coarse, wg, x1, act, pm, wd)
    total = scatter(packed.reshape(8, 2, 4, 2, 32, 384))
    one, low, two = unpack_shard(total)
    return out[None, :, :, :4, :C2].astype(bf16), one, low, two


def solution(mesh):
    return jax.shard_map(
        local,
        mesh=mesh,
        in_specs=(
            P("grp", "tx", "ty", None, None),
            P("grp", "tx", "ty", None),
            P(("grp", "tx", "ty"), None),
            P(("grp", "tx", "ty")),
            P(None, ("tx", "ty")),
            P(None, ("tx", "ty")),
            P(None, ("tx", "ty")),
            P("grp", "tx", "ty", None, None),
        ),
        out_specs=(
            P("grp", "tx", "ty", None, None),
            P(None, ("tx", "ty")),
            P(None, ("tx", "ty")),
            P(None, ("tx", "ty")),
        ),
        check_vma=False,
    )
```

time: 968 us -> 170 us (0.18)
  blocking collectives: 364 us -> 0 us
  waiting for transfers between devices: 276 us -> 0 us
  local copies, waits for them, and re-layouts: 185 us -> 12.7 us
  Pallas kernels: 0 us -> 146 us
  matrix products: 70.1 us -> 0 us
  starting transfers between devices: 33 us -> 0 us
  between operations: 19.1 us -> 1.36 us
    all_gather x2 -> x0, blocking collectives: 364 us -> none  [the longest x1 183 us: local(): lax.all_gather(w_down, ('tx', 'ty'), axis=1, tiled=True)]
    psum x1 -> x0, waiting for transfers between devices: 276 us -> none  [local(): lax.psum((flat_one, flat_down, flat_two), ('grp', 'tx', 'ty'))]
    pallas_call x0 -> x5, Pallas kernels: none -> 146 us  [the longest x1 43.7 us: scatter(): pl.pallas_call(scatter_kernel, in_specs=[pl.BlockSpec(memory_space=pltpu....]
    dot_general x138 -> x0, matrix products: 70.1 us -> none  [the longest x54 42.6 us: tap_grads(): lax.dot_general(piece, flat_grads, (((0,), (0,)), ((), ())), preferred_el...]
    another operation x58 -> x0, local copies, waits for them, and re-layouts: 50.7 us -> none  [the longest x56 50.4 us: tap_grads(): return jnp.stack(terms)]
    reshape x60 -> x2, local copies, waits for them, and re-layouts: 41.5 us -> 1.45 us  [the longest x1 0.77 us: pack_shard(): low = jnp.pad(w_down.reshape(4, 288), ((0, 1), (0, 96)))]
    ppermute x12 -> x0, starting transfers between devices: 32.9 us -> none  [the longest x6 20.3 us: extended(): lax.ppermute(lax.slice_in_dim(block, block.shape[dim] - width, None, axis...]
    squeeze x54 -> x0, local copies, waits for them, and re-layouts: 29.6 us -> none  [conv_taps(): term = jnp.dot(piece, weight[index], preferred_element_type=jnp.float32)]
  transfers between devices with their start and end apart: 14 -> 0, of which waited for: 1 -> 0; matrix products, arithmetic and copies ran while one was open for 9% -> 0% of each run, Pallas kernels for 0% -> 0%
where the time goes in v1:
time: 170 us; the launch traced here: 167 us
  Pallas kernels  146 us (86%)
  local copies, waits for them, and re-layouts  12.7 us (7%)
  other arithmetic  7.07 us (4%)
    pallas_call x1, Pallas kernels, scatter(): pl.pallas_call(scatter_kernel, in_specs=[pl.BlockSpec(memory_space=pltpu....  43.7 us
    pallas_call x1, Pallas kernels, gather(): pl.pallas_call(gather_kernel, in_specs=[pl.BlockSpec(memory_space=pltpu.V...  41.5 us
    pallas_call x1, Pallas kernels, level_two(): pl.pallas_call(second_level, grid_spec=pltpu.PrefetchScalarGridSpec(num_s...  33.8 us
    pallas_call x1, Pallas kernels, level_one(): pl.pallas_call(first_level, grid_spec=pltpu.PrefetchScalarGridSpec(num_sc...  15.7 us
    pallas_call x1, Pallas kernels, halo(): pl.pallas_call(halo_kernel, in_specs=[pl.BlockSpec(memory_space=pltpu.VME...  11.4 us

profile of v1, /device:TPU:8, one launch (start us, length us, event | category | flops | bytes accessed | tf_op | source)
XLA Modules:
  0.0 167.2 jit_solution(18215860114185241125)
XLA Ops:
  1.3 0.7 fusion.4
  2.0 1.2 slice_bitcast_fusion.slots
  3.2 0.1 reshape.63
  3.3 0.1 copy.25
  3.4 0.1 broadcast_in_dim.29
  3.5 0.1 reshape.59
  3.5 0.8 reshape.58
  4.3 0.1 copy.28
  4.4 1.4 fusion.2.shard
  5.9 0.1 copy.26
  5.9 0.0 copy-start.1
  5.9 0.1 broadcast_in_dim.32
  6.0 0.1 broadcast_in_dim.33
  6.1 0.9 bitcast_multiply_fusion
  7.0 0.8 convert_element_type.46
  7.8 0.1 copy.27
  7.9 0.6 convert_element_type.51
  8.5 0.3 multiply_reduce_fusion
  8.8 0.1 copy.30
  8.9 1.2 broadcast_in_dim.34.cm
  10.1 0.0 copy-done.1
  10.1 0.0 copy-start
  10.1 1.2 convert_multiply_fusion.1.grad
  11.3 1.9 %broadcast_in_dim.31.mask = f32[16,32,8,128]{3,2,1,0:T(8,128)} broadcast(f32[16,32,8]{2,1,0:T(8,128)S(1)} %copy.27), dimensions={0,1,2} | broadcast | bytes 2113536 | tf_op jit(solution)/shard_map/broadcast_in_dim | solution.py:684
  13.2 0.0 copy-done
  13.2 1.7 %convert_multiply_fusion.tile = f32[16,32,8,128]{3,2,1,0:T(8,128)} fusion(f32[16,32,8]{2,1,0:T(8,128)S(1)} %copy.27, bf16[16,32,8,96]{3,2,1,0:T(8,128)(2,1)S(1)} %bitcast.25), kind=kLoop, calls=%fused_computation | loop fusion | flops 1048576 | bytes 2899968 | tf_op jit(solution)/shard_map/mul | solution.py:685
  14.9 41.5 %gather.1 = (bf16[8,2,4,2,32,384]{5,4,3,2,1,0:T(8,128)(2,1)}, f32[18,34,8,128]{3,2,1,0:T(8,128)}, f32[10,18,8,256]{3,2,1,0:T(8,128)}) custom-call(bf16[32,384]{1,0:T(8,128)(2,1)} %fusion.2.shard, f32[16,32,8,128]{3,2,1,0:T(8,128)} %convert_multiply_fusion.tile, f32[8,16,8,256]{3,2,1,0:T(8,128)} %convert_multiply_fusion.1.grad), custom_call_target="tpu_custom_call" | custom-call | tf_op jit(solution)/shard_map/gather/pallas_call | solution.py:506
  56.4 15.7 %level_one.1 = (bf16[1024,3456]{1,0:T(8,128)(2,1)}, f32[1024,128]{1,0:T(8,128)}, bf16[256,1024]{1,0:T(8,128)(2,1)}, f32[8,16,8,256]{3,2,1,0:T(8,128)}, bf16[1024,256]{1,0:T(8,128)(2,1)}) custom-call(s32[2]{0:T(128)} %slice_bitcast_fusion.slots, f32[18,34,8,128]{3,2,1,0:T(8,128)} %get-tuple-element.14.mp, f32[16,32,8,128]{3,2,1,0:T(8,128)} %broadcast_in_dim.31.mask, ...), custom_call_target="tpu_custom_call" | custom-call | tf_op jit(solution)/shard_map/level_one/pallas_call | solution.py:141
  72.1 11.4 %halo.1.dp = f32[10,18,8,256]{3,2,1,0:T(8,128)} custom-call(f32[8,16,8,256]{3,2,1,0:T(8,128)} %get-tuple-element.16.tile), custom_call_target="tpu_custom_call" | custom-call | tf_op jit(solution)/shard_map/halo/pallas_call | solution.py:541
  83.5 33.8 %level_two.1 = (f32[8,16,8,256]{3,2,1,0:T(8,128)}, bf16[128,32,384]{2,1,0:T(8,128)(2,1)}) custom-call(s32[2]{0:T(128)} %slice_bitcast_fusion.slots, f32[10,18,8,256]{3,2,1,0:T(8,128)} %halo.1.dp, f32[10,18,8,256]{3,2,1,0:T(8,128)} %get-tuple-element.17.gp, f32[16,32,8,128]{3,2,1,0:T(8,128)} %broadcast_in_dim.31.mask, f32[8,16,8,256]{3,2,1,0:T(8,128)} %broadcast_in_dim.34.cm, ...), custom_call_target="tpu_custom_call" | custom-call | tf_op jit(solution)/shard_map/level_two/pallas_call | solution.py:308
  117.3 2.0 %fusion = bf16[1,8,16,4,192]{4,3,2,1,0:T(4,128)(2,1)} fusion(f32[8,16,8,256]{3,2,1,0:T(8,128)} %get-tuple-element.22), kind=kLoop, calls=%fused_computation.4 | loop fusion | bytes 393216 | tf_op jit(solution)/shard_map/convert_element_type | solution.py:696
  119.3 43.7 %scatter.1 = f32[32,384]{1,0:T(8,128)} custom-call(bf16[8,2,4,2,32,384]{5,4,3,2,1,0:T(8,128)(2,1)} %bitcast.24), custom_call_target="tpu_custom_call" | custom-call | tf_op jit(solution)/shard_map/scatter/pallas_call | solution.py:648
  163.0 0.7 slice.23
  163.7 0.7 reshape.62
  164.4 1.4 slice.22
  165.8 1.4 copy.33
  (5 shorter events, 0.0 us)
Async XLA Ops:
  5.9 4.2 %copy-start.1 = (bf16[1,8,16,4,192]{4,3,2,1,0:T(4,128)(2,1)S(1)}, bf16[1,8,16,4,192]{4,3,2,1,0:T(4,128)(2,1)}, u32[]{:S(2)}) copy-start(bf16[1,8,16,4,192]{4,3,2,1,0:T(4,128)(2,1)} %param.15) | copy-start | bytes 589828
  10.1 3.1 %copy-start = (bf16[1,16,32,8,96]{4,3,2,1,0:T(8,128)(2,1)S(1)}, bf16[1,16,32,8,96]{4,3,2,1,0:T(8,128)(2,1)}, u32[]{:S(2)}) copy-start(bf16[1,16,32,8,96]{4,3,2,1,0:T(8,128)(2,1)} %param.8) | copy-start | bytes 2359300

commit v2 on v0

v2 whole, which is shorter than its diff:
```python
import jax
import jax.numpy as jnp
from jax import lax
from jax.experimental import pallas as pl
from jax.experimental.pallas import tpu as pltpu
from jax.sharding import PartitionSpec as P

C1 = 96
C2 = 192
GX = 2
GY = 4
CAP = 2
GROUPS = 32
N_TX = 8
N_TY = 16
PITCH_W = 33
PITCH_R = 264
PITCH_S = 136
MESH = pl.DeviceIdType.MESH
f32 = jnp.float32
bf16 = jnp.bfloat16
TAPS = [(ox, oy, oz) for ox in range(3) for oy in range(3) for oz in range(3)]
VMEM_LIMIT = 60 * 1024 * 1024


def lane_tiles(rows):
    return [rows[:, i * 128 : (i + 1) * 128] for i in range(rows.shape[1] // 128)]


def relane(count, segments):
    lanes = lax.broadcasted_iota(jnp.int32, segments[0][0][0].shape, 1)
    out = [None] * count
    rolled = {}
    for tiles, src, dst, length in segments:
        while length > 0:
            step = min(length, 128 - src % 128, 128 - dst % 128)
            tile, shift = tiles[src // 128], (dst - src) % 128
            key = (id(tile), shift)
            if key not in rolled:
                rolled[key] = pltpu.roll(tile, shift, 1) if shift else tile
            low, high, target = dst % 128, dst % 128 + step, dst // 128
            base = jnp.zeros_like(tile) if out[target] is None else out[target]
            if step == 128:
                out[target] = rolled[key]
            else:
                inside = lanes < high
                if low:
                    inside = inside & (lanes >= low)
                out[target] = jnp.where(inside, rolled[key], base)
            src, dst, length = src + step, dst + step, length - step
    return [jnp.zeros_like(segments[0][0][0]) if t is None else t for t in out]


PIECES_ONE = [[(0, 0, 0, 72), (1, 0, 72, 24)], [(1, 24, 0, 48), (2, 0, 48, 48)], [(2, 48, 0, 24), (3, 0, 24, 72)]]
PIECES_TWO = [
    [(0, 0, 0, 192)],
    [(0, 192, 0, 96), (1, 0, 96, 96)],
    [(1, 96, 0, 192)],
    [(2, 0, 0, 192)],
    [(2, 192, 0, 96), (3, 0, 96, 96)],
    [(3, 96, 0, 192)],
]
BASE_DOWN = 72


def to_row(shards, pieces, base, count):
    return relane(count, [(shards[s], base + a, b, n) for s, a, b, n in pieces])


def join(tiles):
    return tiles[0] if len(tiles) == 1 else jnp.concatenate(tiles, axis=1)


def depth_shifts(slab):
    axis = slab.ndim - 2
    depth = lax.broadcasted_iota(jnp.int32, slab.shape, axis)
    below = jnp.where(depth == 0, 0.0, pltpu.roll(slab, 1, axis))
    above = jnp.where(depth == 7, 0.0, pltpu.roll(slab, 7, axis))
    return below, slab, above


FIRST, SECOND, WHOLE = pl.ds(0, 16), pl.ds(16, 16), pl.ds(0, 32)


def barrier_with(peers):
    barrier = pltpu.get_barrier_semaphore()
    for peer in peers:
        pl.semaphore_signal(barrier, inc=1, device_id=peer, device_id_type=MESH)
    pl.semaphore_wait(barrier, len(peers))


def place():
    grp, tx, ty = lax.axis_index("grp"), lax.axis_index("tx"), lax.axis_index("ty")
    return grp, tx, ty, ty // 8, (ty // 2) % 4, ty % 2


def other(value, bits):
    if bits == 1:
        return value + 1 - 2 * (value % 2)
    if bits == 2:
        return (value + 2) % 4
    return 3 - value


def ring_peers(grp, tx, ty):
    return [(grp, (tx + d) % N_TX, ty) for d in range(1, N_TX)]


def cube_peers(grp, tx, hi, y, core):
    def ty_of(h, v, c):
        return h * 8 + v * 2 + c

    return {
        "core": (grp, tx, ty_of(hi, y, 1 - core)),
        "y1": (grp, tx, ty_of(hi, other(y, 1), core)),
        "y3": (grp, tx, ty_of(hi, other(y, 3), core)),
        "x": (1 - grp, tx, ty_of(1 - hi, y, core)),
        "grp": (1 - grp, tx, ty_of(hi, y, core)),
    }


STEPS = [(dx, dy) for dx in (-1, 0, 1) for dy in (-1, 0, 1) if dx or dy]


def halo_peers(grp, tx, ty):
    return [(grp, (tx + dx + N_TX) % N_TX, (ty + dy + N_TY) % N_TY) for dx, dy in STEPS]


def edge_out(step, size, shift):
    return pl.ds(shift, 1) if step < 0 else pl.ds(size - 1 + shift, 1) if step > 0 else pl.ds(shift, size)


def edge_in(step, size):
    return pl.ds(size + 1, 1) if step < 0 else pl.ds(0, 1) if step > 0 else pl.ds(1, size)


def clear_edges(dst, tx, ty):
    size_x, size_y = dst.shape[0], dst.shape[1]

    @pl.when(tx == 0)
    def _():
        dst[0:1] = jnp.zeros((1,) + dst.shape[1:], dst.dtype)

    @pl.when(tx == N_TX - 1)
    def _():
        dst[size_x - 1 : size_x] = jnp.zeros((1,) + dst.shape[1:], dst.dtype)

    @pl.when(ty == 0)
    def _():
        dst[:, 0:1] = jnp.zeros((size_x, 1) + dst.shape[2:], dst.dtype)

    @pl.when(ty == N_TY - 1)
    def _():
        dst[:, size_y - 1 : size_y] = jnp.zeros((size_x, 1) + dst.shape[2:], dst.dtype)


class Links:
    def __init__(self, send, recv):
        self.send, self.recv, self.sent = send, recv, []

    def start(self, src, dst, peer):
        k = len(self.sent)
        copy = pltpu.make_async_remote_copy(
            src_ref=src,
            dst_ref=dst,
            send_sem=self.send.at[k],
            recv_sem=self.recv.at[k],
            device_id=peer,
            device_id_type=MESH,
        )
        copy.start()
        self.sent.append(copy)
        return copy

    def halo(self, src, dst, peers, inside):
        size_x, size_y = dst.shape[0] - 2, dst.shape[1] - 2
        shift = 1 if inside else 0
        copies = []
        for peer, (dx, dy) in zip(peers, STEPS):
            copies.append(
                self.start(
                    src.at[edge_out(dx, size_x, shift), edge_out(dy, size_y, shift)],
                    dst.at[edge_in(dx, size_x), edge_in(dy, size_y)],
                    peer,
                )
            )
        return copies


class Gather:
    def __init__(self, links, where, shard, full, own):
        self.links, self.where, self.full = links, where, full
        grp, tx, ty, hi, y, core = where
        self.cube = cube_peers(grp, tx, hi, y, core)
        mine = full.at[tx, hi, y, core]
        self.line = [links.start(shard, mine, peer) for peer in ring_peers(grp, tx, ty)]
        self.own = pltpu.make_async_copy(shard, mine, own)
        self.own.start()
        self.partner = []

    def part(self, v, rows):
        return self.full.at[:, :, v, self.where[5], rows]

    def to_core(self, ref):
        self.partner.append(self.links.start(ref, ref, self.cube["core"]))

    def across(self):
        grp, tx, ty, hi, y, core = self.where
        self.own.wait()
        for copy in self.line:
            copy.wait_recv()
        column = self.full.at[:, hi, y, core]
        self.step = [self.links.start(column, column, self.cube["x"])]
        self.to_core(column)

    def near(self):
        grp, tx, ty, hi, y, core = self.where
        for copy in self.step:
            copy.wait_recv()
        first, second = self.part(y, FIRST), self.part(y, SECOND)
        self.step = [
            self.links.start(first, first, self.cube["y1"]),
            self.links.start(second, second, self.cube["y3"]),
        ]
        self.to_core(self.full.at[:, 1 - hi, y, core])

    def far(self):
        y = self.where[4]
        y1, y3 = other(y, 1), other(y, 3)
        for copy in self.step:
            copy.wait_recv()
        self.step = []
        for v, rows, name in ((y, FIRST, "y3"), (y1, FIRST, "y3"), (y, SECOND, "y1"), (y3, SECOND, "y1")):
            self.step.append(self.links.start(self.part(v, rows), self.part(v, rows), self.cube[name]))
        self.to_core(self.part(y1, FIRST))
        self.to_core(self.part(y3, SECOND))

    def last(self):
        y = self.where[4]
        y1, y2, y3 = other(y, 1), other(y, 2), other(y, 3)
        arrived = [(y3, FIRST), (y2, FIRST), (y1, SECOND), (y2, SECOND)]
        for copy, (v, rows) in zip(self.step, arrived):
            copy.wait_recv()
            self.to_core(self.part(v, rows))

    def done(self):
        for copy in self.partner:
            copy.wait_recv()


class Scatter:
    def __init__(self, links, where, packed, total, sums, rd, ry2, ry1, rx, rz, half, rg):
        self.links, self.where, self.packed, self.total = links, where, packed, total
        self.sums, self.rd, self.ry2, self.ry1 = sums, rd, ry2, ry1
        self.rx, self.rz, self.half, self.rg = rx, rz, half, rg
        grp, tx, ty, hi, y, core = where
        self.cube = cube_peers(grp, tx, hi, y, core)
        self.line = ring_peers(grp, tx, ty)
        self.ys = [other(y, 2), other(y, 3), other(y, 1), y]

    def add(self, z, h, v, rows, left, right):
        both = left[...].astype(f32) + right[...].astype(f32)
        self.sums[z, h, v, rows, :] = both.astype(bf16)

    def part(self, v, rows):
        return self.sums.at[:, :, v, rows]

    def wait(self):
        for copy in self.step:
            copy.wait_recv()

    def cores(self):
        core = self.where[5]
        self.step = [
            self.links.start(self.packed.at[:, :, v, 1 - core], self.rd.at[:, :, v], self.cube["core"])
            for v in self.ys
        ]

    def far(self):
        core = self.where[5]
        y2, y3, y1, y = self.ys
        for copy, v in zip(self.step, self.ys):
            copy.wait_recv()

            def take(z, carry):
                for h in range(2):
                    self.add(z, h, v, WHOLE, self.packed.at[z, h, v, core], self.rd.at[z, h, v])
                return carry

            lax.fori_loop(0, 8, take, 0)
        self.step = [
            self.links.start(self.part(y3, FIRST), self.ry2.at[0, :, :, FIRST], self.cube["y3"]),
            self.links.start(self.part(y2, FIRST), self.ry2.at[1, :, :, FIRST], self.cube["y3"]),
            self.links.start(self.part(y1, SECOND), self.ry2.at[0, :, :, SECOND], self.cube["y1"]),
            self.links.start(self.part(y2, SECOND), self.ry2.at[1, :, :, SECOND], self.cube["y1"]),
        ]

    def near(self):
        y2, y3, y1, y = self.ys
        self.wait()

        def take(z, carry):
            for h in range(2):
                self.add(z, h, y, WHOLE, self.sums.at[z, h, y], self.ry2.at[0, z, h])
                self.add(z, h, y1, FIRST, self.sums.at[z, h, y1, FIRST], self.ry2.at[1, z, h, FIRST])
                self.add(z, h, y3, SECOND, self.sums.at[z, h, y3, SECOND], self.ry2.at[1, z, h, SECOND])
            return carry

        lax.fori_loop(0, 8, take, 0)
        self.step = [
            self.links.start(self.part(y1, FIRST), self.ry1.at[:, :, FIRST], self.cube["y1"]),
            self.links.start(self.part(y3, SECOND), self.ry1.at[:, :, SECOND], self.cube["y3"]),
        ]

    def across(self):
        hi, y = self.where[3], self.where[4]
        self.wait()

        def take(z, carry):
            for h in range(2):
                self.add(z, h, y, WHOLE, self.sums.at[z, h, y], self.ry1.at[z, h])
            return carry

        lax.fori_loop(0, 8, take, 0)
        self.step = [self.links.start(self.sums.at[:, 1 - hi, y], self.rx, self.cube["x"])]

    def along(self):
        tx, hi, y = self.where[1], self.where[3], self.where[4]
        self.wait()

        def take(z, carry):
            self.add(z, hi, y, WHOLE, self.sums.at[z, hi, y], self.rx.at[z])
            return carry

        lax.fori_loop(0, 8, take, 0)
        self.step = [
            self.links.start(self.sums.at[(tx + d + 1) % N_TX, hi, y], self.rz.at[d], peer)
            for d, peer in enumerate(self.line)
        ]

    def swap(self):
        tx, hi, y = self.where[1], self.where[3], self.where[4]
        self.wait()
        value = self.sums[tx, hi, y].astype(f32)
        for d in range(N_TX - 1):
            value = value + self.rz[d].astype(f32)
        self.half[...] = value
        self.step = [self.links.start(self.half, self.rg, self.cube["grp"])]

    def done(self):
        self.wait()
        self.total[...] = self.half[...] + self.rg[...]


def choose(slots, place, blocks):
    value = None
    for i, block in enumerate(blocks):
        term = jnp.where(slots[i] == place, block, 0.0)
        value = term if value is None else value + term
    return value


def corner(slots, i):
    return slots[i] // GY, slots[i] % GY


def unpack_first(full, w9, wd, w1g, wdg, tmp):
    def unpack(a, carry):
        shards = []
        for b in range(4):
            value = full[a // 4, (a // 2) % 2, (a % 2) * 2 + b // 2, b % 2].astype(f32)
            tmp[b] = value
            shards.append([value])
        for k in range(3):
            w1g[pl.ds((a * 3 + k) * PITCH_W, 32), :] = to_row(shards, PIECES_ONE[k], 0, 1)[0]
        chunks = [[tmp[b, pl.ds(j, 8, stride=3), :]] for b in range(4) for j in range(3)]
        for k in range(3):
            segments = [(chunks[4 * k + n], BASE_DOWN, 48 * n, 48) for n in range(4)]
            for c, tile in enumerate(relane(2, segments)):
                wdg[c, pl.ds(pl.multiple_of((a * 3 + k) * 8, 8), 8), :] = tile
        return carry

    lax.fori_loop(0, GROUPS, unpack, 0)
    for t in range(27):
        k, oz = t // 3, t % 3
        w9[k * 128 : k * 128 + C1, oz * 128 : (oz + 1) * 128] = w1g[pl.ds(t, C1, stride=PITCH_W), :].astype(bf16)
    for k in range(9):
        w9[k * 128 + C1 : (k + 1) * 128, :] = jnp.zeros((128 - C1, 384), bf16)
    for t in range(8):
        for c in range(2):
            wd[t * 128 : t * 128 + C1, c * 128 : (c + 1) * 128] = wdg[c, pl.ds(t, C1, stride=8), :].astype(bf16)
        wd[t * 128 + C1 : (t + 1) * 128, :] = jnp.zeros((128 - C1, 256), bf16)


def unpack_second(full, w2, big):
    def unpack(a, carry):
        shards = [
            lane_tiles(full[a // 4, (a // 2) % 2, (a % 2) * 2 + b // 2, b % 2].astype(f32)) for b in range(4)
        ]
        for k in range(6):
            for c, tile in enumerate(to_row(shards, PIECES_TWO[k], 0, 2)):
                big[c, pl.ds((a * 6 + k) * PITCH_W, 32), :] = tile
        return carry

    lax.fori_loop(0, GROUPS, unpack, 0)

    def order(k, carry):
        for oz in range(3):
            for c in range(2):
                w2[pl.ds(pl.multiple_of(k * 256, 256), C2), oz * 256 + c * 128 : oz * 256 + (c + 1) * 128] = big[
                    c, pl.ds(k * 3 + oz, C2, stride=PITCH_W), :
                ].astype(bf16)
        w2[pl.ds(pl.multiple_of(k * 256 + C2, 64), 256 - C2), :] = jnp.zeros((256 - C2, 768), bf16)
        return carry

    lax.fori_loop(0, 9, order, 0)


def windows(dst, i, window, edge, flip):
    lanes = window.shape[-1]
    rows = edge * edge * 8
    for k in range(9):
        ox, oy = k // 3, k % 3
        if flip:
            ox, oy = 2 - ox, 2 - oy
        piece = window[ox : ox + edge, oy : oy + edge].reshape(rows, lanes)
        dst[i * rows : (i + 1) * rows, k * lanes : (k + 1) * lanes] = piece.astype(bf16)


def three(rows, lanes):
    return [rows[:, n * lanes : (n + 1) * lanes].reshape(-1, 8, lanes) for n in range(3)]


def conv(parts):
    low, mid, high = parts
    return (depth_shifts(low)[0] + mid + depth_shifts(high)[2]).reshape(-1, mid.shape[-1])


def spread(value):
    below, mid, above = depth_shifts(value.reshape(-1, 8, value.shape[-1]))
    return jnp.concatenate([v.reshape(value.shape).astype(bf16) for v in (above, mid, below)], axis=1)


def pack_first(packed, r1, rdn, tmp):
    tmp[...] = jnp.zeros_like(tmp)

    def pack(a, carry):
        segments = [[] for _ in range(4)]
        downs = []
        for k in range(3):
            ci = a * 3 + k
            tiles = [r1[pl.ds(ci, 32, stride=PITCH_S), :]]
            for s, at, lane, n in PIECES_ONE[k]:
                segments[s].append((tiles, lane, at, n))
            downs.append([rdn[c, pl.ds(ci, 8, stride=PITCH_S), :] for c in range(2)])
        for b in range(4):
            for j in range(3):
                m = 3 * b + j
                tmp[b, pl.ds(j, 8, stride=3), :] = relane(1, [(downs[m // 4], m % 4 * 48, BASE_DOWN, 48)])[0]
            value = relane(1, segments[b])[0] + tmp[b]
            packed[a // 4, (a // 2) % 2, (a % 2) * 2 + b // 2, b % 2] = value.astype(bf16)
        return carry

    lax.fori_loop(0, GROUPS, pack, 0)


def pack_second(packed, big):
    def pack(a, carry):
        segments = [[] for _ in range(4)]
        for k in range(6):
            tiles = [big[c, pl.ds(a * 6 + k, 32, stride=PITCH_R), :] for c in range(2)]
            for s, at, lane, n in PIECES_TWO[k]:
                segments[s].append((tiles, lane, at, n))
        for b in range(4):
            packed[a // 4, (a // 2) % 2, (a % 2) * 2 + b // 2, b % 2] = join(relane(3, segments[b])).astype(bf16)
        return carry

    lax.fori_loop(0, GROUPS, pack, 0)


def whole_kernel(
    slots, tile, grad, mask, coarse, shard_a, shard_b, out, total_a, total_b,
    full_a, full_b, mp, gp, dp, x9, x2, x3, w9, wd, w2, w1g, wdg, tmp, big, act, pm, hs, gs, r1, rdn,
    packed_a, packed_b, sums_a, rd_a, ry2_a, ry1_a, rx_a, rz_a, half_a, rg_a,
    sums_b, rd_b, ry2_b, ry1_b, rx_b, rz_b, half_b, rg_b, send, recv, own,
):
    where = place()
    grp, tx, ty, hi, y, core = where
    cube = cube_peers(grp, tx, hi, y, core)
    around = halo_peers(grp, tx, ty)
    links = Links(send, recv)
    barrier_with(ring_peers(grp, tx, ty) + [cube[n] for n in ("core", "y1", "y3", "x", "grp")] + around)

    first = Gather(links, where, shard_a, full_a, own.at[0])
    halo_m = links.halo(tile, mp, around, False)
    inner_m = pltpu.make_async_copy(tile, mp.at[pl.ds(1, 16), pl.ds(1, 32)], own.at[2])
    inner_m.start()
    second = Gather(links, where, shard_b, full_b, own.at[1])
    halo_g = links.halo(grad, gp, around, False)
    inner_g = pltpu.make_async_copy(grad, gp.at[pl.ds(1, 8), pl.ds(1, 16)], own.at[3])
    inner_g.start()

    first.across()
    inner_m.wait()
    for copy in halo_m:
        copy.wait_recv()
    clear_edges(mp, tx, ty)
    for i in range(CAP):
        px, py = corner(slots, i)
        windows(x9, i, mp[pl.ds(px * 8, 10), pl.ds(py * 8, 10)], 8, False)
    first.near()
    second.across()
    first.far()
    second.near()
    first.last()
    second.far()
    first.done()
    unpack_first(full_a, w9, wd, w1g, wdg, tmp)
    second.last()

    hs[...] = jnp.zeros_like(hs)
    downs = []
    for i in range(CAP):
        px, py = corner(slots, i)
        value = conv(three(jnp.dot(x9[i * 512 : (i + 1) * 512, :], w9[...], preferred_element_type=f32), 128))
        act[i * 512 : (i + 1) * 512, :] = value
        live = mask[pl.ds(px * 8, 8), pl.ds(py * 8, 8)].reshape(512, 128)
        hidden = (live * jax.nn.silu(value)).astype(bf16).astype(f32).reshape(4, 2, 4, 2, 8, 128)
        for p in range(2):
            for q in range(2):
                for b in range(4):
                    hs[:, p * 2 + q, b * 16 : b * 16 + 8, :] = hidden[:, p, b, q]
        for t in range(8):
            patch = hs[:, t // 2, pl.ds(t % 2, 32, stride=2), :].reshape(128, 128)
            pm[i * 128 : (i + 1) * 128, t * 128 : (t + 1) * 128] = patch.astype(bf16)
        raw = jnp.dot(pm[i * 128 : (i + 1) * 128, :], wd[...], preferred_element_type=f32)
        edge = coarse[pl.ds(px * 4, 4), pl.ds(py * 4, 4)]
        downs.append((edge * raw.reshape(4, 4, 8, 256)).astype(bf16).astype(f32))
    for p in range(GX * GY):
        px, py = p // GY, p % GY
        dp[1 + px * 4 : 5 + px * 4, 1 + py * 4 : 5 + py * 4] = choose(slots, p, downs)
    halo_d = links.halo(dp, dp, around, True)

    inner_g.wait()
    for copy in halo_g:
        copy.wait_recv()
    clear_edges(gp, tx, ty)
    grads, edges = [], []
    for i in range(CAP):
        px, py = corner(slots, i)
        windows(x3, i, gp[pl.ds(px * 4, 6), pl.ds(py * 4, 6)], 4, True)
        grads.append(gp[pl.ds(px * 4 + 1, 4), pl.ds(py * 4 + 1, 4)].reshape(128, 256))
        edges.append(coarse[pl.ds(px * 4, 4), pl.ds(py * 4, 4)].reshape(128, 256))
    grad_two = jnp.concatenate(grads, axis=0)
    edge = jnp.concatenate(edges, axis=0)
    spread_two = spread(grad_two)
    big[:, 27 * PITCH_R : 32 * PITCH_R, :] = jnp.zeros((2, 5 * PITCH_R, 128), f32)
    for copy in halo_d:
        copy.wait_recv()
    clear_edges(dp, tx, ty)
    for i in range(CAP):
        px, py = corner(slots, i)
        windows(x2, i, dp[pl.ds(px * 4, 6), pl.ds(py * 4, 6)], 4, False)
    for k in range(9):
        product = lax.dot_general(
            x2[:, k * 256 : (k + 1) * 256], spread_two, (((0,), (0,)), ((), ())), preferred_element_type=f32
        )
        for oz in range(3):
            for c in range(2):
                at = oz * 256 + c * 128
                big[c, (3 * k + oz) * PITCH_R : (3 * k + oz) * PITCH_R + 256, :] = product[:, at : at + 128]
    pack_second(packed_b, big)
    sum_b = Scatter(
        links, where, packed_b, total_b, sums_b, rd_b, ry2_b, ry1_b, rx_b, rz_b, half_b, rg_b
    )
    sum_b.cores()

    second.done()
    unpack_second(full_b, w2, big)
    sum_b.far()
    parts = []
    for oz in range(3):
        part = None
        for k in range(9):
            term = lax.dot_general(
                x3[:, k * 256 : (k + 1) * 256],
                w2[k * 256 : (k + 1) * 256, oz * 256 : (oz + 1) * 256],
                (((1,), (1,)), ((), ())),
                preferred_element_type=f32,
            )
            part = term if part is None else part + term
        parts.append(part.reshape(-1, 8, 256))
    back = conv(parts[::-1])
    grad_in = (grad_two + edge * back).astype(bf16)
    sum_b.near()

    rdn[...] = jnp.zeros_like(rdn)
    for t in range(8):
        product = lax.dot_general(
            pm[:, t * 128 : (t + 1) * 128], grad_in, (((0,), (0,)), ((), ())), preferred_element_type=f32
        )
        for c in range(2):
            rdn[c, t * PITCH_S : t * PITCH_S + 128, :] = product[:, c * 128 : (c + 1) * 128]
    spreads = []
    for i in range(CAP):
        px, py = corner(slots, i)
        for t in range(8):
            part = lax.dot_general(
                grad_in[i * 128 : (i + 1) * 128],
                wd[t * 128 : (t + 1) * 128, :],
                (((1,), (1,)), ((), ())),
                preferred_element_type=f32,
            )
            gs[:, t // 2, pl.ds(t % 2, 32, stride=2), :] = part.reshape(4, 32, 128)
        rows = []
        for p in range(2):
            for b in range(4):
                for q in range(2):
                    rows.append(gs[:, p * 2 + q, b * 16 : b * 16 + 8, :])
        hidden = jnp.stack(rows, axis=1).reshape(512, 128)
        live = mask[pl.ds(px * 8, 8), pl.ds(py * 8, 8)].reshape(512, 128)
        value = act[i * 512 : (i + 1) * 512, :]
        sig = jax.nn.sigmoid(value)
        spreads.append(spread(live * hidden * (sig * (1.0 + value * (1.0 - sig)))))
    spread_one = jnp.concatenate(spreads, axis=0)
    sum_b.across()
    r1[27 * PITCH_S : 32 * PITCH_S, :] = jnp.zeros((5 * PITCH_S, 128), f32)
    for k in range(9):
        product = lax.dot_general(
            x9[:, k * 128 : (k + 1) * 128], spread_one, (((0,), (0,)), ((), ())), preferred_element_type=f32
        )
        for oz in range(3):
            at = (3 * k + oz) * PITCH_S
            r1[at : at + 128, :] = product[:, oz * 128 : (oz + 1) * 128]
    pack_first(packed_a, r1, rdn, tmp)
    sum_a = Scatter(
        links, where, packed_a, total_a, sums_a, rd_a, ry2_a, ry1_a, rx_a, rz_a, half_a, rg_a
    )
    sum_a.cores()
    sum_b.along()

    value = conv(three(jnp.dot(x2[...], w2[...], preferred_element_type=f32), 256))
    blocks = []
    for i in range(CAP):
        px, py = corner(slots, i)
        down = dp[pl.ds(px * 4 + 1, 4), pl.ds(py * 4 + 1, 4)].reshape(128, 256)
        rows = slice(i * 128, (i + 1) * 128)
        blocks.append((edges[i] * (down + value[rows])).reshape(4, 4, 8, 256))
    sum_a.far()
    for p in range(GX * GY):
        px, py = p // GY, p % GY
        out[px * 4 : px * 4 + 4, py * 4 : py * 4 + 4] = choose(slots, p, blocks)
    sum_a.near()
    sum_b.swap()
    sum_a.across()
    sum_a.along()
    sum_b.done()
    sum_a.swap()
    sum_a.done()
    for copy in links.sent:
        copy.wait_send()


def whole(slots, tile, grad, mask, coarse, shard_a, shard_b):
    def sums(lanes):
        return [
            pltpu.VMEM((8, 2, 4, 32, lanes), bf16),
            pltpu.VMEM((8, 2, 4, 32, lanes), bf16),
            pltpu.VMEM((2, 8, 2, 32, lanes), bf16),
            pltpu.VMEM((8, 2, 32, lanes), bf16),
            pltpu.VMEM((8, 32, lanes), bf16),
            pltpu.VMEM((7, 32, lanes), bf16),
            pltpu.VMEM((32, lanes), f32),
            pltpu.VMEM((32, lanes), f32),
        ]

    copies = 2 * 23 + 24 + 2 * 19
    return pl.pallas_call(
        whole_kernel,
        in_specs=[pl.BlockSpec(memory_space=pltpu.SMEM)] + [pl.BlockSpec(memory_space=pltpu.VMEM)] * 6,
        out_specs=[pl.BlockSpec(memory_space=pltpu.VMEM)] * 3,
        out_shape=[
            jax.ShapeDtypeStruct((8, 16, 8, 256), f32),
            jax.ShapeDtypeStruct((32, 128), f32),
            jax.ShapeDtypeStruct((32, 384), f32),
        ],
        scratch_shapes=[
            pltpu.VMEM((8, 2, 4, 2, 32, 128), bf16),
            pltpu.VMEM((8, 2, 4, 2, 32, 384), bf16),
            pltpu.VMEM((18, 34, 8, 128), f32),
            pltpu.VMEM((10, 18, 8, 256), f32),
            pltpu.VMEM((10, 18, 8, 256), f32),
            pltpu.VMEM((1024, 9 * 128), bf16),
            pltpu.VMEM((256, 9 * 256), bf16),
            pltpu.VMEM((256, 9 * 256), bf16),
            pltpu.VMEM((9 * 128, 384), bf16),
            pltpu.VMEM((1024, 256), bf16),
            pltpu.VMEM((9 * 256, 768), bf16),
            pltpu.VMEM((C1 * PITCH_W + 8, 128), f32),
            pltpu.VMEM((2, C1 * 8, 128), f32),
            pltpu.VMEM((4, 32, 128), f32),
            pltpu.VMEM((2, 32 * PITCH_R, 128), f32),
            pltpu.VMEM((1024, 128), f32),
            pltpu.VMEM((256, 1024), bf16),
            pltpu.VMEM((4, 4, 64, 128), f32),
            pltpu.VMEM((4, 4, 64, 128), f32),
            pltpu.VMEM((32 * PITCH_S, 128), f32),
            pltpu.VMEM((2, 8 * PITCH_S, 128), f32),
            pltpu.VMEM((8, 2, 4, 2, 32, 128), bf16),
            pltpu.VMEM((8, 2, 4, 2, 32, 384), bf16),
        ]
        + sums(128)
        + sums(384)
        + [
            pltpu.SemaphoreType.DMA((copies,)),
            pltpu.SemaphoreType.DMA((copies,)),
            pltpu.SemaphoreType.DMA((4,)),
        ],
        compiler_params=pltpu.CompilerParams(collective_id=0, has_side_effects=True, vmem_limit_bytes=VMEM_LIMIT),
        name="whole",
    )(slots, tile, grad, mask, coarse, shard_a, shard_b)


def live_flags(order, count, bricks):
    places = jnp.arange(bricks, dtype=jnp.int32)
    ranks = jnp.arange(order.shape[0], dtype=jnp.int32)
    match = (order[:, None] == places[None, :]) & (ranks[:, None] < count)
    return jnp.any(match, axis=0).astype(f32)


def local(features, voxel_mask, brick_order, brick_count, w_conv1, w_down, w_conv2, cotangent):
    order = brick_order[0]
    slots = order[:CAP]
    shard_a = jnp.pad(w_conv1, ((0, 5), (0, 56))) + jnp.pad(w_down.reshape(24, 48), ((0, 8), (72, 8)))
    shard_b = jnp.pad(w_conv2, ((0, 5), (0, 96)))
    live = live_flags(order, brick_count[0], GX * GY).reshape(GX, GY)
    live_map = jnp.repeat(jnp.repeat(live, 8, axis=0), 8, axis=1)
    live_mask = voxel_mask[0].astype(f32) * live_map[..., None]
    mask = jnp.broadcast_to(live_mask[..., None], (16, 32, 8, 128))
    masked = jnp.pad(features[0].astype(f32), ((0, 0), (0, 0), (0, 0), (0, 32))) * mask
    coarse = live_mask.reshape(8, 2, 16, 2, 4, 2).max(axis=(1, 3, 5))
    coarse = jnp.broadcast_to(jnp.pad(coarse, ((0, 0), (0, 0), (0, 4)))[..., None], (8, 16, 8, 256))
    grad_two = jnp.pad(cotangent[0].astype(f32), ((0, 0), (0, 0), (0, 4), (0, 64))) * coarse
    out, total_a, total_b = whole(slots, masked, grad_two, mask, coarse, shard_a, shard_b)
    one = total_a[:27, :72]
    low = total_a[:24, 72:120].reshape(8, 144)
    two = total_b[:27, :288]
    return out[None, :, :, :4, :C2].astype(bf16), one, low, two


def solution(mesh):
    return jax.shard_map(
        local,
        mesh=mesh,
        in_specs=(
            P("grp", "tx", "ty", None, None),
            P("grp", "tx", "ty", None),
            P(("grp", "tx", "ty"), None),
            P(("grp", "tx", "ty")),
            P(None, ("tx", "ty")),
            P(None, ("tx", "ty")),
            P(None, ("tx", "ty")),
            P("grp", "tx", "ty", None, None),
        ),
        out_specs=(
            P("grp", "tx", "ty", None, None),
            P(None, ("tx", "ty")),
            P(None, ("tx", "ty")),
            P(None, ("tx", "ty")),
        ),
        check_vma=False,
    )
```

time: 968 us -> 134 us (0.14)
  blocking collectives: 364 us -> 0 us
  waiting for transfers between devices: 276 us -> 0 us
  local copies, waits for them, and re-layouts: 185 us -> 14.1 us
  Pallas kernels: 0 us -> 110 us
  matrix products: 70.1 us -> 0 us
  starting transfers between devices: 33 us -> 0 us
  between operations: 19.1 us -> 1.4 us
    all_gather x2 -> x0, blocking collectives: 364 us -> none  [the longest x1 183 us: local(): lax.all_gather(w_down, ('tx', 'ty'), axis=1, tiled=True)]
    psum x1 -> x0, waiting for transfers between devices: 276 us -> none  [local(): lax.psum((flat_one, flat_down, flat_two), ('grp', 'tx', 'ty'))]
    pallas_call x0 -> x1, Pallas kernels: none -> 110 us  [whole(): pl.pallas_call(whole_kernel, in_specs=[pl.BlockSpec(memory_space=pltpu.SM...]
    dot_general x138 -> x0, matrix products: 70.1 us -> none  [the longest x54 42.6 us: tap_grads(): lax.dot_general(piece, flat_grads, (((0,), (0,)), ((), ())), preferred_el...]
    another operation x58 -> x0, local copies, waits for them, and re-layouts: 50.7 us -> none  [the longest x56 50.4 us: tap_grads(): return jnp.stack(terms)]
    reshape x60 -> x2, local copies, waits for them, and re-layouts: 41.5 us -> 1.44 us  [the longest x1 0.77 us: local(): w_down.reshape(24, 48)]
    ppermute x12 -> x0, starting transfers between devices: 32.9 us -> none  [the longest x6 20.3 us: extended(): lax.ppermute(lax.slice_in_dim(block, block.shape[dim] - width, None, axis...]
    squeeze x54 -> x0, local copies, waits for them, and re-layouts: 29.6 us -> none  [conv_taps(): term = jnp.dot(piece, weight[index], preferred_element_type=jnp.float32)]
  transfers between devices with their start and end apart: 14 -> 0, of which waited for: 1 -> 0; matrix products, arithmetic and copies ran while one was open for 9% -> 0% of each run, Pallas kernels for 0% -> 0%
where the time goes in v2:
time: 134 us; the launch traced here: 132 us
  Pallas kernels  110 us (82%)
  local copies, waits for them, and re-layouts  14.1 us (11%)
  other arithmetic  6.98 us (5%)
  between operations  1.4 us (1%)
    pallas_call x1, Pallas kernels, whole(): pl.pallas_call(whole_kernel, in_specs=[pl.BlockSpec(memory_space=pltpu.SM...  110 us
    unnamed x7, local copies, waits for them, and re-layouts  2.88 us

profile of v2, /device:TPU:8, one launch (start us, length us, event | category | flops | bytes accessed | tf_op | source)
XLA Modules:
  0.0 132.0 jit_solution(13780090786837389214)
XLA Ops:
  0.6 0.0 copy-start.1
  1.3 0.7 fusion.2
  2.1 0.1 reshape.55
  2.2 1.2 slice_bitcast_fusion.slots
  3.3 0.1 copy.25
  3.4 0.1 broadcast_in_dim.12
  3.5 0.1 reshape.52
  3.6 0.8 reshape.53
  4.4 1.4 %pad_add_fusion.shard_a = bf16[32,128]{1,0:T(8,128)(2,1)} fusion(bf16[24,48]{1,0:T(8,128)(2,1)S(1)} %reshape.53, bf16[27,72]{1,0:T(8,128)(2,1)} %param.12), kind=kLoop, calls=%fused_computation.6 | loop fusion | flops 16384 | bytes 14384 | tf_op jit(solution)/shard_map/add | solution.py:734
  5.7 0.1 copy.28
  5.8 0.1 copy.26
  5.9 0.1 broadcast_in_dim.28
  6.0 0.1 broadcast_in_dim.29
  6.1 1.4 %pad.37.shard_b = bf16[32,384]{1,0:T(8,128)(2,1)} pad(bf16[27,288]{1,0:T(8,128)(2,1)} %param.14, bf16[]{:T(256)} %constant.6.clone.1), padding=0_5x0_96 | pad | bytes 40130 | tf_op jit(solution)/shard_map/jit(_pad)/pad | solution.py:735
  7.4 0.8 bitcast_multiply_fusion
  8.3 0.8 convert_element_type.50
  9.1 0.1 copy.27
  9.3 0.6 convert_element_type.55
  9.8 0.0 copy-start
  9.8 0.3 multiply_reduce_fusion
  10.1 0.1 copy.30
  10.2 0.0 copy-done.1
  10.3 1.2 convert_multiply_fusion.1.grad
  11.4 1.2 broadcast_in_dim.30.coarse
  12.7 0.0 copy-done
  12.7 1.7 %convert_multiply_fusion.tile = f32[16,32,8,128]{3,2,1,0:T(8,128)} fusion(f32[16,32,8]{2,1,0:T(8,128)S(1)} %copy.27, bf16[16,32,8,96]{3,2,1,0:T(8,128)(2,1)S(1)} %bitcast.21), kind=kLoop, calls=%fused_computation | loop fusion | flops 1048576 | bytes 2899968 | tf_op jit(solution)/shard_map/mul | solution.py:740
  14.4 1.9 %broadcast_in_dim.27.mask = f32[16,32,8,128]{3,2,1,0:T(8,128)} broadcast(f32[16,32,8]{2,1,0:T(8,128)S(1)} %copy.27), dimensions={0,1,2} | broadcast | bytes 2113536 | tf_op jit(solution)/shard_map/broadcast_in_dim | solution.py:739
  16.3 109.5 %whole.1 = (f32[8,16,8,256]{3,2,1,0:T(8,128)}, f32[32,128]{1,0:T(8,128)}, f32[32,384]{1,0:T(8,128)}) custom-call(s32[2]{0:T(128)} %slice_bitcast_fusion.slots, f32[16,32,8,128]{3,2,1,0:T(8,128)} %convert_multiply_fusion.tile, f32[8,16,8,256]{3,2,1,0:T(8,128)} %convert_multiply_fusion.1.grad, f32[16,32,8,128]{3,2,1,0:T(8,128)} %broadcast_in_dim.27.mask, ...), custom_call_target="tpu_custom_call" | custom-call | tf_op jit(solution)/shard_map/whole/pallas_call | solution.py:678
  125.8 2.0 %fusion = bf16[1,8,16,4,192]{4,3,2,1,0:T(4,128)(2,1)} fusion(f32[8,16,8,256]{3,2,1,0:T(8,128)} %get-tuple-element.7), kind=kLoop, calls=%fused_computation.4 | loop fusion | bytes 393216 | tf_op jit(solution)/shard_map/convert_element_type | solution.py:748
  127.8 0.8 slice.23
  128.6 0.7 reshape.54
  129.3 1.3 %copy.34 = f32[27,72]{1,0:T(8,128)} copy(f32[27,72]{1,0:T(8,128)} %bitcast.23) | data formatting | bytes 15552
  130.6 1.4 %copy.35 = f32[27,288]{1,0:T(8,128)} copy(f32[27,288]{1,0:T(8,128)} %bitcast.24) | data formatting | bytes 62208
  (4 shorter events, 0.0 us)
Async XLA Ops:
  0.6 9.6 %copy-start.1 = (bf16[1,8,16,4,192]{4,3,2,1,0:T(4,128)(2,1)S(1)}, bf16[1,8,16,4,192]{4,3,2,1,0:T(4,128)(2,1)}, u32[]{:S(2)}) copy-start(bf16[1,8,16,4,192]{4,3,2,1,0:T(4,128)(2,1)} %param.15) | copy-start | bytes 589828
  9.8 2.8 %copy-start = (bf16[1,16,32,8,96]{4,3,2,1,0:T(8,128)(2,1)S(1)}, bf16[1,16,32,8,96]{4,3,2,1,0:T(8,128)(2,1)}, u32[]{:S(2)}) copy-start(bf16[1,16,32,8,96]{4,3,2,1,0:T(8,128)(2,1)} %param.8) | copy-start | bytes 2359300

commit v3 on v2

--- a/solution.py
+++ b/solution.py
@@ -79,9 +79,6 @@
     return below, slab, above
 
 
-FIRST, SECOND, WHOLE = pl.ds(0, 16), pl.ds(16, 16), pl.ds(0, 32)
-
-
 def barrier_with(peers):
     barrier = pltpu.get_barrier_semaphore()
     for peer in peers:
@@ -187,9 +184,14 @@
         return copies
 
 
+def halves(rows):
+    return pl.ds(0, rows // 2), pl.ds(rows // 2, rows // 2)
+
+
 class Gather:
     def __init__(self, links, where, shard, full, own):
         self.links, self.where, self.full = links, where, full
+        self.first, self.second = halves(shard.shape[0])
         grp, tx, ty, hi, y, core = where
         self.cube = cube_peers(grp, tx, hi, y, core)
         mine = full.at[tx, hi, y, core]
@@ -217,7 +219,7 @@
         grp, tx, ty, hi, y, core = self.where
         for copy in self.step:
             copy.wait_recv()
-        first, second = self.part(y, FIRST), self.part(y, SECOND)
+        first, second = self.part(y, self.first), self.part(y, self.second)
         self.step = [
             self.links.start(first, first, self.cube["y1"]),
             self.links.start(second, second, self.cube["y3"]),
@@ -230,15 +232,15 @@
         for copy in self.step:
             copy.wait_recv()
         self.step = []
-        for v, rows, name in ((y, FIRST, "y3"), (y1, FIRST, "y3"), (y, SECOND, "y1"), (y3, SECOND, "y1")):
+        for v, rows, name in ((y, self.first, "y3"), (y1, self.first, "y3"), (y, self.second, "y1"), (y3, self.second, "y1")):
             self.step.append(self.links.start(self.part(v, rows), self.part(v, rows), self.cube[name]))
-        self.to_core(self.part(y1, FIRST))
-        self.to_core(self.part(y3, SECOND))
+        self.to_core(self.part(y1, self.first))
+        self.to_core(self.part(y3, self.second))
 
     def last(self):
         y = self.where[4]
         y1, y2, y3 = other(y, 1), other(y, 2), other(y, 3)
-        arrived = [(y3, FIRST), (y2, FIRST), (y1, SECOND), (y2, SECOND)]
+        arrived = [(y3, self.first), (y2, self.first), (y1, self.second), (y2, self.second)]
         for copy, (v, rows) in zip(self.step, arrived):
             copy.wait_recv()
             self.to_core(self.part(v, rows))
@@ -256,6 +258,8 @@
         grp, tx, ty, hi, y, core = where
         self.cube = cube_peers(grp, tx, hi, y, core)
         self.line = ring_peers(grp, tx, ty)
+        rows = half.shape[0]
+        self.whole, (self.first, self.second) = pl.ds(0, rows), halves(rows)
         self.ys = [other(y, 2), other(y, 3), other(y, 1), y]
 
     def add(self, z, h, v, rows, left, right):
@@ -279,21 +283,22 @@
     def far(self):
         core = self.where[5]
         y2, y3, y1, y = self.ys
-        for copy, v in zip(self.step, self.ys):
+        pieces, self.step = self.step, []
+        for k, (copy, v) in enumerate(zip(pieces, self.ys)):
             copy.wait_recv()
 
             def take(z, carry):
                 for h in range(2):
-                    self.add(z, h, v, WHOLE, self.packed.at[z, h, v, core], self.rd.at[z, h, v])
+                    self.add(z, h, v, self.whole, self.packed.at[z, h, v, core], self.rd.at[z, h, v])
                 return carry
 
             lax.fori_loop(0, 8, take, 0)
-        self.step = [
-            self.links.start(self.part(y3, FIRST), self.ry2.at[0, :, :, FIRST], self.cube["y3"]),
-            self.links.start(self.part(y2, FIRST), self.ry2.at[1, :, :, FIRST], self.cube["y3"]),
-            self.links.start(self.part(y1, SECOND), self.ry2.at[0, :, :, SECOND], self.cube["y1"]),
-            self.links.start(self.part(y2, SECOND), self.ry2.at[1, :, :, SECOND], self.cube["y1"]),
-        ]
+            if k in (1, 2):
+                rows, name = (self.first, "y3") if k == 1 else (self.second, "y1")
+                for n, u in enumerate((v, y2)):
+                    self.step.append(
+                        self.links.start(self.part(u, rows), self.ry2.at[n, :, :, rows], self.cube[name])
+                    )
 
     def near(self):
         y2, y3, y1, y = self.ys
@@ -301,15 +306,15 @@
 
         def take(z, carry):
             for h in range(2):
-                self.add(z, h, y, WHOLE, self.sums.at[z, h, y], self.ry2.at[0, z, h])
-                self.add(z, h, y1, FIRST, self.sums.at[z, h, y1, FIRST], self.ry2.at[1, z, h, FIRST])
-                self.add(z, h, y3, SECOND, self.sums.at[z, h, y3, SECOND], self.ry2.at[1, z, h, SECOND])
+                self.add(z, h, y, self.whole, self.sums.at[z, h, y], self.ry2.at[0, z, h])
+                self.add(z, h, y1, self.first, self.sums.at[z, h, y1, self.first], self.ry2.at[1, z, h, self.first])
+                self.add(z, h, y3, self.second, self.sums.at[z, h, y3, self.second], self.ry2.at[1, z, h, self.second])
             return carry
 
         lax.fori_loop(0, 8, take, 0)
         self.step = [
-            self.links.start(self.part(y1, FIRST), self.ry1.at[:, :, FIRST], self.cube["y1"]),
-            self.links.start(self.part(y3, SECOND), self.ry1.at[:, :, SECOND], self.cube["y3"]),
+            self.links.start(self.part(y1, self.first), self.ry1.at[:, :, self.first], self.cube["y1"]),
+            self.links.start(self.part(y3, self.second), self.ry1.at[:, :, self.second], self.cube["y3"]),
         ]
 
     def across(self):
@@ -318,7 +323,7 @@
 
         def take(z, carry):
             for h in range(2):
-                self.add(z, h, y, WHOLE, self.sums.at[z, h, y], self.ry1.at[z, h])
+                self.add(z, h, y, self.whole, self.sums.at[z, h, y], self.ry1.at[z, h])
             return carry
 
         lax.fori_loop(0, 8, take, 0)
@@ -329,7 +334,7 @@
         self.wait()
 
         def take(z, carry):
-            self.add(z, hi, y, WHOLE, self.sums.at[z, hi, y], self.rx.at[z])
+            self.add(z, hi, y, self.whole, self.sums.at[z, hi, y], self.rx.at[z])
             return carry
 
         lax.fori_loop(0, 8, take, 0)
@@ -352,16 +357,103 @@
         self.total[...] = self.half[...] + self.rg[...]
 
 
+def fold(tiles):
+    wide, mid, rest = tiles
+    lanes = lax.broadcasted_iota(jnp.int32, (8, 128), 1)
+    rows = lax.broadcasted_iota(jnp.int32, (8, 128), 0)
+    tail = jnp.zeros((8, 128), f32)
+    for n in range(4):
+        piece = rest[8 * n : 8 * n + 8]
+        piece = pltpu.roll(piece, 32 * n, 1) if n else piece
+        tail = jnp.where((lanes >= 32 * n) & (lanes < 32 * n + 32), piece, tail)
+    last = jnp.where(rows < 3, wide[24:32], jnp.where(rows < 6, pltpu.roll(mid[24:32], 3, 0), 0.0))
+    return jnp.concatenate([wide[:24], mid[:24], tail, last], axis=0)
+
+
+def unfold(rows):
+    tail, last = rows[48:56], rows[56:64]
+    rest = jnp.concatenate([tail] + [pltpu.roll(tail, 128 - 32 * n, 1) for n in range(1, 4)], axis=0)
+    return [
+        jnp.concatenate([rows[:24], last], axis=0),
+        jnp.concatenate([rows[24:48], pltpu.roll(last, 5, 0)], axis=0),
+        rest,
+    ]
+
+
 def choose(slots, place, blocks):
     value = None
     for i, block in enumerate(blocks):
-        term = jnp.where(slots[i] == place, block, 0.0)
+        term = jnp.where(slots[0, i] == place, block, 0.0)
         value = term if value is None else value + term
     return value
 
 
 def corner(slots, i):
-    return slots[i] // GY, slots[i] % GY
+    return slots[0, i] // GY, slots[0, i] % GY
+
+
+def prepare(slots, count, feats, occupancy, cot, w_conv1, w_down, w_conv2, mask, coarse, mp, gp, shard_a, shard_b, tmp, wide):
+    tmp[...] = jnp.zeros_like(tmp)
+    wide[...] = jnp.zeros_like(wide)
+    tmp[0, 0:27, 0:72] = w_conv1[...].astype(f32)
+    wide[0:8, 0:144] = w_down[...].astype(f32)
+    low = lane_tiles(wide[0:8, 0:256])
+    for j in range(3):
+        tmp[1, pl.ds(j, 8, stride=3), :] = relane(1, [(low, 48 * j, BASE_DOWN, 48)])[0]
+    shard_a[...] = (tmp[0] + tmp[1]).astype(bf16)
+    wide[0:27, 0:288] = w_conv2[...].astype(f32)
+    shard_b[...] = fold(lane_tiles(wide[...])).astype(bf16)
+
+    flags = []
+    for p in range(GX * GY):
+        flag = jnp.where(slots[0, 0] == p, 1.0, 0.0)
+        for i in range(1, CAP):
+            flag = flag + jnp.where((slots[0, i] == p) & (count[0] > i), 1.0, 0.0)
+        flags.append(flag)
+
+    def iotas(rows, lanes):
+        return [lax.broadcasted_iota(jnp.int32, (rows, lanes), d) for d in range(2)]
+
+    row, lane = iotas(256, 32)
+    pick_y = jnp.where(row // 8 == lane, 1.0, 0.0).astype(bf16)
+    row, lane = iotas(256, 8)
+    pick_z = row % 8 == lane
+    row, lane = iotas(128, 32)
+    pair_y = jnp.where(row // 8 == lane // 2, 1.0, 0.0).astype(bf16)
+    row, lane = iotas(128, 8)
+    pair_z = row % 8 == lane // 2
+    ones = jnp.ones((8, 256), bf16)
+    mp[1:17, 1:33] = jnp.zeros((16, 32, 8, 128), f32)
+    gp[1:9, 1:17] = jnp.zeros((8, 16, 8, 256), f32)
+    for px in range(GX):
+
+        def first(x, carry):
+            plane = occupancy[0, x].astype(f32).astype(bf16)
+            column = jnp.dot(pick_y, plane, preferred_element_type=f32)
+            column = jnp.where(pick_z, column, 0.0).astype(bf16)
+            value = jnp.dot(column, ones[:, :128], preferred_element_type=f32).reshape(32, 8, 128)
+            for py in range(GY):
+                at = slice(py * 8, py * 8 + 8)
+                live = value[at] * flags[px * GY + py]
+                mask[x, at] = live
+                mp[1 + x, 1 + py * 8 : 9 + py * 8, :, 0:C1] = feats[0, x, at].astype(f32) * live[:, :, 0:C1]
+            return carry
+
+        def second(a, carry):
+            plane = (occupancy[0, 2 * a] + occupancy[0, 2 * a + 1]).astype(f32).astype(bf16)
+            column = jnp.dot(pair_y, plane, preferred_element_type=f32)
+            column = jnp.where(pair_z, column, 0.0).astype(bf16)
+            value = jnp.minimum(jnp.dot(column, ones, preferred_element_type=f32), 1.0).reshape(16, 8, 256)
+            for py in range(GY):
+                at = slice(py * 4, py * 4 + 4)
+                live = value[at] * flags[px * GY + py]
+                coarse[a, at] = live
+                grad = cot[0, a, at].astype(f32) * live[:, 0:4, 0:C2]
+                gp[1 + a, 1 + py * 4 : 5 + py * 4, 0:4, 0:C2] = grad
+            return carry
+
+        lax.fori_loop(px * 8, px * 8 + 8, first, 0)
+        lax.fori_loop(px * 4, px * 4 + 4, second, 0)
 
 
 def unpack_first(full, w9, wd, w1g, wdg, tmp):
@@ -394,9 +486,7 @@
 
 def unpack_second(full, w2, big):
     def unpack(a, carry):
-        shards = [
-            lane_tiles(full[a // 4, (a // 2) % 2, (a % 2) * 2 + b // 2, b % 2].astype(f32)) for b in range(4)
-        ]
+        shards = [unfold(full[a // 4, (a // 2) % 2, (a % 2) * 2 + b // 2, b % 2].astype(f32)) for b in range(4)]
         for k in range(6):
             for c, tile in enumerate(to_row(shards, PIECES_TWO[k], 0, 2)):
                 big[c, pl.ds((a * 6 + k) * PITCH_W, 32), :] = tile
@@ -472,14 +562,15 @@
             for s, at, lane, n in PIECES_TWO[k]:
                 segments[s].append((tiles, lane, at, n))
         for b in range(4):
-            packed[a // 4, (a // 2) % 2, (a % 2) * 2 + b // 2, b % 2] = join(relane(3, segments[b])).astype(bf16)
+            packed[a // 4, (a // 2) % 2, (a % 2) * 2 + b // 2, b % 2] = fold(relane(3, segments[b])).astype(bf16)
         return carry
 
     lax.fori_loop(0, GROUPS, pack, 0)
 
 
 def whole_kernel(
-    slots, tile, grad, mask, coarse, shard_a, shard_b, out, total_a, total_b,
+    slots, count, feats, occupancy, cot, w_conv1, w_down, w_conv2, out, total_a, total_b,
+    mask, coarse, shard_a, shard_b, wide,
     full_a, full_b, mp, gp, dp, x9, x2, x3, w9, wd, w2, w1g, wdg, tmp, big, act, pm, hs, gs, r1, rdn,
     packed_a, packed_b, sums_a, rd_a, ry2_a, ry1_a, rx_a, rz_a, half_a, rg_a,
     sums_b, rd_b, ry2_b, ry1_b, rx_b, rz_b, half_b, rg_b, send, recv, own,
@@ -489,34 +580,33 @@
     cube = cube_peers(grp, tx, hi, y, core)
     around = halo_peers(grp, tx, ty)
     links = Links(send, recv)
-    barrier_with(ring_peers(grp, tx, ty) + [cube[n] for n in ("core", "y1", "y3", "x", "grp")] + around)
+    greeted = ring_peers(grp, tx, ty) + [cube[n] for n in ("core", "y1", "y3", "x", "grp")] + around
+    barrier = pltpu.get_barrier_semaphore()
+    for peer in greeted:
+        pl.semaphore_signal(barrier, inc=1, device_id=peer, device_id_type=MESH)
+    prepare(
+        slots, count, feats, occupancy, cot, w_conv1, w_down, w_conv2, mask, coarse, mp, gp, shard_a, shard_b, tmp, wide
+    )
+    pl.semaphore_wait(barrier, len(greeted))
 
     first = Gather(links, where, shard_a, full_a, own.at[0])
-    halo_m = links.halo(tile, mp, around, False)
-    inner_m = pltpu.make_async_copy(tile, mp.at[pl.ds(1, 16), pl.ds(1, 32)], own.at[2])
-    inner_m.start()
+    halo_m = links.halo(mp, mp, around, True)
+    first.across()
+    first.near()
     second = Gather(links, where, shard_b, full_b, own.at[1])
-    halo_g = links.halo(grad, gp, around, False)
-    inner_g = pltpu.make_async_copy(grad, gp.at[pl.ds(1, 8), pl.ds(1, 16)], own.at[3])
-    inner_g.start()
-
-    first.across()
-    inner_m.wait()
+    halo_g = links.halo(gp, gp, around, True)
     for copy in halo_m:
         copy.wait_recv()
     clear_edges(mp, tx, ty)
     for i in range(CAP):
         px, py = corner(slots, i)
         windows(x9, i, mp[pl.ds(px * 8, 10), pl.ds(py * 8, 10)], 8, False)
-    first.near()
+    first.far()
     second.across()
-    first.far()
-    second.near()
     first.last()
-    second.far()
     first.done()
     unpack_first(full_a, w9, wd, w1g, wdg, tmp)
-    second.last()
+    second.near()
 
     hs[...] = jnp.zeros_like(hs)
     downs = []
@@ -536,12 +626,12 @@
         raw = jnp.dot(pm[i * 128 : (i + 1) * 128, :], wd[...], preferred_element_type=f32)
         edge = coarse[pl.ds(px * 4, 4), pl.ds(py * 4, 4)]
         downs.append((edge * raw.reshape(4, 4, 8, 256)).astype(bf16).astype(f32))
+    second.far()
     for p in range(GX * GY):
         px, py = p // GY, p % GY
         dp[1 + px * 4 : 5 + px * 4, 1 + py * 4 : 5 + py * 4] = choose(slots, p, downs)
     halo_d = links.halo(dp, dp, around, True)
 
-    inner_g.wait()
     for copy in halo_g:
         copy.wait_recv()
     clear_edges(gp, tx, ty)
@@ -555,6 +645,7 @@
     edge = jnp.concatenate(edges, axis=0)
     spread_two = spread(grad_two)
     big[:, 27 * PITCH_R : 32 * PITCH_R, :] = jnp.zeros((2, 5 * PITCH_R, 128), f32)
+    second.last()
     for copy in halo_d:
         copy.wait_recv()
     clear_edges(dp, tx, ty)
@@ -661,32 +752,37 @@
         copy.wait_send()
 
 
-def whole(slots, tile, grad, mask, coarse, shard_a, shard_b):
-    def sums(lanes):
+def whole(order, count, feats, occupancy, cot, w_conv1, w_down, w_conv2):
+    def sums(rows):
         return [
-            pltpu.VMEM((8, 2, 4, 32, lanes), bf16),
-            pltpu.VMEM((8, 2, 4, 32, lanes), bf16),
-            pltpu.VMEM((2, 8, 2, 32, lanes), bf16),
-            pltpu.VMEM((8, 2, 32, lanes), bf16),
-            pltpu.VMEM((8, 32, lanes), bf16),
-            pltpu.VMEM((7, 32, lanes), bf16),
-            pltpu.VMEM((32, lanes), f32),
-            pltpu.VMEM((32, lanes), f32),
+            pltpu.VMEM((8, 2, 4, rows, 128), bf16),
+            pltpu.VMEM((8, 2, 4, rows, 128), bf16),
+            pltpu.VMEM((2, 8, 2, rows, 128), bf16),
+            pltpu.VMEM((8, 2, rows, 128), bf16),
+            pltpu.VMEM((8, rows, 128), bf16),
+            pltpu.VMEM((7, rows, 128), bf16),
+            pltpu.VMEM((rows, 128), f32),
+            pltpu.VMEM((rows, 128), f32),
         ]
 
     copies = 2 * 23 + 24 + 2 * 19
     return pl.pallas_call(
         whole_kernel,
-        in_specs=[pl.BlockSpec(memory_space=pltpu.SMEM)] + [pl.BlockSpec(memory_space=pltpu.VMEM)] * 6,
+        in_specs=[pl.BlockSpec(memory_space=pltpu.SMEM)] * 2 + [pl.BlockSpec(memory_space=pltpu.VMEM)] * 6,
         out_specs=[pl.BlockSpec(memory_space=pltpu.VMEM)] * 3,
         out_shape=[
             jax.ShapeDtypeStruct((8, 16, 8, 256), f32),
             jax.ShapeDtypeStruct((32, 128), f32),
-            jax.ShapeDtypeStruct((32, 384), f32),
+            jax.ShapeDtypeStruct((64, 128), f32),
         ],
         scratch_shapes=[
+            pltpu.VMEM((16, 32, 8, 128), f32),
+            pltpu.VMEM((8, 16, 8, 256), f32),
+            pltpu.VMEM((32, 128), bf16),
+            pltpu.VMEM((64, 128), bf16),
+            pltpu.VMEM((32, 384), f32),
             pltpu.VMEM((8, 2, 4, 2, 32, 128), bf16),
-            pltpu.VMEM((8, 2, 4, 2, 32, 384), bf16),
+            pltpu.VMEM((8, 2, 4, 2, 64, 128), bf16),
             pltpu.VMEM((18, 34, 8, 128), f32),
             pltpu.VMEM((10, 18, 8, 256), f32),
             pltpu.VMEM((10, 18, 8, 256), f32),
@@ -707,44 +803,30 @@
             pltpu.VMEM((32 * PITCH_S, 128), f32),
             pltpu.VMEM((2, 8 * PITCH_S, 128), f32),
             pltpu.VMEM((8, 2, 4, 2, 32, 128), bf16),
-            pltpu.VMEM((8, 2, 4, 2, 32, 384), bf16),
+            pltpu.VMEM((8, 2, 4, 2, 64, 128), bf16),
         ]
-        + sums(128)
-        + sums(384)
+        + sums(32)
+        + sums(64)
         + [
             pltpu.SemaphoreType.DMA((copies,)),
             pltpu.SemaphoreType.DMA((copies,)),
-            pltpu.SemaphoreType.DMA((4,)),
+            pltpu.SemaphoreType.DMA((2,)),
         ],
         compiler_params=pltpu.CompilerParams(collective_id=0, has_side_effects=True, vmem_limit_bytes=VMEM_LIMIT),
         name="whole",
-    )(slots, tile, grad, mask, coarse, shard_a, shard_b)
-
-
-def live_flags(order, count, bricks):
-    places = jnp.arange(bricks, dtype=jnp.int32)
-    ranks = jnp.arange(order.shape[0], dtype=jnp.int32)
-    match = (order[:, None] == places[None, :]) & (ranks[:, None] < count)
-    return jnp.any(match, axis=0).astype(f32)
+    )(order, count, feats, occupancy, cot, w_conv1, w_down, w_conv2)
 
 
 def local(features, voxel_mask, brick_order, brick_count, w_conv1, w_down, w_conv2, cotangent):
-    order = brick_order[0]
-    slots = order[:CAP]
-    shard_a = jnp.pad(w_conv1, ((0, 5), (0, 56))) + jnp.pad(w_down.reshape(24, 48), ((0, 8), (72, 8)))
-    shard_b = jnp.pad(w_conv2, ((0, 5), (0, 96)))
-    live = live_flags(order, brick_count[0], GX * GY).reshape(GX, GY)
-    live_map = jnp.repeat(jnp.repeat(live, 8, axis=0), 8, axis=1)
-    live_mask = voxel_mask[0].astype(f32) * live_map[..., None]
-    mask = jnp.broadcast_to(live_mask[..., None], (16, 32, 8, 128))
-    masked = jnp.pad(features[0].astype(f32), ((0, 0), (0, 0), (0, 0), (0, 32))) * mask
-    coarse = live_mask.reshape(8, 2, 16, 2, 4, 2).max(axis=(1, 3, 5))
-    coarse = jnp.broadcast_to(jnp.pad(coarse, ((0, 0), (0, 0), (0, 4)))[..., None], (8, 16, 8, 256))
-    grad_two = jnp.pad(cotangent[0].astype(f32), ((0, 0), (0, 0), (0, 4), (0, 64))) * coarse
-    out, total_a, total_b = whole(slots, masked, grad_two, mask, coarse, shard_a, shard_b)
+    out, total_a, total_b = whole(
+        brick_order, brick_count, features, voxel_mask, cotangent, w_conv1, w_down, w_conv2
+    )
     one = total_a[:27, :72]
     low = total_a[:24, 72:120].reshape(8, 144)
-    two = total_b[:27, :288]
+    main = jnp.concatenate([total_b[0:24], total_b[24:48]], axis=1)
+    last = jnp.concatenate([total_b[56:59], total_b[59:62]], axis=1)
+    rest = jnp.concatenate([total_b[48:56, 32 * n : 32 * n + 32] for n in range(4)], axis=0)
+    two = jnp.concatenate([jnp.concatenate([main, last], axis=0), rest[:27]], axis=1)
     return out[None, :, :, :4, :C2].astype(bf16), one, low, two
 
 

time: 134 us -> 113 us (0.84)
  local copies, waits for them, and re-layouts: 14.1 us -> 5.12 us
  other arithmetic: 6.98 us -> 0.63 us
  Pallas kernels: 110 us -> 105 us
    pallas_call x1, Pallas kernels: 110 us -> 105 us  [whole(): pl.pallas_call(whole_kernel, in_specs=[pl.BlockSpec(memory_space=pltpu.SM...]
    mul x3 -> x0, other arithmetic: 3.75 us -> none  [the longest x1 1.72 us: local(): jnp.pad(features[0].astype(f32), ((0, 0), (0, 0), (0, 0), (0, 32))) * mask]
    broadcast_in_dim x5 -> x0, local copies, waits for them, and re-layouts: 3.36 us -> none  [the longest x1 1.9 us: local(): mask = jnp.broadcast_to(live_mask[..., None], (16, 32, 8, 128))]
    add x1 -> x0, other arithmetic: 1.37 us -> none  [local(): jnp.pad(w_conv1, ((0, 5), (0, 56)))]
    pad x2 -> x0, local copies, waits for them, and re-layouts: 1.36 us -> none  [the longest x1 1.35 us: local(): shard_b = jnp.pad(w_conv2, ((0, 5), (0, 96)))]
    unnamed x7 -> x6, local copies, waits for them, and re-layouts: 2.88 us -> 2.29 us
where the time goes in v3:
time: 113 us; the launch traced here: 112 us
  Pallas kernels  105 us (93%)
  local copies, waits for them, and re-layouts  5.12 us (5%)
  between operations  1.31 us (1%)
    pallas_call x1, Pallas kernels, whole(): pl.pallas_call(whole_kernel, in_specs=[pl.BlockSpec(memory_space=pltpu.SM...  105 us
    unnamed x6, local copies, waits for them, and re-layouts  2.29 us

profile of v3, /device:TPU:8, one launch (start us, length us, event | category | flops | bytes accessed | tf_op | source)
XLA Modules:
  0.0 111.6 jit_solution(16583644518551430329)
XLA Ops:
  1.3 1.7 %copy.12.occupancy = s32[1,16,32,8]{3,2,1,0:T(8,128)} copy(s32[1,16,32,8]{2,3,1,0:T(8,128)} %param.9) | data formatting | bytes 32768 | tf_op args[1]
  3.0 104.6 %whole.1 = (f32[8,16,8,256]{3,2,1,0:T(8,128)}, f32[32,128]{1,0:T(8,128)}, f32[64,128]{1,0:T(8,128)}) custom-call(s32[1,8]{1,0:T(1,128)} %slots.1, s32[1]{0:T(128)S(6)} %copy.14.count, bf16[1,16,32,8,96]{4,3,2,1,0:T(8,128)(2,1)} %feats.1, s32[1,16,32,8]{3,2,1,0:T(8,128)} %copy.12.occupancy, bf16[1,8,16,4,192]{4,3,2,1,0:T(4,128)(2,1)} %cot.1, ...), custom_call_target="tpu_custom_call" | custom-call | tf_op jit(solution)/shard_map/whole/pallas_call | solution.py:769
  107.5 0.0 copy-start
  107.6 0.0 copy-start.1
  107.6 2.0 %fusion = bf16[1,8,16,4,192]{4,3,2,1,0:T(4,128)(2,1)} fusion(f32[8,16,8,256]{3,2,1,0:T(8,128)} %get-tuple-element.7), kind=kLoop, calls=%fused_computation.1 | loop fusion | bytes 393216 | tf_op jit(solution)/shard_map/convert_element_type | solution.py:830
  109.6 0.0 copy-done
  109.6 0.0 copy-done.1
  109.6 0.1 slice.39
  109.7 0.7 reshape.12
  110.3 0.1 fusion.4
  110.4 0.6 fusion.1
  111.0 0.6 copy.15
  (2 shorter events, 0.0 us)
Async XLA Ops:
  107.5 2.0 %copy-start = (f32[64,128]{1,0:T(8,128)S(1)}, f32[64,128]{1,0:T(8,128)}, u32[]{:S(2)}) copy-start(f32[64,128]{1,0:T(8,128)} %get-tuple-element.9) | copy-start | bytes 98308
  107.6 2.0 %copy-start.1 = (f32[32,128]{1,0:T(8,128)S(1)}, f32[32,128]{1,0:T(8,128)}, u32[]{:S(2)}) copy-start(f32[32,128]{1,0:T(8,128)} %get-tuple-element.8) | copy-start | bytes 49156

commit v4 on v3

--- a/solution.py
+++ b/solution.py
@@ -392,7 +392,7 @@
     return slots[0, i] // GY, slots[0, i] % GY
 
 
-def prepare(slots, count, feats, occupancy, cot, w_conv1, w_down, w_conv2, mask, coarse, mp, gp, shard_a, shard_b, tmp, wide):
+def pack_shards(w_conv1, w_down, w_conv2, shard_a, shard_b, tmp, wide):
     tmp[...] = jnp.zeros_like(tmp)
     wide[...] = jnp.zeros_like(wide)
     tmp[0, 0:27, 0:72] = w_conv1[...].astype(f32)
@@ -404,6 +404,8 @@
     wide[0:27, 0:288] = w_conv2[...].astype(f32)
     shard_b[...] = fold(lane_tiles(wide[...])).astype(bf16)
 
+
+def prepare(slots, count, feats, occupancy, cot, mask, coarse, mp, gp):
     flags = []
     for p in range(GX * GY):
         flag = jnp.where(slots[0, 0] == p, 1.0, 0.0)
@@ -414,23 +416,23 @@
     def iotas(rows, lanes):
         return [lax.broadcasted_iota(jnp.int32, (rows, lanes), d) for d in range(2)]
 
+    row, lane = iotas(256, 8)
+    pick_z = jnp.where(row % 8 == lane, 1.0, 0.0).astype(bf16)
     row, lane = iotas(256, 32)
-    pick_y = jnp.where(row // 8 == lane, 1.0, 0.0).astype(bf16)
-    row, lane = iotas(256, 8)
-    pick_z = row % 8 == lane
+    pick_y = row // 8 == lane
+    row, lane = iotas(128, 8)
+    pair_z = jnp.where(row % 8 == lane // 2, 1.0, 0.0).astype(bf16)
     row, lane = iotas(128, 32)
-    pair_y = jnp.where(row // 8 == lane // 2, 1.0, 0.0).astype(bf16)
-    row, lane = iotas(128, 8)
-    pair_z = row % 8 == lane // 2
-    ones = jnp.ones((8, 256), bf16)
+    pair_y = row // 8 == lane // 2
+    ones = jnp.ones((32, 256), bf16)
     mp[1:17, 1:33] = jnp.zeros((16, 32, 8, 128), f32)
     gp[1:9, 1:17] = jnp.zeros((8, 16, 8, 256), f32)
     for px in range(GX):
 
         def first(x, carry):
             plane = occupancy[0, x].astype(f32).astype(bf16)
-            column = jnp.dot(pick_y, plane, preferred_element_type=f32)
-            column = jnp.where(pick_z, column, 0.0).astype(bf16)
+            column = jnp.dot(pick_z, plane, preferred_element_type=f32)
+            column = jnp.where(pick_y, column, 0.0).astype(bf16)
             value = jnp.dot(column, ones[:, :128], preferred_element_type=f32).reshape(32, 8, 128)
             for py in range(GY):
                 at = slice(py * 8, py * 8 + 8)
@@ -441,8 +443,8 @@
 
         def second(a, carry):
             plane = (occupancy[0, 2 * a] + occupancy[0, 2 * a + 1]).astype(f32).astype(bf16)
-            column = jnp.dot(pair_y, plane, preferred_element_type=f32)
-            column = jnp.where(pair_z, column, 0.0).astype(bf16)
+            column = jnp.dot(pair_z, plane, preferred_element_type=f32)
+            column = jnp.where(pair_y, column, 0.0).astype(bf16)
             value = jnp.minimum(jnp.dot(column, ones, preferred_element_type=f32), 1.0).reshape(16, 8, 256)
             for py in range(GY):
                 at = slice(py * 4, py * 4 + 4)
@@ -452,8 +454,8 @@
                 gp[1 + a, 1 + py * 4 : 5 + py * 4, 0:4, 0:C2] = grad
             return carry
 
-        lax.fori_loop(px * 8, px * 8 + 8, first, 0)
-        lax.fori_loop(px * 4, px * 4 + 4, second, 0)
+        lax.fori_loop(px * 8, px * 8 + 8, first, 0, unroll=4)
+        lax.fori_loop(px * 4, px * 4 + 4, second, 0, unroll=4)
 
 
 def unpack_first(full, w9, wd, w1g, wdg, tmp):
@@ -472,7 +474,7 @@
                 wdg[c, pl.ds(pl.multiple_of((a * 3 + k) * 8, 8), 8), :] = tile
         return carry
 
-    lax.fori_loop(0, GROUPS, unpack, 0)
+    lax.fori_loop(0, GROUPS, unpack, 0, unroll=4)
     for t in range(27):
         k, oz = t // 3, t % 3
         w9[k * 128 : k * 128 + C1, oz * 128 : (oz + 1) * 128] = w1g[pl.ds(t, C1, stride=PITCH_W), :].astype(bf16)
@@ -492,7 +494,7 @@
                 big[c, pl.ds((a * 6 + k) * PITCH_W, 32), :] = tile
         return carry
 
-    lax.fori_loop(0, GROUPS, unpack, 0)
+    lax.fori_loop(0, GROUPS, unpack, 0, unroll=4)
 
     def order(k, carry):
         for oz in range(3):
@@ -503,7 +505,7 @@
         w2[pl.ds(pl.multiple_of(k * 256 + C2, 64), 256 - C2), :] = jnp.zeros((256 - C2, 768), bf16)
         return carry
 
-    lax.fori_loop(0, 9, order, 0)
+    lax.fori_loop(0, 9, order, 0, unroll=3)
 
 
 def windows(dst, i, window, edge, flip):
@@ -551,7 +553,7 @@
             packed[a // 4, (a // 2) % 2, (a % 2) * 2 + b // 2, b % 2] = value.astype(bf16)
         return carry
 
-    lax.fori_loop(0, GROUPS, pack, 0)
+    lax.fori_loop(0, GROUPS, pack, 0, unroll=4)
 
 
 def pack_second(packed, big):
@@ -565,12 +567,12 @@
             packed[a // 4, (a // 2) % 2, (a % 2) * 2 + b // 2, b % 2] = fold(relane(3, segments[b])).astype(bf16)
         return carry
 
-    lax.fori_loop(0, GROUPS, pack, 0)
+    lax.fori_loop(0, GROUPS, pack, 0, unroll=4)
 
 
 def whole_kernel(
-    slots, count, feats, occupancy, cot, w_conv1, w_down, w_conv2, out, total_a, total_b,
-    mask, coarse, shard_a, shard_b, wide,
+    slots, count, feats, occupancy, cot, w_conv1, w_down, w_conv2, out, grad_conv1, grad_down, grad_conv2,
+    total_a, total_b, mask, coarse, shard_a, shard_b, wide,
     full_a, full_b, mp, gp, dp, x9, x2, x3, w9, wd, w2, w1g, wdg, tmp, big, act, pm, hs, gs, r1, rdn,
     packed_a, packed_b, sums_a, rd_a, ry2_a, ry1_a, rx_a, rz_a, half_a, rg_a,
     sums_b, rd_b, ry2_b, ry1_b, rx_b, rz_b, half_b, rg_b, send, recv, own,
@@ -584,17 +586,17 @@
     barrier = pltpu.get_barrier_semaphore()
     for peer in greeted:
         pl.semaphore_signal(barrier, inc=1, device_id=peer, device_id_type=MESH)
-    prepare(
-        slots, count, feats, occupancy, cot, w_conv1, w_down, w_conv2, mask, coarse, mp, gp, shard_a, shard_b, tmp, wide
-    )
+    pack_shards(w_conv1, w_down, w_conv2, shard_a, shard_b, tmp, wide)
     pl.semaphore_wait(barrier, len(greeted))
 
     first = Gather(links, where, shard_a, full_a, own.at[0])
+    second = Gather(links, where, shard_b, full_b, own.at[1])
+    prepare(slots, count, feats, occupancy, cot, mask, coarse, mp, gp)
+    first.across()
     halo_m = links.halo(mp, mp, around, True)
-    first.across()
+    halo_g = links.halo(gp, gp, around, True)
     first.near()
-    second = Gather(links, where, shard_b, full_b, own.at[1])
-    halo_g = links.halo(gp, gp, around, True)
+    second.across()
     for copy in halo_m:
         copy.wait_recv()
     clear_edges(mp, tx, ty)
@@ -602,11 +604,11 @@
         px, py = corner(slots, i)
         windows(x9, i, mp[pl.ds(px * 8, 10), pl.ds(py * 8, 10)], 8, False)
     first.far()
-    second.across()
+    second.near()
     first.last()
     first.done()
     unpack_first(full_a, w9, wd, w1g, wdg, tmp)
-    second.near()
+    second.far()
 
     hs[...] = jnp.zeros_like(hs)
     downs = []
@@ -626,7 +628,7 @@
         raw = jnp.dot(pm[i * 128 : (i + 1) * 128, :], wd[...], preferred_element_type=f32)
         edge = coarse[pl.ds(px * 4, 4), pl.ds(py * 4, 4)]
         downs.append((edge * raw.reshape(4, 4, 8, 256)).astype(bf16).astype(f32))
-    second.far()
+    second.last()
     for p in range(GX * GY):
         px, py = p // GY, p % GY
         dp[1 + px * 4 : 5 + px * 4, 1 + py * 4 : 5 + py * 4] = choose(slots, p, downs)
@@ -645,7 +647,8 @@
     edge = jnp.concatenate(edges, axis=0)
     spread_two = spread(grad_two)
     big[:, 27 * PITCH_R : 32 * PITCH_R, :] = jnp.zeros((2, 5 * PITCH_R, 128), f32)
-    second.last()
+    second.done()
+    unpack_second(full_b, w2, big)
     for copy in halo_d:
         copy.wait_recv()
     clear_edges(dp, tx, ty)
@@ -666,9 +669,6 @@
     )
     sum_b.cores()
 
-    second.done()
-    unpack_second(full_b, w2, big)
-    sum_b.far()
     parts = []
     for oz in range(3):
         part = None
@@ -683,7 +683,7 @@
         parts.append(part.reshape(-1, 8, 256))
     back = conv(parts[::-1])
     grad_in = (grad_two + edge * back).astype(bf16)
-    sum_b.near()
+    sum_b.far()
 
     rdn[...] = jnp.zeros_like(rdn)
     for t in range(8):
@@ -714,7 +714,7 @@
         sig = jax.nn.sigmoid(value)
         spreads.append(spread(live * hidden * (sig * (1.0 + value * (1.0 - sig)))))
     spread_one = jnp.concatenate(spreads, axis=0)
-    sum_b.across()
+    sum_b.near()
     r1[27 * PITCH_S : 32 * PITCH_S, :] = jnp.zeros((5 * PITCH_S, 128), f32)
     for k in range(9):
         product = lax.dot_general(
@@ -728,7 +728,7 @@
         links, where, packed_a, total_a, sums_a, rd_a, ry2_a, ry1_a, rx_a, rz_a, half_a, rg_a
     )
     sum_a.cores()
-    sum_b.along()
+    sum_b.across()
 
     value = conv(three(jnp.dot(x2[...], w2[...], preferred_element_type=f32), 256))
     blocks = []
@@ -738,16 +738,25 @@
         rows = slice(i * 128, (i + 1) * 128)
         blocks.append((edges[i] * (down + value[rows])).reshape(4, 4, 8, 256))
     sum_a.far()
+    sum_b.along()
     for p in range(GX * GY):
         px, py = p // GY, p % GY
-        out[px * 4 : px * 4 + 4, py * 4 : py * 4 + 4] = choose(slots, p, blocks)
+        out[0, px * 4 : px * 4 + 4, py * 4 : py * 4 + 4] = choose(slots, p, blocks)[:, :, 0:4, 0:C2].astype(bf16)
     sum_a.near()
+    sum_a.across()
     sum_b.swap()
-    sum_a.across()
     sum_a.along()
     sum_b.done()
+    wide = unfold(total_b[...])
+    grad_conv2[:, 0:256] = jnp.concatenate(wide[:2], axis=1)[:27]
+    grad_conv2[:, 256:288] = wide[2][:27, :32]
     sum_a.swap()
     sum_a.done()
+    grad_conv1[...] = total_a[:27, :72]
+    low = [(total_a[pl.ds(j, 8, stride=3), :],) for j in range(3)]
+    low = relane(2, [(low[j], BASE_DOWN, 48 * j, 48) for j in range(3)])
+    grad_down[:, 0:128] = low[0]
+    grad_down[:, 128:144] = low[1][:, :16]
     for copy in links.sent:
         copy.wait_send()
 
@@ -769,13 +778,16 @@
     return pl.pallas_call(
         whole_kernel,
         in_specs=[pl.BlockSpec(memory_space=pltpu.SMEM)] * 2 + [pl.BlockSpec(memory_space=pltpu.VMEM)] * 6,
-        out_specs=[pl.BlockSpec(memory_space=pltpu.VMEM)] * 3,
+        out_specs=[pl.BlockSpec(memory_space=pltpu.VMEM)] * 4,
         out_shape=[
-            jax.ShapeDtypeStruct((8, 16, 8, 256), f32),
-            jax.ShapeDtypeStruct((32, 128), f32),
-            jax.ShapeDtypeStruct((64, 128), f32),
+            jax.ShapeDtypeStruct((1, 8, 16, 4, C2), bf16),
+            jax.ShapeDtypeStruct((27, 72), f32),
+            jax.ShapeDtypeStruct((8, 144), f32),
+            jax.ShapeDtypeStruct((27, 288), f32),
         ],
         scratch_shapes=[
+            pltpu.VMEM((32, 128), f32),
+            pltpu.VMEM((64, 128), f32),
             pltpu.VMEM((16, 32, 8, 128), f32),
             pltpu.VMEM((8, 16, 8, 256), f32),
             pltpu.VMEM((32, 128), bf16),
@@ -818,16 +830,9 @@
 
 
 def local(features, voxel_mask, brick_order, brick_count, w_conv1, w_down, w_conv2, cotangent):
-    out, total_a, total_b = whole(
-        brick_order, brick_count, features, voxel_mask, cotangent, w_conv1, w_down, w_conv2
+    return tuple(
+        whole(brick_order, brick_count, features, voxel_mask.transpose(0, 1, 3, 2), cotangent, w_conv1, w_down, w_conv2)
     )
-    one = total_a[:27, :72]
-    low = total_a[:24, 72:120].reshape(8, 144)
-    main = jnp.concatenate([total_b[0:24], total_b[24:48]], axis=1)
-    last = jnp.concatenate([total_b[56:59], total_b[59:62]], axis=1)
-    rest = jnp.concatenate([total_b[48:56, 32 * n : 32 * n + 32] for n in range(4)], axis=0)
-    two = jnp.concatenate([jnp.concatenate([main, last], axis=0), rest[:27]], axis=1)
-    return out[None, :, :, :4, :C2].astype(bf16), one, low, two
 
 
 def solution(mesh):

time: 113 us -> 98.9 us (0.88)
  the two profiles are of different devices: /device:TPU:8 before, /device:TPU:4 now
where the time goes in v4:
time: 98.9 us; the launch traced here: 98.8 us
  Pallas kernels  93.9 us (95%)
  local copies, waits for them, and re-layouts  3.59 us (4%)
  between operations  1.31 us (1%)
    pallas_call x1, Pallas kernels, whole(): pl.pallas_call(whole_kernel, in_specs=[pl.BlockSpec(memory_space=pltpu.SM...  93.9 us
    unnamed x10, local copies, waits for them, and re-layouts  3.59 us

profile of v4, /device:TPU:4, one launch (start us, length us, event | category | flops | bytes accessed | tf_op | source)
XLA Modules:
  0.0 98.8 jit_solution(3988532317753206768)
XLA Ops:
  1.3 93.9 %whole.1 = (bf16[1,8,16,4,192]{4,3,2,1,0:T(4,128)(2,1)}, f32[27,72]{1,0:T(8,128)}, f32[8,144]{1,0:T(8,128)}, f32[27,288]{1,0:T(8,128)}) custom-call(s32[1,8]{1,0:T(1,128)} %slots.1, s32[1]{0:T(128)S(6)} %copy.16.count, bf16[1,16,32,8,96]{4,3,2,1,0:T(8,128)(2,1)} %feats.1, s32[1,16,8,32]{3,2,1,0:T(8,128)} %bitcast.1, bf16[1,8,16,4,192]{4,3,2,1,0:T(4,128)(2,1)} %cot.1, ...), custom_call_target="tpu_custom_call" | custom-call | tf_op jit(solution)/shard_map/whole/pallas_call | solution.py:778
  95.2 0.0 copy-start.1
  95.2 0.0 copy-start.2
  95.2 1.8 %copy.17 = bf16[1,8,16,4,192]{4,3,2,1,0:T(4,128)(2,1)} copy(bf16[1,8,16,4,192]{4,3,2,1,0:T(4,128)(2,1)} %get-tuple-element.8) | data formatting | bytes 393216
  96.9 0.0 copy-done.1
  96.9 0.0 copy-start
  96.9 0.6 copy.18
  97.6 0.0 copy-done.2
  97.6 0.6 copy.19
  98.2 0.0 copy-done
  98.2 0.6 copy.20
Async XLA Ops:
  95.2 1.8 %copy-start.1 = (f32[27,72]{1,0:T(8,128)S(1)}, f32[27,72]{1,0:T(8,128)}, u32[]{:S(2)}) copy-start(f32[27,72]{1,0:T(8,128)} %get-tuple-element.9) | copy-start | bytes 23332
  95.2 2.4 %copy-start.2 = (f32[8,144]{1,0:T(8,128)S(1)}, f32[8,144]{1,0:T(8,128)}, u32[]{:S(2)}) copy-start(f32[8,144]{1,0:T(8,128)} %get-tuple-element.10) | copy-start | bytes 13828
  96.9 1.2 %copy-start = (f32[27,288]{1,0:T(8,128)S(1)}, f32[27,288]{1,0:T(8,128)}, u32[]{:S(2)}) copy-start(f32[27,288]{1,0:T(8,128)} %get-tuple-element.11) | copy-start | bytes 93316

commit v5 on v4

--- a/solution.py
+++ b/solution.py
@@ -112,6 +112,7 @@
         "y1": (grp, tx, ty_of(hi, other(y, 1), core)),
         "y3": (grp, tx, ty_of(hi, other(y, 3), core)),
         "x": (1 - grp, tx, ty_of(1 - hi, y, core)),
+        "xx": (grp, tx, ty_of(1 - hi, y, core)),
         "grp": (1 - grp, tx, ty_of(hi, y, core)),
     }
 
@@ -251,15 +252,16 @@
 
 
 class Scatter:
-    def __init__(self, links, where, packed, total, sums, rd, ry2, ry1, rx, rz, half, rg):
+    def __init__(self, links, where, packed, total, sums, rd, ry2, ry1, rz, half, rg):
         self.links, self.where, self.packed, self.total = links, where, packed, total
         self.sums, self.rd, self.ry2, self.ry1 = sums, rd, ry2, ry1
-        self.rx, self.rz, self.half, self.rg = rx, rz, half, rg
+        self.rz, self.half, self.rg = rz, half, rg
         grp, tx, ty, hi, y, core = where
         self.cube = cube_peers(grp, tx, hi, y, core)
         self.line = ring_peers(grp, tx, ty)
-        rows = half.shape[0]
+        rows = half.shape[1]
         self.whole, (self.first, self.second) = pl.ds(0, rows), halves(rows)
+        self.pieces = {}
         self.ys = [other(y, 2), other(y, 3), other(y, 1), y]
 
     def add(self, z, h, v, rows, left, right):
@@ -273,52 +275,60 @@
         for copy in self.step:
             copy.wait_recv()
 
-    def cores(self):
+    def cores(self, pieces, h):
         core = self.where[5]
-        self.step = [
-            self.links.start(self.packed.at[:, :, v, 1 - core], self.rd.at[:, :, v], self.cube["core"])
-            for v in self.ys
-        ]
+        for k in pieces:
+            v = self.ys[k]
+            copy = self.links.start(
+                self.packed.at[:, h, v, 1 - core], self.rd.at[:, h, v], self.cube["core"]
+            )
+            self.pieces[k, h] = copy
 
     def far(self):
         core = self.where[5]
         y2, y3, y1, y = self.ys
-        pieces, self.step = self.step, []
-        for k, (copy, v) in enumerate(zip(pieces, self.ys)):
+        self.step = []
+        for (k, h), copy in self.pieces.items():
+            v = self.ys[k]
             copy.wait_recv()
 
             def take(z, carry):
-                for h in range(2):
-                    self.add(z, h, v, self.whole, self.packed.at[z, h, v, core], self.rd.at[z, h, v])
+                self.add(z, h, v, self.whole, self.packed.at[z, h, v, core], self.rd.at[z, h, v])
                 return carry
 
-            lax.fori_loop(0, 8, take, 0)
+            lax.fori_loop(0, 8, take, 0, unroll=2)
             if k in (1, 2):
                 rows, name = (self.first, "y3") if k == 1 else (self.second, "y1")
                 for n, u in enumerate((v, y2)):
                     self.step.append(
-                        self.links.start(self.part(u, rows), self.ry2.at[n, :, :, rows], self.cube[name])
+                        self.links.start(
+                            self.sums.at[:, h, u, rows], self.ry2.at[n, :, h, rows], self.cube[name]
+                        )
                     )
 
     def near(self):
         y2, y3, y1, y = self.ys
-        self.wait()
-
-        def take(z, carry):
-            for h in range(2):
+        far, self.step = self.step, []
+        for h in range(2):
+            for copy in far[2 * h : 2 * h + 2] + far[4 + 2 * h : 6 + 2 * h]:
+                copy.wait_recv()
+
+            def take(z, carry):
                 self.add(z, h, y, self.whole, self.sums.at[z, h, y], self.ry2.at[0, z, h])
                 self.add(z, h, y1, self.first, self.sums.at[z, h, y1, self.first], self.ry2.at[1, z, h, self.first])
-                self.add(z, h, y3, self.second, self.sums.at[z, h, y3, self.second], self.ry2.at[1, z, h, self.second])
-            return carry
-
-        lax.fori_loop(0, 8, take, 0)
-        self.step = [
-            self.links.start(self.part(y1, self.first), self.ry1.at[:, :, self.first], self.cube["y1"]),
-            self.links.start(self.part(y3, self.second), self.ry1.at[:, :, self.second], self.cube["y3"]),
-        ]
-
-    def across(self):
-        hi, y = self.where[3], self.where[4]
+                self.add(
+                    z, h, y3, self.second, self.sums.at[z, h, y3, self.second], self.ry2.at[1, z, h, self.second]
+                )
+                return carry
+
+            lax.fori_loop(0, 8, take, 0, unroll=2)
+            for v, rows, name in ((y1, self.first, "y1"), (y3, self.second, "y3")):
+                self.step.append(
+                    self.links.start(self.sums.at[:, h, v, rows], self.ry1.at[:, h, rows], self.cube[name])
+                )
+
+    def along(self):
+        tx, y = self.where[1], self.where[4]
         self.wait()
 
         def take(z, carry):
@@ -327,34 +337,28 @@
             return carry
 
         lax.fori_loop(0, 8, take, 0)
-        self.step = [self.links.start(self.sums.at[:, 1 - hi, y], self.rx, self.cube["x"])]
-
-    def along(self):
-        tx, hi, y = self.where[1], self.where[3], self.where[4]
-        self.wait()
-
-        def take(z, carry):
-            self.add(z, hi, y, self.whole, self.sums.at[z, hi, y], self.rx.at[z])
-            return carry
-
-        lax.fori_loop(0, 8, take, 0)
         self.step = [
-            self.links.start(self.sums.at[(tx + d + 1) % N_TX, hi, y], self.rz.at[d], peer)
+            self.links.start(self.sums.at[(tx + d + 1) % N_TX, :, y], self.rz.at[d], peer)
             for d, peer in enumerate(self.line)
         ]
 
     def swap(self):
         tx, hi, y = self.where[1], self.where[3], self.where[4]
         self.wait()
-        value = self.sums[tx, hi, y].astype(f32)
-        for d in range(N_TX - 1):
-            value = value + self.rz[d].astype(f32)
-        self.half[...] = value
-        self.step = [self.links.start(self.half, self.rg, self.cube["grp"])]
+        for h in range(2):
+            value = self.sums[tx, h, y].astype(f32)
+            for d in range(N_TX - 1):
+                value = value + self.rz[d, h].astype(f32)
+            self.half[h] = value
+        self.step = [
+            self.links.start(self.half.at[hi], self.rg.at[0], self.cube["grp"]),
+            self.links.start(self.half.at[1 - hi], self.rg.at[1], self.cube["x"]),
+            self.links.start(self.half.at[1 - hi], self.rg.at[2], self.cube["xx"]),
+        ]
 
     def done(self):
         self.wait()
-        self.total[...] = self.half[...] + self.rg[...]
+        self.total[...] = (self.half[self.where[3]] + self.rg[0]) + (self.rg[1] + self.rg[2])
 
 
 def fold(tiles):
@@ -533,10 +537,9 @@
     return jnp.concatenate([v.reshape(value.shape).astype(bf16) for v in (above, mid, below)], axis=1)
 
 
-def pack_first(packed, r1, rdn, tmp):
-    tmp[...] = jnp.zeros_like(tmp)
-
-    def pack(a, carry):
+def pack_first(packed, r1, rdn, tmp, pair, h):
+    def pack(z, carry):
+        a = z * 4 + h * 2 + pair
         segments = [[] for _ in range(4)]
         downs = []
         for k in range(3):
@@ -550,39 +553,46 @@
                 m = 3 * b + j
                 tmp[b, pl.ds(j, 8, stride=3), :] = relane(1, [(downs[m // 4], m % 4 * 48, BASE_DOWN, 48)])[0]
             value = relane(1, segments[b])[0] + tmp[b]
-            packed[a // 4, (a // 2) % 2, (a % 2) * 2 + b // 2, b % 2] = value.astype(bf16)
+            packed[z, h, pair * 2 + b // 2, b % 2] = value.astype(bf16)
         return carry
 
-    lax.fori_loop(0, GROUPS, pack, 0, unroll=4)
-
-
-def pack_second(packed, big):
-    def pack(a, carry):
+    lax.fori_loop(0, 8, pack, 0, unroll=4)
+
+
+def pack_second(packed, big, pair, h):
+    def pack(z, carry):
+        a = z * 4 + h * 2 + pair
         segments = [[] for _ in range(4)]
         for k in range(6):
             tiles = [big[c, pl.ds(a * 6 + k, 32, stride=PITCH_R), :] for c in range(2)]
             for s, at, lane, n in PIECES_TWO[k]:
                 segments[s].append((tiles, lane, at, n))
         for b in range(4):
-            packed[a // 4, (a // 2) % 2, (a % 2) * 2 + b // 2, b % 2] = fold(relane(3, segments[b])).astype(bf16)
+            packed[z, h, pair * 2 + b // 2, b % 2] = fold(relane(3, segments[b])).astype(bf16)
         return carry
 
-    lax.fori_loop(0, GROUPS, pack, 0, unroll=4)
+    lax.fori_loop(0, 8, pack, 0, unroll=4)
 
 
 def whole_kernel(
-    slots, count, feats, occupancy, cot, w_conv1, w_down, w_conv2, out, grad_conv1, grad_down, grad_conv2,
-    total_a, total_b, mask, coarse, shard_a, shard_b, wide,
+    slots, count, feats_in, occupancy_in, cot_in, w_conv1, w_down, w_conv2, out, grad_conv1, grad_down, grad_conv2,
+    feats, occupancy, cot, total_a, total_b, mask, coarse, shard_a, shard_b, wide,
     full_a, full_b, mp, gp, dp, x9, x2, x3, w9, wd, w2, w1g, wdg, tmp, big, act, pm, hs, gs, r1, rdn,
-    packed_a, packed_b, sums_a, rd_a, ry2_a, ry1_a, rx_a, rz_a, half_a, rg_a,
-    sums_b, rd_b, ry2_b, ry1_b, rx_b, rz_b, half_b, rg_b, send, recv, own,
+    packed_a, packed_b, sums_a, rd_a, ry2_a, ry1_a, rz_a, half_a, rg_a,
+    sums_b, rd_b, ry2_b, ry1_b, rz_b, half_b, rg_b, send, recv, own,
 ):
     where = place()
     grp, tx, ty, hi, y, core = where
     cube = cube_peers(grp, tx, hi, y, core)
     around = halo_peers(grp, tx, ty)
     links = Links(send, recv)
-    greeted = ring_peers(grp, tx, ty) + [cube[n] for n in ("core", "y1", "y3", "x", "grp")] + around
+    loads = [
+        pltpu.make_async_copy(src, dst, own.at[2 + k])
+        for k, (src, dst) in enumerate(((feats_in, feats), (occupancy_in, occupancy), (cot_in, cot)))
+    ]
+    for load in loads:
+        load.start()
+    greeted = ring_peers(grp, tx, ty) + [cube[n] for n in ("core", "y1", "y3", "x", "xx", "grp")] + around
     barrier = pltpu.get_barrier_semaphore()
     for peer in greeted:
         pl.semaphore_signal(barrier, inc=1, device_id=peer, device_id_type=MESH)
@@ -591,7 +601,13 @@
 
     first = Gather(links, where, shard_a, full_a, own.at[0])
     second = Gather(links, where, shard_b, full_b, own.at[1])
+    for load in loads:
+        load.wait()
     prepare(slots, count, feats, occupancy, cot, mask, coarse, mp, gp)
+    hs[...] = jnp.zeros_like(hs)
+    rdn[...] = jnp.zeros_like(rdn)
+    r1[27 * PITCH_S : 32 * PITCH_S, :] = jnp.zeros((5 * PITCH_S, 128), f32)
+    big[:, 27 * PITCH_R : 32 * PITCH_R, :] = jnp.zeros((2, 5 * PITCH_R, 128), f32)
     first.across()
     halo_m = links.halo(mp, mp, around, True)
     halo_g = links.halo(gp, gp, around, True)
@@ -610,25 +626,27 @@
     unpack_first(full_a, w9, wd, w1g, wdg, tmp)
     second.far()
 
-    hs[...] = jnp.zeros_like(hs)
-    downs = []
+    lives, edges = [], []
     for i in range(CAP):
         px, py = corner(slots, i)
-        value = conv(three(jnp.dot(x9[i * 512 : (i + 1) * 512, :], w9[...], preferred_element_type=f32), 128))
-        act[i * 512 : (i + 1) * 512, :] = value
-        live = mask[pl.ds(px * 8, 8), pl.ds(py * 8, 8)].reshape(512, 128)
-        hidden = (live * jax.nn.silu(value)).astype(bf16).astype(f32).reshape(4, 2, 4, 2, 8, 128)
-        for p in range(2):
-            for q in range(2):
-                for b in range(4):
-                    hs[:, p * 2 + q, b * 16 : b * 16 + 8, :] = hidden[:, p, b, q]
-        for t in range(8):
-            patch = hs[:, t // 2, pl.ds(t % 2, 32, stride=2), :].reshape(128, 128)
-            pm[i * 128 : (i + 1) * 128, t * 128 : (t + 1) * 128] = patch.astype(bf16)
-        raw = jnp.dot(pm[i * 128 : (i + 1) * 128, :], wd[...], preferred_element_type=f32)
-        edge = coarse[pl.ds(px * 4, 4), pl.ds(py * 4, 4)]
-        downs.append((edge * raw.reshape(4, 4, 8, 256)).astype(bf16).astype(f32))
+        lives.append(mask[pl.ds(px * 8, 8), pl.ds(py * 8, 8)].reshape(512, 128))
+        edges.append(coarse[pl.ds(px * 4, 4), pl.ds(py * 4, 4)].reshape(128, 256))
+    live = jnp.concatenate(lives, axis=0)
+    edge = jnp.concatenate(edges, axis=0)
+    value = conv(three(jnp.dot(x9[...], w9[...], preferred_element_type=f32), 128))
+    act[...] = value
+    hidden = (live * jax.nn.silu(value)).astype(bf16).astype(f32).reshape(CAP, 4, 2, 4, 2, 8, 128)
+    for p in range(2):
+        for q in range(2):
+            for b in range(4):
+                hs[:, :, p * 2 + q, b * 16 : b * 16 + 8, :] = hidden[:, :, p, b, q]
     second.last()
+    for t in range(8):
+        patch = hs[:, :, t // 2, pl.ds(t % 2, 32, stride=2), :].reshape(256, 128)
+        pm[:, t * 128 : (t + 1) * 128] = patch.astype(bf16)
+    raw = jnp.dot(pm[...], wd[...], preferred_element_type=f32)
+    down = (edge * raw).astype(bf16).astype(f32)
+    downs = [down[i * 128 : (i + 1) * 128].reshape(4, 4, 8, 256) for i in range(CAP)]
     for p in range(GX * GY):
         px, py = p // GY, p % GY
         dp[1 + px * 4 : 5 + px * 4, 1 + py * 4 : 5 + py * 4] = choose(slots, p, downs)
@@ -637,18 +655,29 @@
     for copy in halo_g:
         copy.wait_recv()
     clear_edges(gp, tx, ty)
-    grads, edges = [], []
+    grads = []
     for i in range(CAP):
         px, py = corner(slots, i)
         windows(x3, i, gp[pl.ds(px * 4, 6), pl.ds(py * 4, 6)], 4, True)
         grads.append(gp[pl.ds(px * 4 + 1, 4), pl.ds(py * 4 + 1, 4)].reshape(128, 256))
-        edges.append(coarse[pl.ds(px * 4, 4), pl.ds(py * 4, 4)].reshape(128, 256))
     grad_two = jnp.concatenate(grads, axis=0)
-    edge = jnp.concatenate(edges, axis=0)
     spread_two = spread(grad_two)
-    big[:, 27 * PITCH_R : 32 * PITCH_R, :] = jnp.zeros((2, 5 * PITCH_R, 128), f32)
     second.done()
     unpack_second(full_b, w2, big)
+    parts = []
+    for oz in range(3):
+        part = None
+        for k in range(9):
+            term = lax.dot_general(
+                x3[:, k * 256 : (k + 1) * 256],
+                w2[k * 256 : (k + 1) * 256, oz * 256 : (oz + 1) * 256],
+                (((1,), (1,)), ((), ())),
+                preferred_element_type=f32,
+            )
+            part = term if part is None else part + term
+        parts.append(part.reshape(-1, 8, 256))
+    back = conv(parts[::-1])
+    grad_in = (grad_two + edge * back).astype(bf16)
     for copy in halo_d:
         copy.wait_recv()
     clear_edges(dp, tx, ty)
@@ -663,59 +692,33 @@
             for c in range(2):
                 at = oz * 256 + c * 128
                 big[c, (3 * k + oz) * PITCH_R : (3 * k + oz) * PITCH_R + 256, :] = product[:, at : at + 128]
-    pack_second(packed_b, big)
-    sum_b = Scatter(
-        links, where, packed_b, total_b, sums_b, rd_b, ry2_b, ry1_b, rx_b, rz_b, half_b, rg_b
-    )
-    sum_b.cores()
-
-    parts = []
-    for oz in range(3):
-        part = None
-        for k in range(9):
-            term = lax.dot_general(
-                x3[:, k * 256 : (k + 1) * 256],
-                w2[k * 256 : (k + 1) * 256, oz * 256 : (oz + 1) * 256],
-                (((1,), (1,)), ((), ())),
-                preferred_element_type=f32,
-            )
-            part = term if part is None else part + term
-        parts.append(part.reshape(-1, 8, 256))
-    back = conv(parts[::-1])
-    grad_in = (grad_two + edge * back).astype(bf16)
-    sum_b.far()
-
-    rdn[...] = jnp.zeros_like(rdn)
+    sum_b = Scatter(links, where, packed_b, total_b, sums_b, rd_b, ry2_b, ry1_b, rz_b, half_b, rg_b)
+    for pair, pieces in ((1 - y // 2, (0, 1)), (y // 2, (2, 3))):
+        for h in range(2):
+            pack_second(packed_b, big, pair, h)
+            sum_b.cores(pieces, h)
+
     for t in range(8):
         product = lax.dot_general(
             pm[:, t * 128 : (t + 1) * 128], grad_in, (((0,), (0,)), ((), ())), preferred_element_type=f32
         )
         for c in range(2):
             rdn[c, t * PITCH_S : t * PITCH_S + 128, :] = product[:, c * 128 : (c + 1) * 128]
-    spreads = []
-    for i in range(CAP):
-        px, py = corner(slots, i)
-        for t in range(8):
-            part = lax.dot_general(
-                grad_in[i * 128 : (i + 1) * 128],
-                wd[t * 128 : (t + 1) * 128, :],
-                (((1,), (1,)), ((), ())),
-                preferred_element_type=f32,
-            )
-            gs[:, t // 2, pl.ds(t % 2, 32, stride=2), :] = part.reshape(4, 32, 128)
-        rows = []
-        for p in range(2):
-            for b in range(4):
-                for q in range(2):
-                    rows.append(gs[:, p * 2 + q, b * 16 : b * 16 + 8, :])
-        hidden = jnp.stack(rows, axis=1).reshape(512, 128)
-        live = mask[pl.ds(px * 8, 8), pl.ds(py * 8, 8)].reshape(512, 128)
-        value = act[i * 512 : (i + 1) * 512, :]
-        sig = jax.nn.sigmoid(value)
-        spreads.append(spread(live * hidden * (sig * (1.0 + value * (1.0 - sig)))))
-    spread_one = jnp.concatenate(spreads, axis=0)
-    sum_b.near()
-    r1[27 * PITCH_S : 32 * PITCH_S, :] = jnp.zeros((5 * PITCH_S, 128), f32)
+    for t in range(8):
+        part = lax.dot_general(
+            grad_in, wd[t * 128 : (t + 1) * 128, :], (((1,), (1,)), ((), ())), preferred_element_type=f32
+        )
+        gs[:, :, t // 2, pl.ds(t % 2, 32, stride=2), :] = part.reshape(CAP, 4, 32, 128)
+    rows = []
+    for p in range(2):
+        for b in range(4):
+            for q in range(2):
+                rows.append(gs[:, :, p * 2 + q, b * 16 : b * 16 + 8, :])
+    hidden = jnp.stack(rows, axis=2).reshape(1024, 128)
+    value = act[...]
+    sig = jax.nn.sigmoid(value)
+    spread_one = spread(live * hidden * (sig * (1.0 + value * (1.0 - sig))))
+    sum_b.far()
     for k in range(9):
         product = lax.dot_general(
             x9[:, k * 128 : (k + 1) * 128], spread_one, (((0,), (0,)), ((), ())), preferred_element_type=f32
@@ -723,29 +726,34 @@
         for oz in range(3):
             at = (3 * k + oz) * PITCH_S
             r1[at : at + 128, :] = product[:, oz * 128 : (oz + 1) * 128]
-    pack_first(packed_a, r1, rdn, tmp)
-    sum_a = Scatter(
-        links, where, packed_a, total_a, sums_a, rd_a, ry2_a, ry1_a, rx_a, rz_a, half_a, rg_a
-    )
-    sum_a.cores()
-    sum_b.across()
-
-    value = conv(three(jnp.dot(x2[...], w2[...], preferred_element_type=f32), 256))
+    tmp[...] = jnp.zeros_like(tmp)
+    sum_a = Scatter(links, where, packed_a, total_a, sums_a, rd_a, ry2_a, ry1_a, rz_a, half_a, rg_a)
+    for pair, pieces in ((1 - y // 2, (0, 1)), (y // 2, (2, 3))):
+        for h in range(2):
+            pack_first(packed_a, r1, rdn, tmp, pair, h)
+            sum_a.cores(pieces, h)
+    sum_b.near()
+
+    parts = [
+        jnp.dot(x2[...], w2[:, oz * 256 : (oz + 1) * 256], preferred_element_type=f32).reshape(-1, 8, 256)
+        for oz in range(2)
+    ]
+    sum_a.far()
+    parts.append(jnp.dot(x2[...], w2[:, 512:768], preferred_element_type=f32).reshape(-1, 8, 256))
+    value = conv(parts)
+    sum_b.along()
     blocks = []
     for i in range(CAP):
         px, py = corner(slots, i)
         down = dp[pl.ds(px * 4 + 1, 4), pl.ds(py * 4 + 1, 4)].reshape(128, 256)
         rows = slice(i * 128, (i + 1) * 128)
         blocks.append((edges[i] * (down + value[rows])).reshape(4, 4, 8, 256))
-    sum_a.far()
-    sum_b.along()
+    sum_a.near()
     for p in range(GX * GY):
         px, py = p // GY, p % GY
         out[0, px * 4 : px * 4 + 4, py * 4 : py * 4 + 4] = choose(slots, p, blocks)[:, :, 0:4, 0:C2].astype(bf16)
-    sum_a.near()
-    sum_a.across()
+    sum_a.along()
     sum_b.swap()
-    sum_a.along()
     sum_b.done()
     wide = unfold(total_b[...])
     grad_conv2[:, 0:256] = jnp.concatenate(wide[:2], axis=1)[:27]
@@ -768,16 +776,17 @@
             pltpu.VMEM((8, 2, 4, rows, 128), bf16),
             pltpu.VMEM((2, 8, 2, rows, 128), bf16),
             pltpu.VMEM((8, 2, rows, 128), bf16),
-            pltpu.VMEM((8, rows, 128), bf16),
-            pltpu.VMEM((7, rows, 128), bf16),
-            pltpu.VMEM((rows, 128), f32),
-            pltpu.VMEM((rows, 128), f32),
+            pltpu.VMEM((7, 2, rows, 128), bf16),
+            pltpu.VMEM((2, rows, 128), f32),
+            pltpu.VMEM((3, rows, 128), f32),
         ]
 
-    copies = 2 * 23 + 24 + 2 * 19
+    copies = 2 * 23 + 24 + 2 * 30
     return pl.pallas_call(
         whole_kernel,
-        in_specs=[pl.BlockSpec(memory_space=pltpu.SMEM)] * 2 + [pl.BlockSpec(memory_space=pltpu.VMEM)] * 6,
+        in_specs=[pl.BlockSpec(memory_space=pltpu.SMEM)] * 2
+        + [pl.BlockSpec(memory_space=pl.ANY)] * 3
+        + [pl.BlockSpec(memory_space=pltpu.VMEM)] * 3,
         out_specs=[pl.BlockSpec(memory_space=pltpu.VMEM)] * 4,
         out_shape=[
             jax.ShapeDtypeStruct((1, 8, 16, 4, C2), bf16),
@@ -786,6 +795,9 @@
             jax.ShapeDtypeStruct((27, 288), f32),
         ],
         scratch_shapes=[
+            pltpu.VMEM((1, 16, 32, 8, C1), bf16),
+            pltpu.VMEM((1, 16, 8, 32), jnp.int32),
+            pltpu.VMEM((1, 8, 16, 4, C2), bf16),
             pltpu.VMEM((32, 128), f32),
             pltpu.VMEM((64, 128), f32),
             pltpu.VMEM((16, 32, 8, 128), f32),
@@ -810,8 +822,8 @@
             pltpu.VMEM((2, 32 * PITCH_R, 128), f32),
             pltpu.VMEM((1024, 128), f32),
             pltpu.VMEM((256, 1024), bf16),
-            pltpu.VMEM((4, 4, 64, 128), f32),
-            pltpu.VMEM((4, 4, 64, 128), f32),
+            pltpu.VMEM((CAP, 4, 4, 64, 128), f32),
+            pltpu.VMEM((CAP, 4, 4, 64, 128), f32),
             pltpu.VMEM((32 * PITCH_S, 128), f32),
             pltpu.VMEM((2, 8 * PITCH_S, 128), f32),
             pltpu.VMEM((8, 2, 4, 2, 32, 128), bf16),
@@ -822,7 +834,7 @@
         + [
             pltpu.SemaphoreType.DMA((copies,)),
             pltpu.SemaphoreType.DMA((copies,)),
-            pltpu.SemaphoreType.DMA((2,)),
+            pltpu.SemaphoreType.DMA((5,)),
         ],
         compiler_params=pltpu.CompilerParams(collective_id=0, has_side_effects=True, vmem_limit_bytes=VMEM_LIMIT),
         name="whole",

time: 98.9 us -> 91.2 us (0.922)
  the two profiles are of different devices: /device:TPU:4 before, /device:TPU:8 now
where the time goes in v5:
time: 91.2 us; the launch traced here: 91 us
  Pallas kernels  86.1 us (94%)
  local copies, waits for them, and re-layouts  3.59 us (4%)
  between operations  1.31 us (1%)
    pallas_call x1, Pallas kernels, whole(): pl.pallas_call(whole_kernel, in_specs=[pl.BlockSpec(memory_space=pltpu.SM...  86.1 us
    unnamed x10, local copies, waits for them, and re-layouts  3.59 us

profile of v5, /device:TPU:8, one launch (start us, length us, event | category | flops | bytes accessed | tf_op | source)
XLA Modules:
  0.0 91.0 jit_solution(731928531464470029)
XLA Ops:
  1.3 86.1 %whole.1 = (bf16[1,8,16,4,192]{4,3,2,1,0:T(4,128)(2,1)}, f32[27,72]{1,0:T(8,128)}, f32[8,144]{1,0:T(8,128)}, f32[27,288]{1,0:T(8,128)}) custom-call(s32[1,8]{1,0:T(1,128)} %slots.1, s32[1]{0:T(128)S(6)} %copy.16.count, bf16[1,16,32,8,96]{4,3,2,1,0:T(8,128)(2,1)} %feats_in.1, s32[1,16,8,32]{3,2,1,0:T(8,128)} %bitcast.1, bf16[1,8,16,4,192]{4,3,2,1,0:T(4,128)(2,1)} %cot_in.1, ...), custom_call_target="tpu_custom_call" | custom-call | tf_op jit(solution)/shard_map/whole/pallas_call | solution.py:785
  87.4 0.0 copy-start.1
  87.4 0.0 copy-start.2
  87.4 1.8 %copy.17 = bf16[1,8,16,4,192]{4,3,2,1,0:T(4,128)(2,1)} copy(bf16[1,8,16,4,192]{4,3,2,1,0:T(4,128)(2,1)} %get-tuple-element.8) | data formatting | bytes 393216
  89.2 0.0 copy-done.1
  89.2 0.0 copy-start
  89.2 0.6 copy.18
  89.8 0.0 copy-done.2
  89.8 0.6 copy.19
  90.4 0.0 copy-done
  90.4 0.6 copy.20
Async XLA Ops:
  87.4 1.8 %copy-start.1 = (f32[27,72]{1,0:T(8,128)S(1)}, f32[27,72]{1,0:T(8,128)}, u32[]{:S(2)}) copy-start(f32[27,72]{1,0:T(8,128)} %get-tuple-element.9) | copy-start | bytes 23332
  87.4 2.4 %copy-start.2 = (f32[8,144]{1,0:T(8,128)S(1)}, f32[8,144]{1,0:T(8,128)}, u32[]{:S(2)}) copy-start(f32[8,144]{1,0:T(8,128)} %get-tuple-element.10) | copy-start | bytes 13828
  89.2 1.2 %copy-start = (f32[27,288]{1,0:T(8,128)S(1)}, f32[27,288]{1,0:T(8,128)}, u32[]{:S(2)}) copy-start(f32[27,288]{1,0:T(8,128)} %get-tuple-element.11) | copy-start | bytes 93316

commit v6 on v5

--- a/solution.py
+++ b/solution.py
@@ -103,6 +103,10 @@
     return [(grp, (tx + d) % N_TX, ty) for d in range(1, N_TX)]
 
 
+def across_peers(grp, tx, hi, y, core):
+    return [(1 - grp, (tx + d) % N_TX, (1 - hi) * 8 + y * 2 + core) for d in range(N_TX)]
+
+
 def cube_peers(grp, tx, hi, y, core):
     def ty_of(h, v, c):
         return h * 8 + v * 2 + c
@@ -197,6 +201,7 @@
         self.cube = cube_peers(grp, tx, hi, y, core)
         mine = full.at[tx, hi, y, core]
         self.line = [links.start(shard, mine, peer) for peer in ring_peers(grp, tx, ty)]
+        self.line += [links.start(shard, mine, peer) for peer in across_peers(grp, tx, hi, y, core)]
         self.own = pltpu.make_async_copy(shard, mine, own)
         self.own.start()
         self.partner = []
@@ -207,25 +212,17 @@
     def to_core(self, ref):
         self.partner.append(self.links.start(ref, ref, self.cube["core"]))
 
-    def across(self):
+    def near(self):
         grp, tx, ty, hi, y, core = self.where
         self.own.wait()
         for copy in self.line:
-            copy.wait_recv()
-        column = self.full.at[:, hi, y, core]
-        self.step = [self.links.start(column, column, self.cube["x"])]
-        self.to_core(column)
-
-    def near(self):
-        grp, tx, ty, hi, y, core = self.where
-        for copy in self.step:
             copy.wait_recv()
         first, second = self.part(y, self.first), self.part(y, self.second)
         self.step = [
             self.links.start(first, first, self.cube["y1"]),
             self.links.start(second, second, self.cube["y3"]),
         ]
-        self.to_core(self.full.at[:, 1 - hi, y, core])
+        self.to_core(self.full.at[:, :, y, core])
 
     def far(self):
         y = self.where[4]
@@ -409,7 +406,7 @@
     shard_b[...] = fold(lane_tiles(wide[...])).astype(bf16)
 
 
-def prepare(slots, count, feats, occupancy, cot, mask, coarse, mp, gp):
+def prepare(slots, count, feats, occupancy, cot, mask, coarse, mp, gp, fine):
     flags = []
     for p in range(GX * GY):
         flag = jnp.where(slots[0, 0] == p, 1.0, 0.0)
@@ -429,9 +426,11 @@
     row, lane = iotas(128, 32)
     pair_y = row // 8 == lane // 2
     ones = jnp.ones((32, 256), bf16)
-    mp[1:17, 1:33] = jnp.zeros((16, 32, 8, 128), f32)
-    gp[1:9, 1:17] = jnp.zeros((8, 16, 8, 256), f32)
-    for px in range(GX):
+    if fine:
+        mp[1:17, 1:33] = jnp.zeros((16, 32, 8, 128), f32)
+    else:
+        gp[1:9, 1:17] = jnp.zeros((8, 16, 8, 256), f32)
+    for px in range(GX) if fine else ():
 
         def first(x, carry):
             plane = occupancy[0, x].astype(f32).astype(bf16)
@@ -444,6 +443,10 @@
                 mask[x, at] = live
                 mp[1 + x, 1 + py * 8 : 9 + py * 8, :, 0:C1] = feats[0, x, at].astype(f32) * live[:, :, 0:C1]
             return carry
+
+        lax.fori_loop(px * 8, px * 8 + 8, first, 0, unroll=4)
+
+    for px in range(GX) if not fine else ():
 
         def second(a, carry):
             plane = (occupancy[0, 2 * a] + occupancy[0, 2 * a + 1]).astype(f32).astype(bf16)
@@ -458,7 +461,6 @@
                 gp[1 + a, 1 + py * 4 : 5 + py * 4, 0:4, 0:C2] = grad
             return carry
 
-        lax.fori_loop(px * 8, px * 8 + 8, first, 0, unroll=4)
         lax.fori_loop(px * 4, px * 4 + 4, second, 0, unroll=4)
 
 
@@ -466,11 +468,11 @@
     def unpack(a, carry):
         shards = []
         for b in range(4):
-            value = full[a // 4, (a // 2) % 2, (a % 2) * 2 + b // 2, b % 2].astype(f32)
-            tmp[b] = value
+            value = full[a // 4, (a // 2) % 2, (a % 2) * 2 + b // 2, b % 2]
+            tmp[b] = value.astype(f32)
             shards.append([value])
         for k in range(3):
-            w1g[pl.ds((a * 3 + k) * PITCH_W, 32), :] = to_row(shards, PIECES_ONE[k], 0, 1)[0]
+            w1g[pl.ds((a * 3 + k) * PITCH_W, 32), :] = to_row(shards, PIECES_ONE[k], 0, 1)[0].astype(f32)
         chunks = [[tmp[b, pl.ds(j, 8, stride=3), :]] for b in range(4) for j in range(3)]
         for k in range(3):
             segments = [(chunks[4 * k + n], BASE_DOWN, 48 * n, 48) for n in range(4)]
@@ -492,10 +494,16 @@
 
 def unpack_second(full, w2, big):
     def unpack(a, carry):
-        shards = [unfold(full[a // 4, (a // 2) % 2, (a % 2) * 2 + b // 2, b % 2].astype(f32)) for b in range(4)]
+        shards = [
+            [
+                tile.astype(bf16)
+                for tile in unfold(full[a // 4, (a // 2) % 2, (a % 2) * 2 + b // 2, b % 2].astype(f32))
+            ]
+            for b in range(4)
+        ]
         for k in range(6):
             for c, tile in enumerate(to_row(shards, PIECES_TWO[k], 0, 2)):
-                big[c, pl.ds((a * 6 + k) * PITCH_W, 32), :] = tile
+                big[c, pl.ds((a * 6 + k) * PITCH_W, 32), :] = tile.astype(f32)
         return carry
 
     lax.fori_loop(0, GROUPS, unpack, 0, unroll=4)
@@ -544,7 +552,7 @@
         downs = []
         for k in range(3):
             ci = a * 3 + k
-            tiles = [r1[pl.ds(ci, 32, stride=PITCH_S), :]]
+            tiles = [r1[pl.ds(ci, 32, stride=PITCH_S), :].astype(bf16)]
             for s, at, lane, n in PIECES_ONE[k]:
                 segments[s].append((tiles, lane, at, n))
             downs.append([rdn[c, pl.ds(ci, 8, stride=PITCH_S), :] for c in range(2)])
@@ -552,7 +560,7 @@
             for j in range(3):
                 m = 3 * b + j
                 tmp[b, pl.ds(j, 8, stride=3), :] = relane(1, [(downs[m // 4], m % 4 * 48, BASE_DOWN, 48)])[0]
-            value = relane(1, segments[b])[0] + tmp[b]
+            value = relane(1, segments[b])[0].astype(f32) + tmp[b]
             packed[z, h, pair * 2 + b // 2, b % 2] = value.astype(bf16)
         return carry
 
@@ -564,11 +572,13 @@
         a = z * 4 + h * 2 + pair
         segments = [[] for _ in range(4)]
         for k in range(6):
-            tiles = [big[c, pl.ds(a * 6 + k, 32, stride=PITCH_R), :] for c in range(2)]
+            tiles = [big[c, pl.ds(a * 6 + k, 32, stride=PITCH_R), :].astype(bf16) for c in range(2)]
             for s, at, lane, n in PIECES_TWO[k]:
                 segments[s].append((tiles, lane, at, n))
         for b in range(4):
-            packed[z, h, pair * 2 + b // 2, b % 2] = fold(relane(3, segments[b])).astype(bf16)
+            packed[z, h, pair * 2 + b // 2, b % 2] = fold(
+                [tile.astype(f32) for tile in relane(3, segments[b])]
+            ).astype(bf16)
         return carry
 
     lax.fori_loop(0, 8, pack, 0, unroll=4)
@@ -592,7 +602,7 @@
     ]
     for load in loads:
         load.start()
-    greeted = ring_peers(grp, tx, ty) + [cube[n] for n in ("core", "y1", "y3", "x", "xx", "grp")] + around
+    greeted = ring_peers(grp, tx, ty) + across_peers(grp, tx, hi, y, core) + [cube[n] for n in ("core", "y1", "y3", "xx", "grp")] + around
     barrier = pltpu.get_barrier_semaphore()
     for peer in greeted:
         pl.semaphore_signal(barrier, inc=1, device_id=peer, device_id_type=MESH)
@@ -603,28 +613,27 @@
     second = Gather(links, where, shard_b, full_b, own.at[1])
     for load in loads:
         load.wait()
-    prepare(slots, count, feats, occupancy, cot, mask, coarse, mp, gp)
-    hs[...] = jnp.zeros_like(hs)
-    rdn[...] = jnp.zeros_like(rdn)
-    r1[27 * PITCH_S : 32 * PITCH_S, :] = jnp.zeros((5 * PITCH_S, 128), f32)
-    big[:, 27 * PITCH_R : 32 * PITCH_R, :] = jnp.zeros((2, 5 * PITCH_R, 128), f32)
-    first.across()
+    prepare(slots, count, feats, occupancy, cot, mask, coarse, mp, gp, True)
     halo_m = links.halo(mp, mp, around, True)
+    first.near()
+    prepare(slots, count, feats, occupancy, cot, mask, coarse, mp, gp, False)
+    second.near()
+    first.far()
     halo_g = links.halo(gp, gp, around, True)
-    first.near()
-    second.across()
     for copy in halo_m:
         copy.wait_recv()
     clear_edges(mp, tx, ty)
     for i in range(CAP):
         px, py = corner(slots, i)
         windows(x9, i, mp[pl.ds(px * 8, 10), pl.ds(py * 8, 10)], 8, False)
-    first.far()
-    second.near()
     first.last()
+    second.far()
+    hs[...] = jnp.zeros_like(hs)
+    rdn[...] = jnp.zeros_like(rdn)
+    r1[27 * PITCH_S : 32 * PITCH_S, :] = jnp.zeros((5 * PITCH_S, 128), f32)
+    big[:, 27 * PITCH_R : 32 * PITCH_R, :] = jnp.zeros((2, 5 * PITCH_R, 128), f32)
     first.done()
     unpack_first(full_a, w9, wd, w1g, wdg, tmp)
-    second.far()
 
     lives, edges = [], []
     for i in range(CAP):
@@ -781,7 +790,7 @@
             pltpu.VMEM((3, rows, 128), f32),
         ]
 
-    copies = 2 * 23 + 24 + 2 * 30
+    copies = 2 * 30 + 24 + 2 * 30
     return pl.pallas_call(
         whole_kernel,
         in_specs=[pl.BlockSpec(memory_space=pltpu.SMEM)] * 2

time: 91.2 us -> 85 us (0.932)
  Pallas kernels: 86.1 us -> 79.6 us
    pallas_call x1, Pallas kernels: 86.1 us -> 79.6 us  [whole(): pl.pallas_call(whole_kernel, in_specs=[pl.BlockSpec(memory_space=pltpu.SM...]
where the time goes in v6:
time: 85 us; the launch traced here: 84.5 us
  Pallas kernels  79.6 us (94%)
  local copies, waits for them, and re-layouts  3.59 us (4%)
  between operations  1.31 us (2%)
    pallas_call x1, Pallas kernels, whole(): pl.pallas_call(whole_kernel, in_specs=[pl.BlockSpec(memory_space=pltpu.SM...  79.6 us
    unnamed x10, local copies, waits for them, and re-layouts  3.59 us

profile of v6, /device:TPU:8, one launch (start us, length us, event | category | flops | bytes accessed | tf_op | source)
XLA Modules:
  0.0 84.5 jit_solution(17957379022379154192)
XLA Ops:
  1.3 79.6 %whole.1 = (bf16[1,8,16,4,192]{4,3,2,1,0:T(4,128)(2,1)}, f32[27,72]{1,0:T(8,128)}, f32[8,144]{1,0:T(8,128)}, f32[27,288]{1,0:T(8,128)}) custom-call(s32[1,8]{1,0:T(1,128)} %slots.1, s32[1]{0:T(128)S(6)} %copy.16.count, bf16[1,16,32,8,96]{4,3,2,1,0:T(8,128)(2,1)} %feats_in.1, s32[1,16,8,32]{3,2,1,0:T(8,128)} %bitcast.1, bf16[1,8,16,4,192]{4,3,2,1,0:T(4,128)(2,1)} %cot_in.1, ...), custom_call_target="tpu_custom_call" | custom-call | tf_op jit(solution)/shard_map/whole/pallas_call | solution.py:794
  80.9 0.0 copy-start.1
  80.9 0.0 copy-start.2
  80.9 1.8 %copy.17 = bf16[1,8,16,4,192]{4,3,2,1,0:T(4,128)(2,1)} copy(bf16[1,8,16,4,192]{4,3,2,1,0:T(4,128)(2,1)} %get-tuple-element.8) | data formatting | bytes 393216
  82.7 0.0 copy-done.1
  82.7 0.0 copy-start
  82.7 0.6 copy.18
  83.3 0.0 copy-done.2
  83.3 0.6 copy.19
  83.9 0.0 copy-done
  83.9 0.6 copy.20
Async XLA Ops:
  80.9 1.8 %copy-start.1 = (f32[27,72]{1,0:T(8,128)S(1)}, f32[27,72]{1,0:T(8,128)}, u32[]{:S(2)}) copy-start(f32[27,72]{1,0:T(8,128)} %get-tuple-element.9) | copy-start | bytes 23332
  80.9 2.4 %copy-start.2 = (f32[8,144]{1,0:T(8,128)S(1)}, f32[8,144]{1,0:T(8,128)}, u32[]{:S(2)}) copy-start(f32[8,144]{1,0:T(8,128)} %get-tuple-element.10) | copy-start | bytes 13828
  82.7 1.2 %copy-start = (f32[27,288]{1,0:T(8,128)S(1)}, f32[27,288]{1,0:T(8,128)}, u32[]{:S(2)}) copy-start(f32[27,288]{1,0:T(8,128)} %get-tuple-element.11) | copy-start | bytes 93316

commit v7 on v6

--- a/solution.py
+++ b/solution.py
@@ -136,6 +136,32 @@
     return pl.ds(size + 1, 1) if step < 0 else pl.ds(0, 1) if step > 0 else pl.ds(1, size)
 
 
+def squeeze(slabs, narrow):
+    if narrow:
+        pairs = slabs.reshape(slabs.shape[0] // 2, 2, 8, slabs.shape[2])
+        slabs = pairs[:, 0] + pltpu.roll(pairs[:, 1], 4, 1)
+    return slabs.reshape(-1, slabs.shape[2]).astype(bf16)
+
+
+def widen(rows, narrow):
+    slabs = rows.astype(f32).reshape(-1, 8, rows.shape[1])
+    if not narrow:
+        return slabs
+    low = lax.broadcasted_iota(jnp.int32, slabs.shape, 1) < 4
+    pairs = [jnp.where(low, slabs, 0.0), jnp.where(low, pltpu.roll(slabs, 4, 1), 0.0)]
+    return jnp.stack(pairs, axis=1).reshape(-1, 8, rows.shape[1])
+
+
+def land(dst, copies, bufs, narrow):
+    size_x, size_y = dst.shape[0] - 2, dst.shape[1] - 2
+    for copy in copies:
+        copy.wait_recv()
+    for n, (at_x, at_y) in enumerate(((0, 0), (size_x + 1, size_y + 1))):
+        side_x, side_y = widen(bufs[2][n], narrow), widen(bufs[3][n], narrow)
+        dst[at_x : at_x + 1, 1 : size_y + 1] = side_x.reshape(1, size_y, 8, -1)
+        dst[1 : size_x + 1, at_y : at_y + 1] = side_y.reshape(size_x, 1, 8, -1)
+
+
 def clear_edges(dst, tx, ty):
     size_x, size_y = dst.shape[0], dst.shape[1]
 
@@ -174,18 +200,23 @@
         self.sent.append(copy)
         return copy
 
-    def halo(self, src, dst, peers, inside):
+    def halo(self, dst, peers, bufs, narrow):
+        send_x, send_y, recv_x, recv_y = bufs
         size_x, size_y = dst.shape[0] - 2, dst.shape[1] - 2
-        shift = 1 if inside else 0
+        for n, (at_x, at_y) in enumerate(((1, 1), (size_x, size_y))):
+            send_x[n] = squeeze(dst[at_x, 1 : size_y + 1], narrow)
+            send_y[n] = squeeze(dst[1 : size_x + 1, at_y], narrow)
         copies = []
         for peer, (dx, dy) in zip(peers, STEPS):
-            copies.append(
-                self.start(
-                    src.at[edge_out(dx, size_x, shift), edge_out(dy, size_y, shift)],
-                    dst.at[edge_in(dx, size_x), edge_in(dy, size_y)],
-                    peer,
-                )
-            )
+            side = (dx + dy + 1) // 2
+            if dy == 0:
+                src, to = send_x.at[side], recv_x.at[1 - side]
+            elif dx == 0:
+                src, to = send_y.at[side], recv_y.at[1 - side]
+            else:
+                src = dst.at[edge_out(dx, size_x, 1), edge_out(dy, size_y, 1)]
+                to = dst.at[edge_in(dx, size_x), edge_in(dy, size_y)]
+            copies.append(self.start(src, to, peer))
         return copies
 
 
@@ -589,8 +620,10 @@
     feats, occupancy, cot, total_a, total_b, mask, coarse, shard_a, shard_b, wide,
     full_a, full_b, mp, gp, dp, x9, x2, x3, w9, wd, w2, w1g, wdg, tmp, big, act, pm, hs, gs, r1, rdn,
     packed_a, packed_b, sums_a, rd_a, ry2_a, ry1_a, rz_a, half_a, rg_a,
-    sums_b, rd_b, ry2_b, ry1_b, rz_b, half_b, rg_b, send, recv, own,
+    sums_b, rd_b, ry2_b, ry1_b, rz_b, half_b, rg_b, *rest,
 ):
+    bufs_m, bufs_g, bufs_d = rest[0:4], rest[4:8], rest[8:12]
+    send, recv, own = rest[12:]
     where = place()
     grp, tx, ty, hi, y, core = where
     cube = cube_peers(grp, tx, hi, y, core)
@@ -614,20 +647,19 @@
     for load in loads:
         load.wait()
     prepare(slots, count, feats, occupancy, cot, mask, coarse, mp, gp, True)
-    halo_m = links.halo(mp, mp, around, True)
+    halo_m = links.halo(mp, around, bufs_m, False)
     first.near()
     prepare(slots, count, feats, occupancy, cot, mask, coarse, mp, gp, False)
     second.near()
     first.far()
-    halo_g = links.halo(gp, gp, around, True)
-    for copy in halo_m:
-        copy.wait_recv()
+    halo_g = links.halo(gp, around, bufs_g, True)
+    land(mp, halo_m, bufs_m, False)
     clear_edges(mp, tx, ty)
     for i in range(CAP):
         px, py = corner(slots, i)
         windows(x9, i, mp[pl.ds(px * 8, 10), pl.ds(py * 8, 10)], 8, False)
+    second.far()
     first.last()
-    second.far()
     hs[...] = jnp.zeros_like(hs)
     rdn[...] = jnp.zeros_like(rdn)
     r1[27 * PITCH_S : 32 * PITCH_S, :] = jnp.zeros((5 * PITCH_S, 128), f32)
@@ -659,10 +691,9 @@
     for p in range(GX * GY):
         px, py = p // GY, p % GY
         dp[1 + px * 4 : 5 + px * 4, 1 + py * 4 : 5 + py * 4] = choose(slots, p, downs)
-    halo_d = links.halo(dp, dp, around, True)
-
-    for copy in halo_g:
-        copy.wait_recv()
+    halo_d = links.halo(dp, around, bufs_d, True)
+
+    land(gp, halo_g, bufs_g, True)
     clear_edges(gp, tx, ty)
     grads = []
     for i in range(CAP):
@@ -687,8 +718,7 @@
         parts.append(part.reshape(-1, 8, 256))
     back = conv(parts[::-1])
     grad_in = (grad_two + edge * back).astype(bf16)
-    for copy in halo_d:
-        copy.wait_recv()
+    land(dp, halo_d, bufs_d, True)
     clear_edges(dp, tx, ty)
     for i in range(CAP):
         px, py = corner(slots, i)
@@ -718,6 +748,7 @@
             grad_in, wd[t * 128 : (t + 1) * 128, :], (((1,), (1,)), ((), ())), preferred_element_type=f32
         )
         gs[:, :, t // 2, pl.ds(t % 2, 32, stride=2), :] = part.reshape(CAP, 4, 32, 128)
+    sum_b.far()
     rows = []
     for p in range(2):
         for b in range(4):
@@ -727,7 +758,6 @@
     value = act[...]
     sig = jax.nn.sigmoid(value)
     spread_one = spread(live * hidden * (sig * (1.0 + value * (1.0 - sig))))
-    sum_b.far()
     for k in range(9):
         product = lax.dot_general(
             x9[:, k * 128 : (k + 1) * 128], spread_one, (((0,), (0,)), ((), ())), preferred_element_type=f32
@@ -763,11 +793,11 @@
         out[0, px * 4 : px * 4 + 4, py * 4 : py * 4 + 4] = choose(slots, p, blocks)[:, :, 0:4, 0:C2].astype(bf16)
     sum_a.along()
     sum_b.swap()
+    sum_a.swap()
     sum_b.done()
     wide = unfold(total_b[...])
     grad_conv2[:, 0:256] = jnp.concatenate(wide[:2], axis=1)[:27]
     grad_conv2[:, 256:288] = wide[2][:27, :32]
-    sum_a.swap()
     sum_a.done()
     grad_conv1[...] = total_a[:27, :72]
     low = [(total_a[pl.ds(j, 8, stride=3), :],) for j in range(3)]
@@ -841,6 +871,11 @@
         + sums(32)
         + sums(64)
         + [
+            pltpu.VMEM((2, rows, lanes), bf16)
+            for sides, lanes in (((256, 128), 128), ((64, 32), 256), ((64, 32), 256))
+            for rows in sides + sides
+        ]
+        + [
             pltpu.SemaphoreType.DMA((copies,)),
             pltpu.SemaphoreType.DMA((copies,)),
             pltpu.SemaphoreType.DMA((5,)),

time: 85 us -> 82.4 us (0.969)
  Pallas kernels: 79.6 us -> 77.4 us
    pallas_call x1, Pallas kernels: 79.6 us -> 77.4 us  [whole(): pl.pallas_call(whole_kernel, in_specs=[pl.BlockSpec(memory_space=pltpu.SM...]
where the time goes in v7:
time: 82.4 us; the launch traced here: 82.3 us
  Pallas kernels  77.4 us (94%)
  local copies, waits for them, and re-layouts  3.59 us (4%)
  between operations  1.31 us (2%)
    pallas_call x1, Pallas kernels, whole(): pl.pallas_call(whole_kernel, in_specs=[pl.BlockSpec(memory_space=pltpu.SM...  77.4 us
    unnamed x10, local copies, waits for them, and re-layouts  3.59 us

profile of v7, /device:TPU:8, one launch (start us, length us, event | category | flops | bytes accessed | tf_op | source)
XLA Modules:
  0.0 82.3 jit_solution(16572178068363144346)
XLA Ops:
  1.3 77.4 %whole.1 = (bf16[1,8,16,4,192]{4,3,2,1,0:T(4,128)(2,1)}, f32[27,72]{1,0:T(8,128)}, f32[8,144]{1,0:T(8,128)}, f32[27,288]{1,0:T(8,128)}) custom-call(s32[1,8]{1,0:T(1,128)} %slots.1, s32[1]{0:T(128)S(6)} %copy.16.count, bf16[1,16,32,8,96]{4,3,2,1,0:T(8,128)(2,1)} %feats_in.1, s32[1,16,8,32]{3,2,1,0:T(8,128)} %bitcast.1, bf16[1,8,16,4,192]{4,3,2,1,0:T(4,128)(2,1)} %cot_in.1, ...), custom_call_target="tpu_custom_call" | custom-call | tf_op jit(solution)/shard_map/whole/pallas_call | solution.py:824
  78.7 0.0 copy-start.1
  78.7 0.0 copy-start.2
  78.7 1.8 %copy.17 = bf16[1,8,16,4,192]{4,3,2,1,0:T(4,128)(2,1)} copy(bf16[1,8,16,4,192]{4,3,2,1,0:T(4,128)(2,1)} %get-tuple-element.8) | data formatting | bytes 393216
  80.4 0.0 copy-done.1
  80.4 0.0 copy-start
  80.4 0.6 copy.18
  81.0 0.0 copy-done.2
  81.1 0.6 copy.19
  81.7 0.0 copy-done
  81.7 0.6 copy.20
Async XLA Ops:
  78.7 1.8 %copy-start.1 = (f32[27,72]{1,0:T(8,128)S(1)}, f32[27,72]{1,0:T(8,128)}, u32[]{:S(2)}) copy-start(f32[27,72]{1,0:T(8,128)} %get-tuple-element.9) | copy-start | bytes 23332
  78.7 2.4 %copy-start.2 = (f32[8,144]{1,0:T(8,128)S(1)}, f32[8,144]{1,0:T(8,128)}, u32[]{:S(2)}) copy-start(f32[8,144]{1,0:T(8,128)} %get-tuple-element.10) | copy-start | bytes 13828
  80.4 1.2 %copy-start = (f32[27,288]{1,0:T(8,128)S(1)}, f32[27,288]{1,0:T(8,128)}, u32[]{:S(2)}) copy-start(f32[27,288]{1,0:T(8,128)} %get-tuple-element.11) | copy-start | bytes 93316

commit v8 on v7

--- a/solution.py
+++ b/solution.py
@@ -184,7 +184,7 @@
 
 class Links:
     def __init__(self, send, recv):
-        self.send, self.recv, self.sent = send, recv, []
+        self.send, self.recv, self.sent, self.left = send, recv, [], 0
 
     def start(self, src, dst, peer):
         k = len(self.sent)
@@ -199,6 +199,11 @@
         copy.start()
         self.sent.append(copy)
         return copy
+
+    def flush(self, upto):
+        for copy in self.sent[self.left : upto]:
+            copy.wait_send()
+        self.left = upto
 
     def halo(self, dst, peers, bufs, narrow):
         send_x, send_y, recv_x, recv_y = bufs
@@ -791,9 +796,13 @@
     for p in range(GX * GY):
         px, py = p // GY, p % GY
         out[0, px * 4 : px * 4 + 4, py * 4 : py * 4 + 4] = choose(slots, p, blocks)[:, :, 0:4, 0:C2].astype(bf16)
+    before = len(links.sent)
     sum_a.along()
+    links.flush(before)
+    before = len(links.sent)
     sum_b.swap()
     sum_a.swap()
+    links.flush(before)
     sum_b.done()
     wide = unfold(total_b[...])
     grad_conv2[:, 0:256] = jnp.concatenate(wide[:2], axis=1)[:27]
@@ -804,8 +813,7 @@
     low = relane(2, [(low[j], BASE_DOWN, 48 * j, 48) for j in range(3)])
     grad_down[:, 0:128] = low[0]
     grad_down[:, 128:144] = low[1][:, :16]
-    for copy in links.sent:
-        copy.wait_send()
+    links.flush(len(links.sent))
 
 
 def whole(order, count, feats, occupancy, cot, w_conv1, w_down, w_conv2):

time: 82.4 us -> 82.2 us (level)
  no operation moved by 1% of the time
where the time goes in v8:
time: 82.2 us; the launch traced here: 82.1 us
  Pallas kernels  77.2 us (94%)
  local copies, waits for them, and re-layouts  3.59 us (4%)
  between operations  1.31 us (2%)
    pallas_call x1, Pallas kernels, whole(): pl.pallas_call(whole_kernel, in_specs=[pl.BlockSpec(memory_space=pltpu.SM...  77.2 us
    unnamed x10, local copies, waits for them, and re-layouts  3.59 us

profile of v8, /device:TPU:8, one launch (start us, length us, event | category | flops | bytes accessed | tf_op | source)
XLA Modules:
  0.0 82.1 jit_solution(8460074370937519811)
XLA Ops:
  1.3 77.2 %whole.1 = (bf16[1,8,16,4,192]{4,3,2,1,0:T(4,128)(2,1)}, f32[27,72]{1,0:T(8,128)}, f32[8,144]{1,0:T(8,128)}, f32[27,288]{1,0:T(8,128)}) custom-call(s32[1,8]{1,0:T(1,128)} %slots.1, s32[1]{0:T(128)S(6)} %copy.16.count, bf16[1,16,32,8,96]{4,3,2,1,0:T(8,128)(2,1)} %feats_in.1, s32[1,16,8,32]{3,2,1,0:T(8,128)} %bitcast.1, bf16[1,8,16,4,192]{4,3,2,1,0:T(4,128)(2,1)} %cot_in.1, ...), custom_call_target="tpu_custom_call" | custom-call | tf_op jit(solution)/shard_map/whole/pallas_call | solution.py:832
  78.5 0.0 copy-start.1
  78.5 0.0 copy-start.2
  78.5 1.8 %copy.17 = bf16[1,8,16,4,192]{4,3,2,1,0:T(4,128)(2,1)} copy(bf16[1,8,16,4,192]{4,3,2,1,0:T(4,128)(2,1)} %get-tuple-element.8) | data formatting | bytes 393216
  80.2 0.0 copy-done.1
  80.2 0.0 copy-start
  80.2 0.6 copy.18
  80.8 0.0 copy-done.2
  80.8 0.6 copy.19
  81.4 0.0 copy-done
  81.4 0.6 copy.20
Async XLA Ops:
  78.5 1.8 %copy-start.1 = (f32[27,72]{1,0:T(8,128)S(1)}, f32[27,72]{1,0:T(8,128)}, u32[]{:S(2)}) copy-start(f32[27,72]{1,0:T(8,128)} %get-tuple-element.9) | copy-start | bytes 23332
  78.5 2.4 %copy-start.2 = (f32[8,144]{1,0:T(8,128)S(1)}, f32[8,144]{1,0:T(8,128)}, u32[]{:S(2)}) copy-start(f32[8,144]{1,0:T(8,128)} %get-tuple-element.10) | copy-start | bytes 13828
  80.2 1.2 %copy-start = (f32[27,288]{1,0:T(8,128)S(1)}, f32[27,288]{1,0:T(8,128)}, u32[]{:S(2)}) copy-start(f32[27,288]{1,0:T(8,128)} %get-tuple-element.11) | copy-start | bytes 93316
